TPU v7x, 32 devices: a whole 2x2x4 slice. The times are simulated.
32 devices in a mesh: seq: 8 (over y, x, core), head: 4 (over z).
Axes of the slice: x: 2, y: 2, z: 4, core: 2. Of those that a mesh axis runs over, the one named last changes fastest.
Arguments:
- queries: bfloat16 [8192, 8192], P(('seq', 'head')), may hold values from -6 to 6
- key_vectors: bfloat16 [8192, 8192], P(('seq', 'head')), may hold values from -6 to 6
- value_vectors: bfloat16 [8192, 8192], P(('seq', 'head')), may hold values from -6 to 6
- out_gain: float32 [64, 128], P('head'), may hold values from 0.1 to 1.9
Outputs:
- attended: bfloat16 [8192, 8192], P(('seq', 'head'))
All inputs are finite; a program needn't handle non-finite values.
Results may differ from a plain program's by a relative error of at most 0.0049.
Values may be sent and summed in bfloat16 or wider, within the bound.
No kernel may reach another device: no remote copies, remote signals or barrier semaphores. Data moves between devices by JAX's collectives and lax.ppermute only.
A program may use at most 128 MiB of HBM per device.

v0:
```python
import jax
import jax.numpy as jnp
from jax import lax
from jax.sharding import PartitionSpec as P

HEADS = 64
HD = 128
BLOCK = 512


def passed_along(block, axis, distance):
    devices = range(lax.axis_size(axis))
    route = [(i - distance, i) for i in devices if i - distance in devices]
    return lax.ppermute(block, axis, route)


def split_heads(matrix):
    return matrix.reshape(matrix.shape[0], HEADS, HD)


def to_blocks(tensor):
    return tensor.reshape(tensor.shape[0] // BLOCK, BLOCK, tensor.shape[1], HD)


def block_states(key_heads, value_heads):
    return jnp.einsum(
        "nbhd,nbhe->nhde",
        to_blocks(key_heads),
        to_blocks(value_heads),
        preferred_element_type=jnp.float32,
    )


def carried_states(states):
    own = jnp.sum(states, axis=0)
    seq_count = lax.axis_size("seq")

    def relay(step, prefix):
        return passed_along(prefix + own, "seq", 1)

    prefix = lax.fori_loop(0, seq_count - 1, relay, jnp.zeros_like(own))
    carried = prefix[None] + (jnp.cumsum(states, axis=0) - states)
    return carried.astype(jnp.bfloat16)


def per_device(queries, key_vectors, value_vectors, out_gain):
    query_heads, key_heads, value_heads = (
        lax.all_to_all(split_heads(queries), "head", split_axis=1, concat_axis=0, tiled=True),
        lax.all_to_all(split_heads(key_vectors), "head", split_axis=1, concat_axis=0, tiled=True),
        lax.all_to_all(split_heads(value_vectors), "head", split_axis=1, concat_axis=0, tiled=True),
    )
    carried = carried_states(block_states(key_heads, value_heads))
    query_blocks = to_blocks(query_heads)
    key_blocks = to_blocks(key_heads)
    value_blocks = to_blocks(value_heads)
    inter = jnp.einsum("nbhd,nhde->nbhe", query_blocks, carried, preferred_element_type=jnp.float32)
    scores = jnp.einsum(
        "nbhd,nchd->nhbc", query_blocks, key_blocks, preferred_element_type=jnp.float32
    )
    causal = jnp.arange(BLOCK)[:, None] >= jnp.arange(BLOCK)[None, :]
    scores = jnp.where(causal[None, None], scores, jnp.float32(0.0)).astype(jnp.bfloat16)
    intra = jnp.einsum("nhbc,nchd->nbhd", scores, value_blocks, preferred_element_type=jnp.float32)
    raw = inter + intra
    scale = lax.rsqrt(jnp.mean(raw * raw, axis=-1, keepdims=True) + 1e-06)
    normed = (raw * scale * out_gain[None, None]).astype(jnp.bfloat16)
    normed = normed.reshape(query_heads.shape[0], query_heads.shape[1], HD)
    tokens_back = lax.all_to_all(normed, "head", split_axis=0, concat_axis=1, tiled=True)
    return tokens_back.reshape(tokens_back.shape[0], HEADS * HD)


def solution(mesh):
    return jax.shard_map(
        per_device,
        mesh=mesh,
        in_specs=(
            P(("seq", "head"), None),
            P(("seq", "head"), None),
            P(("seq", "head"), None),
            P("head", None),
        ),
        out_specs=P(("seq", "head"), None),
        check_vma=False,
    )
```

profile of v0, /device:TPU:3, one launch (start us, length us, event | category | flops | bytes accessed | tf_op | source)
XLA Modules:
  0.0 590.1 jit_solution(9999195893356626681)
XLA Ops:
  0.0 6.4 %copy.55 = bf16[256,8192]{0,1:T(8,128)(2,1)} copy(bf16[256,8192]{1,0:T(8,128)(2,1)} %param.6) | data formatting | bytes 8388608 | tf_op args[0]
  6.4 6.4 %copy.56 = bf16[256,64,128]{2,0,1:T(8,128)(2,1)} copy(bf16[256,64,128]{0,2,1:T(8,128)(2,1)} %bitcast.39) | data formatting | bytes 8388608 | tf_op jit(solution)/shard_map/reshape | solution.py:18
  17.6 6.4 %copy.45 = bf16[256,8192]{0,1:T(8,128)(2,1)} copy(bf16[256,8192]{1,0:T(8,128)(2,1)} %param.7) | data formatting | bytes 8388608 | tf_op args[1]
  24.0 6.4 %copy.46 = bf16[256,64,128]{2,0,1:T(8,128)(2,1)} copy(bf16[256,64,128]{0,2,1:T(8,128)(2,1)} %bitcast.40) | data formatting | bytes 8388608 | tf_op jit(solution)/shard_map/reshape | solution.py:18
  30.4 79.9 %all-to-all-done.2 = bf16[256,64,128]{2,0,1:T(8,128)(2,1)} async-done(((bf16[256,64,128]{2,0,1:T(8,128)(2,1)}), bf16[256,64,128]{2,0,1:T(8,128)(2,1)}, u32[]{:S(2)}, u32[]{:S(2)}) %all-to-all-start.2) | async-done | bytes 4194336 | tf_op jit(solution)/shard_map/all_to_all | solution.py:48
  115.1 6.4 %copy.49 = bf16[256,8192]{0,1:T(8,128)(2,1)} copy(bf16[256,8192]{1,0:T(8,128)(2,1)} %param.8) | data formatting | bytes 8388608 | tf_op args[2]
  121.5 6.4 %copy.50 = bf16[256,64,128]{2,0,1:T(8,128)(2,1)} copy(bf16[256,64,128]{0,2,1:T(8,128)(2,1)} %bitcast.41) | data formatting | bytes 8388608 | tf_op jit(solution)/shard_map/reshape | solution.py:18
  127.9 80.0 %all-to-all-done = bf16[256,64,128]{2,0,1:T(8,128)(2,1)} async-done(((bf16[256,64,128]{2,0,1:T(8,128)(2,1)}), bf16[256,64,128]{2,0,1:T(8,128)(2,1)}, u32[]{:S(2)}, u32[]{:S(2)}) %all-to-all-start) | async-done | bytes 4194336 | tf_op jit(solution)/shard_map/all_to_all | solution.py:49
  212.8 6.8 %copy.58 = bf16[4,256,16,128]{3,2,1,0:T(8,128)(2,1)} copy(bf16[4,256,16,128]{3,1,2,0:T(8,128)(2,1)} %bitcast.13) | data formatting | bytes 8388608 | tf_op jit(solution)/shard_map/all_to_all | solution.py:48
  219.6 6.9 %copy.48 = bf16[4,256,16,128]{3,2,1,0:T(8,128)(2,1)} copy(bf16[4,256,16,128]{3,1,2,0:T(8,128)(2,1)} %bitcast.3) | data formatting | bytes 8388608 | tf_op jit(solution)/shard_map/all_to_all | solution.py:49
  226.5 78.9 %all-to-all-done.1 = bf16[256,64,128]{2,0,1:T(8,128)(2,1)} async-done(((bf16[256,64,128]{2,0,1:T(8,128)(2,1)}), bf16[256,64,128]{2,0,1:T(8,128)(2,1)}, u32[]{:S(2)}, u32[]{:S(2)}) %all-to-all-start.1) | async-done | bytes 4194336 | tf_op jit(solution)/shard_map/all_to_all | solution.py:50
  310.5 5.5 fusion.12
  316.1 119.3 %while.10 = (s32[]{:T(128)}, f32[16,128,128]{2,1,0:T(8,128)S(1)}, f32[16,128,128]{2,1,0:T(8,128)S(1)}, s32[]{:T(128)}) while((s32[]{:T(128)}, f32[16,128,128]{2,1,0:T(8,128)S(1)}, f32[16,128,128]{2,1,0:T(8,128)S(1)}, s32[]{:T(128)}) %tuple.20), condition=%wide.region_2.0_spmd, body=%wide.region_1.0_spmd.sunk | while | flops 262146 | bytes 7340125 | solution.py:41
  320.7 11.7 %collective-permute-done = f32[16,128,128]{2,1,0:T(8,128)S(1)} collective-permute-done((f32[16,128,128]{2,1,0:T(8,128)S(1)}, f32[16,128,128]{2,1,0:T(8,128)S(1)}, u32[]{:S(2)}, u32[]{:S(2)}) %collective-permute-start) | collective-permute-done | bytes 1048608 | tf_op jit(solution)/shard_map/while/body/eval_jaxpr/ppermute | solution.py:14
  332.6 5.3 collective-permute-start
  337.9 11.7 %collective-permute-done = f32[16,128,128]{2,1,0:T(8,128)S(1)} collective-permute-done((f32[16,128,128]{2,1,0:T(8,128)S(1)}, f32[16,128,128]{2,1,0:T(8,128)S(1)}, u32[]{:S(2)}, u32[]{:S(2)}) %collective-permute-start) | collective-permute-done | bytes 1048608 | tf_op jit(solution)/shard_map/while/body/eval_jaxpr/ppermute | solution.py:14
  349.7 5.3 collective-permute-start
  355.0 11.7 %collective-permute-done = f32[16,128,128]{2,1,0:T(8,128)S(1)} collective-permute-done((f32[16,128,128]{2,1,0:T(8,128)S(1)}, f32[16,128,128]{2,1,0:T(8,128)S(1)}, u32[]{:S(2)}, u32[]{:S(2)}) %collective-permute-start) | collective-permute-done | bytes 1048608 | tf_op jit(solution)/shard_map/while/body/eval_jaxpr/ppermute | solution.py:14
  366.9 5.3 collective-permute-start
  372.2 11.7 %collective-permute-done = f32[16,128,128]{2,1,0:T(8,128)S(1)} collective-permute-done((f32[16,128,128]{2,1,0:T(8,128)S(1)}, f32[16,128,128]{2,1,0:T(8,128)S(1)}, u32[]{:S(2)}, u32[]{:S(2)}) %collective-permute-start) | collective-permute-done | bytes 1048608 | tf_op jit(solution)/shard_map/while/body/eval_jaxpr/ppermute | solution.py:14
  384.0 5.3 collective-permute-start
  389.3 11.7 %collective-permute-done = f32[16,128,128]{2,1,0:T(8,128)S(1)} collective-permute-done((f32[16,128,128]{2,1,0:T(8,128)S(1)}, f32[16,128,128]{2,1,0:T(8,128)S(1)}, u32[]{:S(2)}, u32[]{:S(2)}) %collective-permute-start) | collective-permute-done | bytes 1048608 | tf_op jit(solution)/shard_map/while/body/eval_jaxpr/ppermute | solution.py:14
  406.5 11.7 %collective-permute-done = f32[16,128,128]{2,1,0:T(8,128)S(1)} collective-permute-done((f32[16,128,128]{2,1,0:T(8,128)S(1)}, f32[16,128,128]{2,1,0:T(8,128)S(1)}, u32[]{:S(2)}, u32[]{:S(2)}) %collective-permute-start) | collective-permute-done | bytes 1048608 | tf_op jit(solution)/shard_map/while/body/eval_jaxpr/ppermute | solution.py:14
  418.3 5.3 collective-permute-start
  423.6 11.7 %collective-permute-done = f32[16,128,128]{2,1,0:T(8,128)S(1)} collective-permute-done((f32[16,128,128]{2,1,0:T(8,128)S(1)}, f32[16,128,128]{2,1,0:T(8,128)S(1)}, u32[]{:S(2)}, u32[]{:S(2)}) %collective-permute-start) | collective-permute-done | bytes 1048608 | tf_op jit(solution)/shard_map/while/body/eval_jaxpr/ppermute | solution.py:14
  438.8 5.8 fusion.7
  444.6 19.6 %multiply_reduce_fusion = (f32[2,512,16]{1,2,0:T(8,128)S(1)}, f32[2,16,512,128]{2,3,1,0:T(8,128)}) fusion(f32[2,16,128,512]{3,2,1,0:T(8,128)} %fusion.7, bf16[2,512,16,128]{3,2,1,0:T(8,128)(2,1)} %bitcast.45, pred[512,512]{1,0:T(8,128)(4,1)S(1)} %iota_compare_fusion, bf16[2,512,16,128]{3,2,1,0:T(8,128)(2,1)} %bitcast.42, bf16[2,512,16,128]{3,2,1,0:T(8,128)(2,1)} %bitcast.34), kind=kOutput, calls=%fused_computation.3 | convolution fusion | flops 4318019584 | bytes 29687808 | tf_op jit(solution)/shard_map/nhbc,nchd->nbhd/dot_general | solution.py:62
  464.2 8.6 %multiply_convert_fusion = bf16[2,512,16,128]{1,3,2,0:T(8,128)(2,1)} fusion(f32[16,128]{1,0:T(8,128)S(1)} %copy-done.3, f32[2,512,16]{1,2,0:T(8,128)S(1)} %add_rsqrt_fusion, f32[2,16,512,128]{2,3,1,0:T(8,128)} %get-tuple-element.32, f32[2,16,128,512]{3,2,1,0:T(8,128)} %fusion.7), kind=kLoop, calls=%fused_computation.2 | loop fusion | flops 8388608 | bytes 21045248 | tf_op jit(solution)/shard_map/convert_element_type | solution.py:65
  472.8 7.9 %copy.65 = bf16[2,512,16,128]{3,2,1,0:T(8,128)(2,1)} copy(bf16[2,512,16,128]{1,3,2,0:T(8,128)(2,1)} %multiply_convert_fusion) | data formatting | bytes 8388608 | tf_op jit(solution)/shard_map/convert_element_type | solution.py:65
  480.7 95.5 %all_to_all.60 = bf16[1024,16,128]{2,1,0:T(8,128)(2,1)} all-to-all(bf16[1024,16,128]{2,1,0:T(8,128)(2,1)} %bitcast.36), channel_id=1, replica_groups=mesh['seq'=8,'head'=4] {'head'}, dimensions={0} | all-to-all | bytes 8388608 | tf_op jit(solution)/shard_map/all_to_all | solution.py:67
  576.2 7.5 %copy.66 = bf16[256,4,16,128]{0,3,2,1:T(8,128)(2,1)} copy(bf16[256,4,16,128]{3,2,0,1:T(8,128)(2,1)} %bitcast.37) | data formatting | bytes 8388608 | tf_op jit(solution)/shard_map/all_to_all | solution.py:67
  583.8 6.3 %copy.67 = bf16[256,8192]{1,0:T(8,128)(2,1)} copy(bf16[256,8192]{0,1:T(8,128)(2,1)} %bitcast.38) | data formatting | bytes 8388608 | tf_op jit(solution)/shard_map/reshape | solution.py:68
  (25 shorter events, 33.9 us)
Async XLA Ops:
  12.8 97.5 %all-to-all-start.2 = ((bf16[256,64,128]{2,0,1:T(8,128)(2,1)}), bf16[256,64,128]{2,0,1:T(8,128)(2,1)}, u32[]{:S(2)}, u32[]{:S(2)}) async-start(bf16[256,64,128]{2,0,1:T(8,128)(2,1)} %copy.56), calls=%async_computation.2 | async-start | bytes 8388608 | tf_op jit(solution)/shard_map/all_to_all | solution.py:48
  110.3 97.5 %all-to-all-start = ((bf16[256,64,128]{2,0,1:T(8,128)(2,1)}), bf16[256,64,128]{2,0,1:T(8,128)(2,1)}, u32[]{:S(2)}, u32[]{:S(2)}) async-start(bf16[256,64,128]{2,0,1:T(8,128)(2,1)} %copy.46), calls=%async_computation | async-start | bytes 8388608 | tf_op jit(solution)/shard_map/all_to_all | solution.py:49
  207.8 97.6 %all-to-all-start.1 = ((bf16[256,64,128]{2,0,1:T(8,128)(2,1)}), bf16[256,64,128]{2,0,1:T(8,128)(2,1)}, u32[]{:S(2)}, u32[]{:S(2)}) async-start(bf16[256,64,128]{2,0,1:T(8,128)(2,1)} %copy.50), calls=%async_computation.1 | async-start | bytes 8388608 | tf_op jit(solution)/shard_map/all_to_all | solution.py:50
  305.4 5.1 copy-start.1
  310.5 5.5 copy-start.2
  316.3 16.2 %collective-permute-start = (f32[16,128,128]{2,1,0:T(8,128)S(1)}, f32[16,128,128]{2,1,0:T(8,128)S(1)}, u32[]{:S(2)}, u32[]{:S(2)}) collective-permute-start(f32[16,128,128]{2,1,0:T(8,128)S(1)} %add.45), channel_id=1, source_target_pairs={{0,4},{4,8},{8,12},{12,16},{16,20},{20,24},{24,28},{1,5},{5,9},{9,... | collective-permute-start | bytes 3145736 | tf_op jit(solution)/shard_map/while/body/eval_jaxpr/ppermute | solution.py:14
  332.6 17.0 %collective-permute-start = (f32[16,128,128]{2,1,0:T(8,128)S(1)}, f32[16,128,128]{2,1,0:T(8,128)S(1)}, u32[]{:S(2)}, u32[]{:S(2)}) collective-permute-start(f32[16,128,128]{2,1,0:T(8,128)S(1)} %add.45), channel_id=1, source_target_pairs={{0,4},{4,8},{8,12},{12,16},{16,20},{20,24},{24,28},{1,5},{5,9},{9,... | collective-permute-start | bytes 3145736 | tf_op jit(solution)/shard_map/while/body/eval_jaxpr/ppermute | solution.py:14
  349.7 17.0 %collective-permute-start = (f32[16,128,128]{2,1,0:T(8,128)S(1)}, f32[16,128,128]{2,1,0:T(8,128)S(1)}, u32[]{:S(2)}, u32[]{:S(2)}) collective-permute-start(f32[16,128,128]{2,1,0:T(8,128)S(1)} %add.45), channel_id=1, source_target_pairs={{0,4},{4,8},{8,12},{12,16},{16,20},{20,24},{24,28},{1,5},{5,9},{9,... | collective-permute-start | bytes 3145736 | tf_op jit(solution)/shard_map/while/body/eval_jaxpr/ppermute | solution.py:14
  366.9 17.0 %collective-permute-start = (f32[16,128,128]{2,1,0:T(8,128)S(1)}, f32[16,128,128]{2,1,0:T(8,128)S(1)}, u32[]{:S(2)}, u32[]{:S(2)}) collective-permute-start(f32[16,128,128]{2,1,0:T(8,128)S(1)} %add.45), channel_id=1, source_target_pairs={{0,4},{4,8},{8,12},{12,16},{16,20},{20,24},{24,28},{1,5},{5,9},{9,... | collective-permute-start | bytes 3145736 | tf_op jit(solution)/shard_map/while/body/eval_jaxpr/ppermute | solution.py:14
  384.0 17.0 %collective-permute-start = (f32[16,128,128]{2,1,0:T(8,128)S(1)}, f32[16,128,128]{2,1,0:T(8,128)S(1)}, u32[]{:S(2)}, u32[]{:S(2)}) collective-permute-start(f32[16,128,128]{2,1,0:T(8,128)S(1)} %add.45), channel_id=1, source_target_pairs={{0,4},{4,8},{8,12},{12,16},{16,20},{20,24},{24,28},{1,5},{5,9},{9,... | collective-permute-start | bytes 3145736 | tf_op jit(solution)/shard_map/while/body/eval_jaxpr/ppermute | solution.py:14
  401.2 17.0 %collective-permute-start = (f32[16,128,128]{2,1,0:T(8,128)S(1)}, f32[16,128,128]{2,1,0:T(8,128)S(1)}, u32[]{:S(2)}, u32[]{:S(2)}) collective-permute-start(f32[16,128,128]{2,1,0:T(8,128)S(1)} %add.45), channel_id=1, source_target_pairs={{0,4},{4,8},{8,12},{12,16},{16,20},{20,24},{24,28},{1,5},{5,9},{9,... | collective-permute-start | bytes 3145736 | tf_op jit(solution)/shard_map/while/body/eval_jaxpr/ppermute | solution.py:14
  418.3 17.0 %collective-permute-start = (f32[16,128,128]{2,1,0:T(8,128)S(1)}, f32[16,128,128]{2,1,0:T(8,128)S(1)}, u32[]{:S(2)}, u32[]{:S(2)}) collective-permute-start(f32[16,128,128]{2,1,0:T(8,128)S(1)} %add.45), channel_id=1, source_target_pairs={{0,4},{4,8},{8,12},{12,16},{16,20},{20,24},{24,28},{1,5},{5,9},{9,... | collective-permute-start | bytes 3145736 | tf_op jit(solution)/shard_map/while/body/eval_jaxpr/ppermute | solution.py:14
  435.4 3.4 copy-start
  444.6 19.6 %copy-start.3 = (f32[16,128]{1,0:T(8,128)S(1)}, f32[16,128]{1,0:T(8,128)}, u32[]{:S(2)}) copy-start(f32[16,128]{1,0:T(8,128)} %param.9) | copy-start | bytes 24580
where the time goes:
time: 592 us; the launch traced here: 590 us
  waiting for transfers between devices  321 us (54%)
  blocking collectives  95.5 us (16%)
  local copies, waits for them, and re-layouts  79.4 us (13%)
  starting transfers between devices  50.8 us (9%)
  matrix products  30.9 us (5%)
  other arithmetic  12.5 us (2%)
    all_to_all x1, blocking collectives, per_device(): lax.all_to_all(normed, 'head', split_axis=0, concat_axis=1, tiled=True)  95.5 us
    ppermute x7, waiting for transfers between devices, passed_along(): return lax.ppermute(block, axis, route)  82 us
    all_to_all x1, waiting for transfers between devices, per_device(): lax.all_to_all(split_heads(key_vectors), 'head', split_axis=1, concat_axi...  80 us
    all_to_all x1, waiting for transfers between devices, per_device(): lax.all_to_all(split_heads(queries), 'head', split_axis=1, concat_axis=0,...  79.9 us
    all_to_all x1, waiting for transfers between devices, per_device(): lax.all_to_all(split_heads(value_vectors), 'head', split_axis=1, concat_a...  78.9 us
    ppermute x7, starting transfers between devices, passed_along(): return lax.ppermute(block, axis, route)  36.2 us
    unnamed x11, local copies, waits for them, and re-layouts  19.7 us
    dot_general x1, matrix products, per_device(): jnp.einsum('nhbc,nchd->nbhd', scores, value_blocks, preferred_element_typ...  19.6 us
  transfers between devices with their start and end apart: 10, of which 10 were waited for; matrix products, arithmetic and copies ran while one was open for 7% of the time, Pallas kernels for 0%

commit v1 on v0

v1 whole, which is shorter than its diff:
```python
import functools

import jax
import jax.numpy as jnp
from jax import lax
from jax.experimental import pallas as pl
from jax.experimental.pallas import tpu as pltpu
from jax.sharding import PartitionSpec as P

HD = 128
CHUNKS = 4
STATE_HEADS = 4
OUT_HEADS = 4


def state_kernel(key_ref, value_ref, state_ref):
    for head in range(state_ref.shape[0]):
        columns = slice(head * HD, (head + 1) * HD)
        state = lax.dot_general(
            key_ref[:, columns],
            value_ref[:, columns],
            (((0,), (0,)), ((), ())),
            preferred_element_type=jnp.float32,
        )
        state_ref[head] = state.astype(jnp.bfloat16)


def states_of(key_vectors, value_vectors, first, count):
    tokens = key_vectors.shape[0]
    step = min(STATE_HEADS, count)
    tokens_spec = pl.BlockSpec((tokens, step * HD), lambda i: (0, first // step + i))
    return pl.pallas_call(
        state_kernel,
        grid=(count // step,),
        in_specs=[tokens_spec, tokens_spec],
        out_specs=pl.BlockSpec((step, HD, HD), lambda i: (i, 0, 0)),
        out_shape=jax.ShapeDtypeStruct((count, HD, HD), jnp.bfloat16),
        cost_estimate=pl.CostEstimate(
            flops=2 * tokens * HD * HD * count,
            bytes_accessed=2 * count * HD * (2 * tokens + HD),
            transcendentals=0,
        ),
    )(key_vectors, value_vectors)


def output_kernel(query_ref, key_ref, value_ref, carried_ref, gain_ref, out_ref):
    tokens = query_ref.shape[0]
    rows = lax.broadcasted_iota(jnp.int32, (tokens, tokens), 0)
    causal = rows >= lax.broadcasted_iota(jnp.int32, (tokens, tokens), 1)
    for head in range(carried_ref.shape[0]):
        columns = slice(head * HD, (head + 1) * HD)
        query = query_ref[:, columns]
        scores = lax.dot_general(
            query,
            key_ref[:, columns],
            (((1,), (1,)), ((), ())),
            preferred_element_type=jnp.float32,
        )
        scores = jnp.where(causal, scores, 0.0).astype(jnp.bfloat16)
        raw = jnp.dot(query, carried_ref[head], preferred_element_type=jnp.float32)
        raw += jnp.dot(scores, value_ref[:, columns], preferred_element_type=jnp.float32)
        scale = lax.rsqrt(jnp.mean(raw * raw, axis=-1, keepdims=True) + 1e-06)
        out_ref[:, columns] = (raw * scale * gain_ref[head]).astype(jnp.bfloat16)


def outputs_of(queries, key_vectors, value_vectors, carried, gain, first):
    tokens, count = queries.shape[0], carried.shape[0]
    step = min(OUT_HEADS, count)
    tokens_spec = pl.BlockSpec((tokens, step * HD), lambda i: (0, first // step + i))
    return pl.pallas_call(
        output_kernel,
        grid=(count // step,),
        in_specs=[
            tokens_spec,
            tokens_spec,
            tokens_spec,
            pl.BlockSpec((step, HD, HD), lambda i: (i, 0, 0)),
            pl.BlockSpec((step, 1, HD), lambda i: (first // step + i, 0, 0)),
        ],
        out_specs=pl.BlockSpec((tokens, step * HD), lambda i: (0, i)),
        out_shape=jax.ShapeDtypeStruct((tokens, count * HD), jnp.bfloat16),
        cost_estimate=pl.CostEstimate(
            flops=2 * tokens * HD * count * (2 * tokens + HD),
            bytes_accessed=2 * count * HD * (4 * tokens + HD),
            transcendentals=tokens * count,
        ),
    )(queries, key_vectors, value_vectors, carried, gain)


def added(*terms):
    return functools.reduce(jnp.add, [term.astype(jnp.float32) for term in terms])


def packed(total):
    return total.astype(jnp.bfloat16)


def carried_of(states):
    place, line = lax.axis_index("head"), lax.axis_size("head")
    shard, shards = lax.axis_index("seq"), lax.axis_size("seq")

    arrived = []
    for hop in range(1, line):
        sent = packed(added(arrived[-1], states)) if arrived else states
        route = [(hop - 1, hop), (line - hop, line - hop - 1)]
        arrived.append(lax.ppermute(sent, "head", route))
    carried = added(*[jnp.where(place == hop + 1, block, jnp.zeros_like(block)) for hop, block in enumerate(arrived)])
    total = added(states, *arrived)

    earlier = jnp.zeros_like(total)
    whole = total
    step = 2
    while step < shards:
        last = 2 * step == shards
        route = [(i, i ^ step) for i in range(shards) if not last or not i & step]
        block = lax.ppermute(packed(whole), "seq", route).astype(jnp.float32)
        earlier += jnp.where(shard & step != 0, block, 0.0)
        whole += block
        step *= 2

    sent = packed(earlier + jnp.where(shard & 1 == 0, total, 0.0))
    block = lax.ppermute(sent, "seq", [(i, i ^ 1) for i in range(shards)])
    return packed(carried + earlier + block.astype(jnp.float32))


def per_device(queries, key_vectors, value_vectors, out_gain):
    heads = queries.shape[1] // HD
    gain = lax.all_gather(out_gain, "head", axis=0, tiled=True).reshape(heads, 1, HD)
    count = heads // CHUNKS
    outs = []
    for first in range(0, heads, count):
        states = states_of(key_vectors, value_vectors, first, count)
        carried = carried_of(states)
        outs.append(outputs_of(queries, key_vectors, value_vectors, carried, gain, first))
    return jnp.concatenate(outs, axis=1)


def solution(mesh):
    return jax.shard_map(
        per_device,
        mesh=mesh,
        in_specs=(
            P(("seq", "head"), None),
            P(("seq", "head"), None),
            P(("seq", "head"), None),
            P("head", None),
        ),
        out_specs=P(("seq", "head"), None),
        check_vma=False,
    )
```

time: 592 us -> 214 us (0.36)
  the two profiles are of different devices: /device:TPU:3 before, /device:TPU:0 now
where the time goes in v1:
time: 214 us; the launch traced here: 210 us
  waiting for transfers between devices  69.1 us (32%)
  Pallas kernels  40.3 us (19%)
  blocking collectives  38.2 us (18%)
  starting transfers between devices  34.8 us (16%)
  other arithmetic  27.3 us (13%)
    ppermute x12, waiting for transfers between devices, carried_of(): arrived.append(lax.ppermute(sent, 'head', route))  40.6 us
    all_gather x1, blocking collectives, per_device(): lax.all_gather(out_gain, 'head', axis=0, tiled=True).reshape(heads, 1, HD)  38.2 us
    ppermute x8, waiting for transfers between devices, carried_of(): block = lax.ppermute(packed(whole), 'seq', route).astype(jnp.float32)  28.5 us
    pallas_call x4, Pallas kernels, outputs_of(): pl.pallas_call(output_kernel, grid=(count // step,), in_specs=[tokens_spe...  24.5 us
    convert_element_type x24, other arithmetic, packed(): return total.astype(jnp.bfloat16)  23.9 us
    ppermute x12, starting transfers between devices, carried_of(): arrived.append(lax.ppermute(sent, 'head', route))  18.7 us
    ppermute x8, starting transfers between devices, carried_of(): block = lax.ppermute(packed(whole), 'seq', route).astype(jnp.float32)  16 us
    pallas_call x4, Pallas kernels, states_of(): pl.pallas_call(state_kernel, grid=(count // step,), in_specs=[tokens_spec...  15.8 us
  transfers between devices with their start and end apart: 24, of which 9 were waited for; matrix products, arithmetic and copies ran while one was open for 10% of the time, Pallas kernels for 14%

profile of v1, /device:TPU:0, one launch (start us, length us, event | category | flops | bytes accessed | tf_op | source)
XLA Modules:
  0.0 210.3 jit_solution(7059554832187764253)
XLA Ops:
  0.0 4.0 %shard_map.52 = bf16[16,128,128]{2,1,0:T(8,128)(2,1)} custom-call(bf16[256,8192]{1,0:T(8,128)(2,1)} %key_ref.15, bf16[256,8192]{1,0:T(8,128)(2,1)} %value_ref.15), custom_call_target="tpu_custom_call" | custom-call | flops 134217728 | bytes 2621440 | tf_op jit(solution)/shard_map/pallas_call | solution.py:32
  4.0 5.7 %collective-permute-start.18 = (bf16[16,128,128]{2,1,0:T(8,128)(2,1)}, bf16[16,128,128]{2,1,0:T(8,128)(2,1)}, u32[]{:S(2)}, u32[]{:S(2)}) collective-permute-start(bf16[16,128,128]{2,1,0:T(8,128)(2,1)} %shard_map.52), channel_id=1, source_target_pairs={{0,1},{3,2},{4,5},{7,6},{8,9},{11,10},{12,13},{15,14},{16,17},{19,... | collective-permute-start | bytes 1572872 | tf_op jit(solution)/shard_map/ppermute | solution.py:106
  9.7 3.9 %shard_map.46 = bf16[16,128,128]{2,1,0:T(8,128)(2,1)} custom-call(bf16[256,8192]{1,0:T(8,128)(2,1)} %key_ref.15, bf16[256,8192]{1,0:T(8,128)(2,1)} %value_ref.15), custom_call_target="tpu_custom_call" | custom-call | flops 134217728 | bytes 2621440 | tf_op jit(solution)/shard_map/pallas_call | solution.py:32
  13.6 2.1 %collective-permute-start = (bf16[16,128,128]{2,1,0:T(8,128)(2,1)}, bf16[16,128,128]{2,1,0:T(8,128)(2,1)}, u32[]{:S(2)}, u32[]{:S(2)}) collective-permute-start(bf16[16,128,128]{2,1,0:T(8,128)(2,1)} %shard_map.46), channel_id=1, source_target_pairs={{0,1},{3,2},{4,5},{7,6},{8,9},{11,10},{12,13},{15,14},{16,17},{19,... | collective-permute-start | bytes 1572872 | tf_op jit(solution)/shard_map/ppermute | solution.py:106
  15.7 3.9 %shard_map.48 = bf16[16,128,128]{2,1,0:T(8,128)(2,1)} custom-call(bf16[256,8192]{1,0:T(8,128)(2,1)} %key_ref.15, bf16[256,8192]{1,0:T(8,128)(2,1)} %value_ref.15), custom_call_target="tpu_custom_call" | custom-call | flops 134217728 | bytes 2621440 | tf_op jit(solution)/shard_map/pallas_call | solution.py:32
  21.2 4.0 %shard_map.50 = bf16[16,128,128]{2,1,0:T(8,128)(2,1)} custom-call(bf16[256,8192]{1,0:T(8,128)(2,1)} %key_ref.15, bf16[256,8192]{1,0:T(8,128)(2,1)} %value_ref.15), custom_call_target="tpu_custom_call" | custom-call | flops 134217728 | bytes 2621440 | tf_op jit(solution)/shard_map/pallas_call | solution.py:32
  26.6 38.2 %all_gather.3 = f32[64,128]{1,0:T(8,128)} all-gather(f32[16,128]{1,0:T(8,128)S(1)} %copy-done.22), channel_id=1, replica_groups=mesh['seq'=8,'head'=4] {'head'}, dimensions={0}, use_global_device_ids=true | all-gather | bytes 40960 | tf_op jit(solution)/shard_map/all_gather | solution.py:128
  76.2 17.6 %collective-permute-done.20 = bf16[16,128,128]{2,1,0:T(8,128)(2,1)S(1)} collective-permute-done((bf16[16,128,128]{2,1,0:T(8,128)(2,1)S(1)}, bf16[16,128,128]{2,1,0:T(8,128)(2,1)S(1)}, u32[]{:S(2)}, u32[]{:S(2)}) %collective-permute-start.20) | collective-permute-done | bytes 524320 | tf_op jit(solution)/shard_map/ppermute | solution.py:106
  95.2 1.6 collective-permute-start.21
  96.8 8.3 %collective-permute-done.2 = bf16[16,128,128]{2,1,0:T(8,128)(2,1)S(1)} collective-permute-done((bf16[16,128,128]{2,1,0:T(8,128)(2,1)S(1)}, bf16[16,128,128]{2,1,0:T(8,128)(2,1)S(1)}, u32[]{:S(2)}, u32[]{:S(2)}) %collective-permute-start.2) | collective-permute-done | bytes 524320 | tf_op jit(solution)/shard_map/ppermute | solution.py:106
  106.5 1.6 collective-permute-start.3
  108.0 8.3 %collective-permute-done.8 = bf16[16,128,128]{2,1,0:T(8,128)(2,1)S(1)} collective-permute-done((bf16[16,128,128]{2,1,0:T(8,128)(2,1)S(1)}, bf16[16,128,128]{2,1,0:T(8,128)(2,1)S(1)}, u32[]{:S(2)}, u32[]{:S(2)}) %collective-permute-start.8) | collective-permute-done | bytes 524320 | tf_op jit(solution)/shard_map/ppermute | solution.py:106
  116.7 1.6 collective-permute-start.9
  118.2 6.3 %collective-permute-done.14 = bf16[16,128,128]{2,1,0:T(8,128)(2,1)S(1)} collective-permute-done((bf16[16,128,128]{2,1,0:T(8,128)(2,1)S(1)}, bf16[16,128,128]{2,1,0:T(8,128)(2,1)S(1)}, u32[]{:S(2)}, u32[]{:S(2)}) %collective-permute-start.14) | collective-permute-done | bytes 524320 | tf_op jit(solution)/shard_map/ppermute | solution.py:106
  124.9 1.6 collective-permute-start.15
  126.4 1.5 fusion.15
  127.9 3.5 %collective-permute-start.22 = (bf16[16,128,128]{2,1,0:T(8,128)(2,1)S(1)}, bf16[16,128,128]{2,1,0:T(8,128)(2,1)S(1)}, u32[]{:S(2)}, u32[]{:S(2)}) collective-permute-start(bf16[16,128,128]{2,1,0:T(8,128)(2,1)S(1)} %fusion.15), channel_id=1, source_target_pairs={{0,16},{4,20},{8,24},{12,28},{1,17},{5,21},{9,25},{13,29},{2,18},{... | collective-permute-start | bytes 1572872 | tf_op jit(solution)/shard_map/ppermute | solution.py:116
  131.4 1.5 fusion.3
  135.9 2.2 %collective-permute-done.15 = bf16[16,128,128]{2,1,0:T(8,128)(2,1)S(1)} collective-permute-done((bf16[16,128,128]{2,1,0:T(8,128)(2,1)S(1)}, bf16[16,128,128]{2,1,0:T(8,128)(2,1)S(1)}, u32[]{:S(2)}, u32[]{:S(2)}) %collective-permute-start.15) | collective-permute-done | bytes 524320 | tf_op jit(solution)/shard_map/ppermute | solution.py:116
  138.6 3.6 %collective-permute-start.16 = (bf16[16,128,128]{2,1,0:T(8,128)(2,1)S(1)}, bf16[16,128,128]{2,1,0:T(8,128)(2,1)S(1)}, u32[]{:S(2)}, u32[]{:S(2)}) collective-permute-start(bf16[16,128,128]{2,1,0:T(8,128)(2,1)S(1)} %fusion.11), channel_id=1, source_target_pairs={{0,16},{4,20},{8,24},{12,28},{1,17},{5,21},{9,25},{13,29},{2,18},{... | collective-permute-start | bytes 1572872 | tf_op jit(solution)/shard_map/ppermute | solution.py:116
  143.7 1.6 add_convert_fusion.1
  145.3 9.6 %collective-permute-done.4 = bf16[16,128,128]{2,1,0:T(8,128)(2,1)S(1)} collective-permute-done((bf16[16,128,128]{2,1,0:T(8,128)(2,1)S(1)}, bf16[16,128,128]{2,1,0:T(8,128)(2,1)S(1)}, u32[]{:S(2)}, u32[]{:S(2)}) %collective-permute-start.4) | collective-permute-done | bytes 524320 | tf_op jit(solution)/shard_map/ppermute | solution.py:116
  154.9 1.6 add_convert_fusion.7
  156.6 9.6 %collective-permute-done.10 = bf16[16,128,128]{2,1,0:T(8,128)(2,1)S(1)} collective-permute-done((bf16[16,128,128]{2,1,0:T(8,128)(2,1)S(1)}, bf16[16,128,128]{2,1,0:T(8,128)(2,1)S(1)}, u32[]{:S(2)}, u32[]{:S(2)}) %collective-permute-start.10) | collective-permute-done | bytes 524320 | tf_op jit(solution)/shard_map/ppermute | solution.py:116
  167.5 5.7 %collective-permute-done.16 = bf16[16,128,128]{2,1,0:T(8,128)(2,1)S(1)} collective-permute-done((bf16[16,128,128]{2,1,0:T(8,128)(2,1)S(1)}, bf16[16,128,128]{2,1,0:T(8,128)(2,1)S(1)}, u32[]{:S(2)}, u32[]{:S(2)}) %collective-permute-start.16) | collective-permute-done | bytes 524320 | tf_op jit(solution)/shard_map/ppermute | solution.py:116
  177.4 6.0 %shard_map.53 = bf16[256,2048]{1,0:T(8,128)(2,1)} custom-call(bf16[256,8192]{1,0:T(8,128)(2,1)} %query_ref.7, bf16[256,8192]{1,0:T(8,128)(2,1)} %key_ref.15, bf16[256,8192]{1,0:T(8,128)(2,1)} %value_ref.15, bf16[16,128,128]{2,1,0:T(8,128)(2,1)} %add_convert_fusion.carried_ref, f32[64,1,128]{2,1,0:T(1,128)} %bitcast.1), custom_call_target="tpu_custom_call" | custom-call | flops 671088640 | bytes 4718592 | tf_op jit(solution)/shard_map/pallas_call | solution.py:70
  183.4 6.2 %shard_map.47 = bf16[256,2048]{1,0:T(8,128)(2,1)} custom-call(bf16[256,8192]{1,0:T(8,128)(2,1)} %query_ref.7, bf16[256,8192]{1,0:T(8,128)(2,1)} %key_ref.15, bf16[256,8192]{1,0:T(8,128)(2,1)} %value_ref.15, bf16[16,128,128]{2,1,0:T(8,128)(2,1)} %add_convert_fusion.6.carried_ref, f32[64,1,128]{2,1,0:T(1,128)} %bitcast.2), custom_call_target="tpu_custom_call" | custom-call | flops 671088640 | bytes 4718592 | tf_op jit(solution)/shard_map/pallas_call | solution.py:70
  189.6 2.4 %add_convert_fusion.4.carried_ref = bf16[16,128,128]{2,1,0:T(8,128)(2,1)} fusion(bf16[16,128,128]{2,1,0:T(8,128)(2,1)} %collective-permute-done.11, bf16[16,128,128]{2,1,0:T(8,128)(2,1)S(1)} %copy-done.21, bf16[16,128,128]{2,1,0:T(8,128)(2,1)S(1)} %copy-done.15, bf16[16,128,128]{2,1,0:T(8,128)(2,1)S(1)} %copy-done.11, ...), kind=kLoop, calls=%fused_computation.41 | loop fusion | flops 4456448 | bytes 3670021 | tf_op jit(solution)/shard_map/convert_element_type | solution.py:95
  192.0 6.2 %shard_map.49 = bf16[256,2048]{1,0:T(8,128)(2,1)} custom-call(bf16[256,8192]{1,0:T(8,128)(2,1)} %query_ref.7, bf16[256,8192]{1,0:T(8,128)(2,1)} %key_ref.15, bf16[256,8192]{1,0:T(8,128)(2,1)} %value_ref.15, bf16[16,128,128]{2,1,0:T(8,128)(2,1)} %add_convert_fusion.4.carried_ref, f32[64,1,128]{2,1,0:T(1,128)} %bitcast.3), custom_call_target="tpu_custom_call" | custom-call | flops 671088640 | bytes 4718592 | tf_op jit(solution)/shard_map/pallas_call | solution.py:70
  198.3 2.4 %add_convert_fusion.2.carried_ref = bf16[16,128,128]{2,1,0:T(8,128)(2,1)} fusion(bf16[16,128,128]{2,1,0:T(8,128)(2,1)} %collective-permute-done.17, bf16[16,128,128]{2,1,0:T(8,128)(2,1)S(1)} %copy-done.19, bf16[16,128,128]{2,1,0:T(8,128)(2,1)S(1)} %copy-done.13, bf16[16,128,128]{2,1,0:T(8,128)(2,1)S(1)} %copy-done.9, bf16[16,128,128]{2,1,0:T(8,128)(2,1)S(1)} %copy-done.5, ...), kind=kLoop, calls=%fused_computation.39 | loop fusion | flops 4456448 | bytes 3670021 | tf_op jit(solution)/shard_map/convert_element_type | solution.py:95
  200.7 6.2 %shard_map.51 = bf16[256,2048]{1,0:T(8,128)(2,1)} custom-call(bf16[256,8192]{1,0:T(8,128)(2,1)} %query_ref.7, bf16[256,8192]{1,0:T(8,128)(2,1)} %key_ref.15, bf16[256,8192]{1,0:T(8,128)(2,1)} %value_ref.15, bf16[16,128,128]{2,1,0:T(8,128)(2,1)} %add_convert_fusion.2.carried_ref, f32[64,1,128]{2,1,0:T(1,128)} %bitcast.4), custom_call_target="tpu_custom_call" | custom-call | flops 671088640 | bytes 4718592 | tf_op jit(solution)/shard_map/pallas_call | solution.py:70
  206.9 3.4 %pad_maximum_fusion = bf16[256,8192]{1,0:T(8,128)(2,1)} fusion(bf16[256,2048]{1,0:T(8,128)(2,1)S(1)} %copy-done.16, bf16[256,2048]{1,0:T(8,128)(2,1)} %shard_map.51, bf16[256,2048]{1,0:T(8,128)(2,1)} %shard_map.49, bf16[256,2048]{1,0:T(8,128)(2,1)S(1)} %copy-done.17), kind=kLoop, calls=%fused_computation | loop fusion | flops 16777216 | bytes 8388608 | tf_op jit(solution)/shard_map/concatenate | solution.py:135
  (96 shorter events, 28.2 us)
Async XLA Ops:
  4.0 60.8 %collective-permute-start.18 = (bf16[16,128,128]{2,1,0:T(8,128)(2,1)}, bf16[16,128,128]{2,1,0:T(8,128)(2,1)}, u32[]{:S(2)}, u32[]{:S(2)}) collective-permute-start(bf16[16,128,128]{2,1,0:T(8,128)(2,1)} %shard_map.52), channel_id=1, source_target_pairs={{0,1},{3,2},{4,5},{7,6},{8,9},{11,10},{12,13},{15,14},{16,17},{19,... | collective-permute-start | bytes 1572872 | tf_op jit(solution)/shard_map/ppermute | solution.py:106
  13.6 53.1 %collective-permute-start = (bf16[16,128,128]{2,1,0:T(8,128)(2,1)}, bf16[16,128,128]{2,1,0:T(8,128)(2,1)}, u32[]{:S(2)}, u32[]{:S(2)}) collective-permute-start(bf16[16,128,128]{2,1,0:T(8,128)(2,1)} %shard_map.46), channel_id=1, source_target_pairs={{0,1},{3,2},{4,5},{7,6},{8,9},{11,10},{12,13},{15,14},{16,17},{19,... | collective-permute-start | bytes 1572872 | tf_op jit(solution)/shard_map/ppermute | solution.py:106
  19.7 45.1 %copy-start.3 = (bf16[16,128,128]{2,1,0:T(8,128)(2,1)S(1)}, bf16[16,128,128]{2,1,0:T(8,128)(2,1)}, u32[]{:S(2)}) copy-start(bf16[16,128,128]{2,1,0:T(8,128)(2,1)} %shard_map.52) | copy-start | bytes 1572868
  19.7 47.0 %copy-start.2 = (bf16[16,128,128]{2,1,0:T(8,128)(2,1)S(1)}, bf16[16,128,128]{2,1,0:T(8,128)(2,1)}, u32[]{:S(2)}) copy-start(bf16[16,128,128]{2,1,0:T(8,128)(2,1)} %shard_map.46) | copy-start | bytes 1572868
  19.7 48.9 %copy-start.1 = (bf16[16,128,128]{2,1,0:T(8,128)(2,1)S(1)}, bf16[16,128,128]{2,1,0:T(8,128)(2,1)}, u32[]{:S(2)}) copy-start(bf16[16,128,128]{2,1,0:T(8,128)(2,1)} %shard_map.48) | copy-start | bytes 1572868
  19.7 48.9 %collective-permute-start.6 = (bf16[16,128,128]{2,1,0:T(8,128)(2,1)}, bf16[16,128,128]{2,1,0:T(8,128)(2,1)S(1)}, u32[]{:S(2)}, u32[]{:S(2)}) collective-permute-start(bf16[16,128,128]{2,1,0:T(8,128)(2,1)} %shard_map.48), channel_id=1, source_target_pairs={{0,1},{3,2},{4,5},{7,6},{8,9},{11,10},{12,13},{15,14},{16,17},{19,... | collective-permute-start | bytes 1572872 | tf_op jit(solution)/shard_map/ppermute | solution.py:106
  25.1 44.4 %copy-start = (bf16[16,128,128]{2,1,0:T(8,128)(2,1)S(1)}, bf16[16,128,128]{2,1,0:T(8,128)(2,1)}, u32[]{:S(2)}) copy-start(bf16[16,128,128]{2,1,0:T(8,128)(2,1)} %shard_map.50) | copy-start | bytes 1572868
  25.1 44.3 %collective-permute-start.12 = (bf16[16,128,128]{2,1,0:T(8,128)(2,1)}, bf16[16,128,128]{2,1,0:T(8,128)(2,1)S(1)}, u32[]{:S(2)}, u32[]{:S(2)}) collective-permute-start(bf16[16,128,128]{2,1,0:T(8,128)(2,1)} %shard_map.50), channel_id=1, source_target_pairs={{0,1},{3,2},{4,5},{7,6},{8,9},{11,10},{12,13},{15,14},{16,17},{19,... | collective-permute-start | bytes 1572872 | tf_op jit(solution)/shard_map/ppermute | solution.py:106
  66.0 4.4 %collective-permute-start.19 = (bf16[16,128,128]{2,1,0:T(8,128)(2,1)S(1)}, bf16[16,128,128]{2,1,0:T(8,128)(2,1)S(1)}, u32[]{:S(2)}, u32[]{:S(2)}) collective-permute-start(bf16[16,128,128]{2,1,0:T(8,128)(2,1)S(1)} %fusion.19), channel_id=1, source_target_pairs={{1,2},{2,1},{5,6},{6,5},{9,10},{10,9},{13,14},{14,13},{17,18},{18,... | collective-permute-start | bytes 1572872 | tf_op jit(solution)/shard_map/ppermute | solution.py:106
  67.9 3.9 %collective-permute-start.1 = (bf16[16,128,128]{2,1,0:T(8,128)(2,1)S(1)}, bf16[16,128,128]{2,1,0:T(8,128)(2,1)S(1)}, u32[]{:S(2)}, u32[]{:S(2)}) collective-permute-start(bf16[16,128,128]{2,1,0:T(8,128)(2,1)S(1)} %fusion.16), channel_id=1, source_target_pairs={{1,2},{2,1},{5,6},{6,5},{9,10},{10,9},{13,14},{14,13},{17,18},{18,... | collective-permute-start | bytes 1572872 | tf_op jit(solution)/shard_map/ppermute | solution.py:106
  68.8 4.5 %collective-permute-start.7 = (bf16[16,128,128]{2,1,0:T(8,128)(2,1)S(1)}, bf16[16,128,128]{2,1,0:T(8,128)(2,1)S(1)}, u32[]{:S(2)}, u32[]{:S(2)}) collective-permute-start(bf16[16,128,128]{2,1,0:T(8,128)(2,1)S(1)} %fusion.17), channel_id=1, source_target_pairs={{1,2},{2,1},{5,6},{6,5},{9,10},{10,9},{13,14},{14,13},{17,18},{18,... | collective-permute-start | bytes 1572872 | tf_op jit(solution)/shard_map/ppermute | solution.py:106
  69.6 5.1 %collective-permute-start.13 = (bf16[16,128,128]{2,1,0:T(8,128)(2,1)S(1)}, bf16[16,128,128]{2,1,0:T(8,128)(2,1)S(1)}, u32[]{:S(2)}, u32[]{:S(2)}) collective-permute-start(bf16[16,128,128]{2,1,0:T(8,128)(2,1)S(1)} %fusion.18), channel_id=1, source_target_pairs={{1,2},{2,1},{5,6},{6,5},{9,10},{10,9},{13,14},{14,13},{17,18},{18,... | collective-permute-start | bytes 1572872 | tf_op jit(solution)/shard_map/ppermute | solution.py:106
  70.5 23.3 %collective-permute-start.20 = (bf16[16,128,128]{2,1,0:T(8,128)(2,1)S(1)}, bf16[16,128,128]{2,1,0:T(8,128)(2,1)S(1)}, u32[]{:S(2)}, u32[]{:S(2)}) collective-permute-start(bf16[16,128,128]{2,1,0:T(8,128)(2,1)S(1)} %fusion.12), channel_id=1, source_target_pairs={{2,3},{1,0},{6,7},{5,4},{10,11},{9,8},{14,15},{13,12},{18,19},{17,... | collective-permute-start | bytes 1572872 | tf_op jit(solution)/shard_map/ppermute | solution.py:106
  72.0 33.1 %collective-permute-start.2 = (bf16[16,128,128]{2,1,0:T(8,128)(2,1)S(1)}, bf16[16,128,128]{2,1,0:T(8,128)(2,1)S(1)}, u32[]{:S(2)}, u32[]{:S(2)}) collective-permute-start(bf16[16,128,128]{2,1,0:T(8,128)(2,1)S(1)} %fusion), channel_id=1, source_target_pairs={{2,3},{1,0},{6,7},{5,4},{10,11},{9,8},{14,15},{13,12},{18,19},{17,... | collective-permute-start | bytes 1572872 | tf_op jit(solution)/shard_map/ppermute | solution.py:106
  73.3 92.9 %copy-start.6 = (bf16[16,128,128]{2,1,0:T(8,128)(2,1)}, bf16[16,128,128]{2,1,0:T(8,128)(2,1)S(1)}, u32[]{:S(2)}) copy-start(bf16[16,128,128]{2,1,0:T(8,128)(2,1)S(1)} %collective-permute-done.7) | copy-start | bytes 1572868
  73.4 42.9 %collective-permute-start.8 = (bf16[16,128,128]{2,1,0:T(8,128)(2,1)S(1)}, bf16[16,128,128]{2,1,0:T(8,128)(2,1)S(1)}, u32[]{:S(2)}, u32[]{:S(2)}) collective-permute-start(bf16[16,128,128]{2,1,0:T(8,128)(2,1)S(1)} %fusion.4), channel_id=1, source_target_pairs={{2,3},{1,0},{6,7},{5,4},{10,11},{9,8},{14,15},{13,12},{18,19},{17,... | collective-permute-start | bytes 1572872 | tf_op jit(solution)/shard_map/ppermute | solution.py:106
  74.8 98.4 %copy-start.4 = (bf16[16,128,128]{2,1,0:T(8,128)(2,1)}, bf16[16,128,128]{2,1,0:T(8,128)(2,1)S(1)}, u32[]{:S(2)}) copy-start(bf16[16,128,128]{2,1,0:T(8,128)(2,1)S(1)} %collective-permute-done.13) | copy-start | bytes 1572868
  74.9 49.6 %collective-permute-start.14 = (bf16[16,128,128]{2,1,0:T(8,128)(2,1)S(1)}, bf16[16,128,128]{2,1,0:T(8,128)(2,1)S(1)}, u32[]{:S(2)}, u32[]{:S(2)}) collective-permute-start(bf16[16,128,128]{2,1,0:T(8,128)(2,1)S(1)} %fusion.8), channel_id=1, source_target_pairs={{2,3},{1,0},{6,7},{5,4},{10,11},{9,8},{14,15},{13,12},{18,19},{17,... | collective-permute-start | bytes 1572872 | tf_op jit(solution)/shard_map/ppermute | solution.py:106
  95.2 31.2 %collective-permute-start.21 = (bf16[16,128,128]{2,1,0:T(8,128)(2,1)S(1)}, bf16[16,128,128]{2,1,0:T(8,128)(2,1)S(1)}, u32[]{:S(2)}, u32[]{:S(2)}) collective-permute-start(bf16[16,128,128]{2,1,0:T(8,128)(2,1)S(1)} %fusion.20), channel_id=1, source_target_pairs={{0,8},{4,12},{8,0},{12,4},{16,24},{20,28},{24,16},{28,20},{1,9},{5... | collective-permute-start | bytes 1572872 | tf_op jit(solution)/shard_map/ppermute | solution.py:116
  106.5 24.9 %collective-permute-start.3 = (bf16[16,128,128]{2,1,0:T(8,128)(2,1)S(1)}, bf16[16,128,128]{2,1,0:T(8,128)(2,1)S(1)}, u32[]{:S(2)}, u32[]{:S(2)}) collective-permute-start(bf16[16,128,128]{2,1,0:T(8,128)(2,1)S(1)} %fusion.23), channel_id=1, source_target_pairs={{0,8},{4,12},{8,0},{12,4},{16,24},{20,28},{24,16},{28,20},{1,9},{5... | collective-permute-start | bytes 1572872 | tf_op jit(solution)/shard_map/ppermute | solution.py:116
  116.3 49.8 %copy-start.10 = (bf16[16,128,128]{2,1,0:T(8,128)(2,1)}, bf16[16,128,128]{2,1,0:T(8,128)(2,1)S(1)}, u32[]{:S(2)}) copy-start(bf16[16,128,128]{2,1,0:T(8,128)(2,1)S(1)} %collective-permute-done.8) | copy-start | bytes 1572868
  116.7 17.5 %collective-permute-start.9 = (bf16[16,128,128]{2,1,0:T(8,128)(2,1)S(1)}, bf16[16,128,128]{2,1,0:T(8,128)(2,1)S(1)}, u32[]{:S(2)}, u32[]{:S(2)}) collective-permute-start(bf16[16,128,128]{2,1,0:T(8,128)(2,1)S(1)} %fusion.22), channel_id=1, source_target_pairs={{0,8},{4,12},{8,0},{12,4},{16,24},{20,28},{24,16},{28,20},{1,9},{5... | collective-permute-start | bytes 1572872 | tf_op jit(solution)/shard_map/ppermute | solution.py:116
  124.5 48.6 %copy-start.8 = (bf16[16,128,128]{2,1,0:T(8,128)(2,1)}, bf16[16,128,128]{2,1,0:T(8,128)(2,1)S(1)}, u32[]{:S(2)}) copy-start(bf16[16,128,128]{2,1,0:T(8,128)(2,1)S(1)} %collective-permute-done.14) | copy-start | bytes 1572868
  124.9 13.3 %collective-permute-start.15 = (bf16[16,128,128]{2,1,0:T(8,128)(2,1)S(1)}, bf16[16,128,128]{2,1,0:T(8,128)(2,1)S(1)}, u32[]{:S(2)}, u32[]{:S(2)}) collective-permute-start(bf16[16,128,128]{2,1,0:T(8,128)(2,1)S(1)} %fusion.21), channel_id=1, source_target_pairs={{0,8},{4,12},{8,0},{12,4},{16,24},{20,28},{24,16},{28,20},{1,9},{5... | collective-permute-start | bytes 1572872 | tf_op jit(solution)/shard_map/ppermute | solution.py:116
  127.9 15.8 %collective-permute-start.22 = (bf16[16,128,128]{2,1,0:T(8,128)(2,1)S(1)}, bf16[16,128,128]{2,1,0:T(8,128)(2,1)S(1)}, u32[]{:S(2)}, u32[]{:S(2)}) collective-permute-start(bf16[16,128,128]{2,1,0:T(8,128)(2,1)S(1)} %fusion.15), channel_id=1, source_target_pairs={{0,16},{4,20},{8,24},{12,28},{1,17},{5,21},{9,25},{13,29},{2,18},{... | collective-permute-start | bytes 1572872 | tf_op jit(solution)/shard_map/ppermute | solution.py:116
  132.8 22.1 %collective-permute-start.4 = (bf16[16,128,128]{2,1,0:T(8,128)(2,1)S(1)}, bf16[16,128,128]{2,1,0:T(8,128)(2,1)S(1)}, u32[]{:S(2)}, u32[]{:S(2)}) collective-permute-start(bf16[16,128,128]{2,1,0:T(8,128)(2,1)S(1)} %fusion.3), channel_id=1, source_target_pairs={{0,16},{4,20},{8,24},{12,28},{1,17},{5,21},{9,25},{13,29},{2,18},{... | collective-permute-start | bytes 1572872 | tf_op jit(solution)/shard_map/ppermute | solution.py:116
  134.6 31.5 %collective-permute-start.10 = (bf16[16,128,128]{2,1,0:T(8,128)(2,1)S(1)}, bf16[16,128,128]{2,1,0:T(8,128)(2,1)S(1)}, u32[]{:S(2)}, u32[]{:S(2)}) collective-permute-start(bf16[16,128,128]{2,1,0:T(8,128)(2,1)S(1)} %fusion.7), channel_id=1, source_target_pairs={{0,16},{4,20},{8,24},{12,28},{1,17},{5,21},{9,25},{13,29},{2,18},{... | collective-permute-start | bytes 1572872 | tf_op jit(solution)/shard_map/ppermute | solution.py:116
  138.6 34.5 %collective-permute-start.16 = (bf16[16,128,128]{2,1,0:T(8,128)(2,1)S(1)}, bf16[16,128,128]{2,1,0:T(8,128)(2,1)S(1)}, u32[]{:S(2)}, u32[]{:S(2)}) collective-permute-start(bf16[16,128,128]{2,1,0:T(8,128)(2,1)S(1)} %fusion.11), channel_id=1, source_target_pairs={{0,16},{4,20},{8,24},{12,28},{1,17},{5,21},{9,25},{13,29},{2,18},{... | collective-permute-start | bytes 1572872 | tf_op jit(solution)/shard_map/ppermute | solution.py:116
  145.2 29.3 %collective-permute-start.23 = (bf16[16,128,128]{2,1,0:T(8,128)(2,1)S(1)}, bf16[16,128,128]{2,1,0:T(8,128)(2,1)S(1)}, u32[]{:S(2)}, u32[]{:S(2)}) collective-permute-start(bf16[16,128,128]{2,1,0:T(8,128)(2,1)S(1)} %add_convert_fusion.1), channel_id=1, source_target_pairs={{0,4},{4,0},{8,12},{12,8},{16,20},{20,16},{24,28},{28,24},{1,5},{5... | collective-permute-start | bytes 1572872 | tf_op jit(solution)/shard_map/ppermute | solution.py:122
  156.5 19.5 %collective-permute-start.5 = (bf16[16,128,128]{2,1,0:T(8,128)(2,1)S(1)}, bf16[16,128,128]{2,1,0:T(8,128)(2,1)S(1)}, u32[]{:S(2)}, u32[]{:S(2)}) collective-permute-start(bf16[16,128,128]{2,1,0:T(8,128)(2,1)S(1)} %add_convert_fusion.7), channel_id=1, source_target_pairs={{0,4},{4,0},{8,12},{12,8},{16,20},{20,16},{24,28},{28,24},{1,5},{5... | collective-permute-start | bytes 1572872 | tf_op jit(solution)/shard_map/ppermute | solution.py:122
  167.5 22.1 %collective-permute-start.11 = (bf16[16,128,128]{2,1,0:T(8,128)(2,1)}, bf16[16,128,128]{2,1,0:T(8,128)(2,1)}, u32[]{:S(2)}, u32[]{:S(2)}) collective-permute-start(bf16[16,128,128]{2,1,0:T(8,128)(2,1)} %add_convert_fusion.5), channel_id=1, source_target_pairs={{0,4},{4,0},{8,12},{12,8},{16,20},{20,16},{24,28},{28,24},{1,5},{5... | collective-permute-start | bytes 1572872 | tf_op jit(solution)/shard_map/ppermute | solution.py:122
  174.5 23.7 %collective-permute-start.17 = (bf16[16,128,128]{2,1,0:T(8,128)(2,1)}, bf16[16,128,128]{2,1,0:T(8,128)(2,1)}, u32[]{:S(2)}, u32[]{:S(2)}) collective-permute-start(bf16[16,128,128]{2,1,0:T(8,128)(2,1)} %add_convert_fusion.3), channel_id=1, source_target_pairs={{0,4},{4,0},{8,12},{12,8},{16,20},{20,16},{24,28},{28,24},{1,5},{5... | collective-permute-start | bytes 1572872 | tf_op jit(solution)/shard_map/ppermute | solution.py:122
  (15 other events, 150.0 us)

commit v2 on v0

v2 whole, which is shorter than its diff:
```python
import functools

import jax
import jax.numpy as jnp
from jax import lax
from jax.experimental import pallas as pl
from jax.experimental.pallas import tpu as pltpu
from jax.sharding import PartitionSpec as P

HD = 128
SIZES = ((16, 1),) * 4
LOCAL_STEP = 8
LOCAL_SWAP = 4
LOCAL_TIE = True
STEPS = "0 1 2 3 0 1,01 2,11 3,21 0 1 2 3 0 1 2 3 0 1 2 3 0 1 2 3 0 1 2 3"
VMEM = 24 << 20


def f32(block):
    return block.astype(jnp.float32)


def packed(total):
    return total.astype(jnp.bfloat16)


def added(*terms):
    return functools.reduce(jnp.add, [f32(term) for term in terms])


def kept(condition, block):
    return jnp.where(condition, f32(block), 0.0)


def state_kernel(side_ref, key_ref, value_ref, mine_ref, theirs_ref):
    half = mine_ref.shape[0]
    for side, state_ref in enumerate((mine_ref, theirs_ref)):
        base = (side_ref[0] ^ side) * half
        for head in range(half):
            columns = pl.ds(pl.multiple_of((base + head) * HD, HD), HD)
            state = lax.dot_general(
                key_ref[:, columns],
                value_ref[:, columns],
                (((0,), (0,)), ((), ())),
                preferred_element_type=jnp.float32,
            )
            state_ref[head] = packed(state)


def states_of(side, key_vectors, value_vectors, first, step, steps):
    tokens, half = key_vectors.shape[0], step // 2
    tokens_spec = pl.BlockSpec((tokens, step * HD), lambda i, side: (0, first // step + i))
    side_spec = pl.BlockSpec((half, HD, HD), lambda i, side: (i, 0, 0))
    half_shape = jax.ShapeDtypeStruct((steps * half, HD, HD), jnp.bfloat16)
    return pl.pallas_call(
        state_kernel,
        grid_spec=pltpu.PrefetchScalarGridSpec(
            num_scalar_prefetch=1,
            grid=(steps,),
            in_specs=[tokens_spec, tokens_spec],
            out_specs=[side_spec, side_spec],
        ),
        out_shape=[half_shape, half_shape],
        compiler_params=pltpu.CompilerParams(vmem_limit_bytes=VMEM),
        cost_estimate=pl.CostEstimate(
            flops=2 * tokens * HD * HD * step * steps,
            bytes_accessed=2 * step * steps * HD * (2 * tokens + HD),
            transcendentals=0,
        ),
    )(side, key_vectors, value_vectors)


def local_kernel(query_ref, key_ref, value_ref, local_ref):
    tokens = query_ref.shape[0]
    rows = lax.broadcasted_iota(jnp.int32, (tokens, tokens), 0)
    causal = rows >= lax.broadcasted_iota(jnp.int32, (tokens, tokens), 1)
    for head in range(query_ref.shape[1] // HD):
        columns = slice(head * HD, (head + 1) * HD)
        scores = lax.dot_general(
            query_ref[:, columns],
            key_ref[:, columns],
            (((1,), (1,)), ((), ())),
            preferred_element_type=jnp.float32,
        )
        scores = packed(jnp.where(causal, scores, 0.0))
        local_ref[:, columns] = jnp.dot(scores, value_ref[:, columns], preferred_element_type=jnp.float32)


def locals_of(queries, key_vectors, value_vectors, first, count):
    tokens, step = queries.shape[0], min(count, LOCAL_STEP)
    tokens_spec = pl.BlockSpec((tokens, step * HD), lambda i: (0, first // step + i))
    return pl.pallas_call(
        local_kernel,
        grid=(count // step,),
        in_specs=[tokens_spec] * 3,
        out_specs=pl.BlockSpec((tokens, step * HD), lambda i: (0, i)),
        out_shape=jax.ShapeDtypeStruct((tokens, count * HD), jnp.float32),
        compiler_params=pltpu.CompilerParams(vmem_limit_bytes=VMEM),
        cost_estimate=pl.CostEstimate(
            flops=4 * tokens * HD * count * tokens,
            bytes_accessed=count * HD * 10 * tokens,
            transcendentals=0,
        ),
    )(queries, key_vectors, value_vectors)


def output_kernel(side_ref, query_ref, local_ref, mine_ref, theirs_ref, gain_ref, *refs):
    out_ref = refs[-1]
    own = pl.program_id(0) == 0
    for head in range(mine_ref.shape[0]):
        columns = slice(head * HD, (head + 1) * HD)
        carried = jnp.where(own, mine_ref[head], theirs_ref[head])
        raw = jnp.dot(query_ref[:, columns], carried, preferred_element_type=jnp.float32) + local_ref[:, columns]
        scale = lax.rsqrt(jnp.mean(raw * raw, axis=-1, keepdims=True) + 1e-06)
        out_ref[:, columns] = packed(raw * scale * gain_ref[head])


def outputs_of(side, queries, local, mine, theirs, gain, first, before):
    tokens, half = queries.shape[0], mine.shape[0]
    tokens_spec = pl.BlockSpec((tokens, half * HD), lambda i, side: (0, first // half + (side[0] ^ i)))
    local_spec = pl.BlockSpec((tokens, half * HD), lambda i, side: (0, side[0] ^ i))
    side_spec = pl.BlockSpec((half, HD, HD), lambda i, side: (0, 0, 0))
    gain_spec = pl.BlockSpec((half, 1, HD), lambda i, side: (first // half + (side[0] ^ i), 0, 0))
    operands = [queries, local, mine, theirs, gain]
    in_specs = [tokens_spec, local_spec, side_spec, side_spec, gain_spec]
    aliases = {}
    if before is not None:
        operands.append(before)
        in_specs.append(pl.BlockSpec(memory_space=pl.ANY))
        aliases = {6: 0}
    return pl.pallas_call(
        output_kernel,
        grid_spec=pltpu.PrefetchScalarGridSpec(
            num_scalar_prefetch=1, grid=(2,), in_specs=in_specs, out_specs=tokens_spec
        ),
        out_shape=jax.ShapeDtypeStruct(queries.shape, jnp.bfloat16),
        input_output_aliases=aliases,
        compiler_params=pltpu.CompilerParams(vmem_limit_bytes=VMEM),
        cost_estimate=pl.CostEstimate(
            flops=4 * tokens * HD * half * HD,
            bytes_accessed=2 * half * HD * (8 * tokens + HD),
            transcendentals=2 * tokens * half,
        ),
    )(side, *operands)


def after(block, done):
    return lax.optimization_barrier((block, *done))[0] if done else block


def swapped(block, axis, step):
    return lax.ppermute(block, axis, [(i, i ^ step) for i in range(lax.axis_size(axis))])


def scan_of(mine, theirs, extra):
    half, side = mine.shape[0], lax.axis_index("head") % 2
    done = yield
    sent = theirs if extra is None else jnp.concatenate([theirs, extra])
    arrived = swapped(after(sent, done), "head", 1)
    arrived = after(arrived, (yield arrived))
    neighbour = arrived[:half]
    whole = added(mine, neighbour)
    if extra is not None:
        extra = added(extra, arrived[half:])
    earlier = jnp.zeros_like(whole)
    for axis, step in [("head", 2), ("seq", 1)]:
        index = lax.axis_index(axis)
        while step < lax.axis_size(axis):
            sent = packed(whole)
            with_extra = extra is not None and axis == "head"
            if with_extra:
                sent = jnp.concatenate([sent, packed(extra)])
            arrived = swapped(sent, axis, step)
            if (axis, step) in (("head", 2), ("seq", 1), ("seq", 2), ("seq", 4)):
                arrived = after(arrived, (yield arrived))
            earlier += kept(index & step != 0, arrived[:half])
            whole += f32(arrived[:half])
            if with_extra:
                extra = extra + f32(arrived[half:])
            step *= 2
    carried_mine = packed(earlier + kept(side == 1, neighbour))
    carried_theirs = packed(earlier + kept(side == 0, mine))
    arrived = swapped(carried_theirs, "head", 1)
    arrived = after(arrived, (yield arrived))
    yield carried_mine, arrived, extra


def parts_of(gain, heads):
    rows = jnp.zeros((heads, HD), jnp.float32)
    rows = lax.dynamic_update_slice(rows, gain, (lax.axis_index("head") * gain.shape[0], 0))
    parts = []
    for _ in range(3):
        part = lax.reduce_precision(rows, 8, 7)
        parts.append(packed(part))
        rows = rows - part
    parts.append(jnp.zeros((-3 * heads % HD, HD), jnp.bfloat16))
    return jnp.concatenate(parts).reshape(-1, HD, HD)


def per_device(queries, key_vectors, value_vectors, out_gain):
    heads = queries.shape[1] // HD
    side = (lax.axis_index("head") % 2).astype(jnp.int32).reshape(1)
    gain_parts = parts_of(out_gain, heads)


    firsts, sizes, scans, locals_by_piece = [], [], [], {}
    first = 0
    for size, count in SIZES:
        own, other = states_of(side, key_vectors, value_vectors, first, size, count)
        for piece in range(count):
            part = slice(piece * size // 2, (piece + 1) * size // 2)
            scans.append(scan_of(own[part], other[part], None if scans else gain_parts))
            firsts.append(first)
            sizes.append(size)
            first += size
            next(scans[-1])

    count = len(scans)
    done, out, gain = [[] for _ in scans], None, None
    for step in STEPS.split():
        piece, *wait_for = step.split(",")
        piece = int(piece)
        wait_for = [done[int(item[0])][int(item[1])] for item in wait_for]
        swap = len(done[piece])
        if swap == LOCAL_SWAP:
            local = locals_of(queries, key_vectors, value_vectors, firsts[piece], sizes[piece])
            wait_for += [local] if LOCAL_TIE else []
        result = scans[piece].send(wait_for)
        if swap == LOCAL_SWAP:
            locals_by_piece[piece] = local
        if isinstance(result, tuple):
            mine, theirs, extra = result
            if extra is not None:
                rows = extra.reshape(-1, HD)
                gain = rows[:heads] + rows[heads : 2 * heads] + rows[2 * heads : 3 * heads]
                gain = gain.reshape(heads, 1, HD)
            out = outputs_of(side, queries, locals_by_piece[piece], mine, theirs, gain, firsts[piece], out)
            result = out
        done[piece].append(result)
    return out


def solution(mesh):
    return jax.shard_map(
        per_device,
        mesh=mesh,
        in_specs=(
            P(("seq", "head"), None),
            P(("seq", "head"), None),
            P(("seq", "head"), None),
            P("head", None),
        ),
        out_specs=P(("seq", "head"), None),
        check_vma=False,
    )
```

time: 592 us -> 125 us (0.21)
  the two profiles are of different devices: /device:TPU:3 before, /device:TPU:0 now
where the time goes in v2:
time: 125 us; the launch traced here: 124 us
  waiting for transfers between devices  39.4 us (32%)
  starting transfers between devices  29.5 us (24%)
  other arithmetic  23.6 us (19%)
  Pallas kernels  22.3 us (18%)
  local copies, waits for them, and re-layouts  9.16 us (7%)
    ppermute x24, waiting for transfers between devices, swapped(): lax.ppermute(block, axis, [(i, i ^ step) for i in range(lax.axis_size(axi...  39.4 us
    ppermute x24, starting transfers between devices, swapped(): lax.ppermute(block, axis, [(i, i ^ step) for i in range(lax.axis_size(axi...  29.5 us
    convert_element_type x22, other arithmetic, packed(): return total.astype(jnp.bfloat16)  21.8 us
    pallas_call x4, Pallas kernels, locals_of(): pl.pallas_call(local_kernel, grid=(count // step,), in_specs=[tokens_spec...  8.79 us
    pallas_call x4, Pallas kernels, outputs_of(): pl.pallas_call(output_kernel, grid_spec=pltpu.PrefetchScalarGridSpec(num_...  8.42 us
    unnamed x24, local copies, waits for them, and re-layouts  8.38 us
    pallas_call x4, Pallas kernels, states_of(): pl.pallas_call(state_kernel, grid_spec=pltpu.PrefetchScalarGridSpec(num_s...  5.12 us
  transfers between devices with their start and end apart: 24, of which 7 were waited for; matrix products, arithmetic and copies ran while one was open for 18% of the time, Pallas kernels for 16%

profile of v2, /device:TPU:0, one launch (start us, length us, event | category | flops | bytes accessed | tf_op | source)
XLA Modules:
  0.0 124.4 jit_solution(1488657852603607541)
XLA Ops:
  0.8 2.2 %copy-done.2 = bf16[256,8192]{1,0:T(8,128)(2,1)S(1)} copy-done((bf16[256,8192]{1,0:T(8,128)(2,1)S(1)}, bf16[256,8192]{1,0:T(8,128)(2,1)}, u32[]{:S(2)}) %copy-start.2) | copy-done | bytes 4194328
  3.0 2.2 %copy-done.3 = bf16[256,8192]{1,0:T(8,128)(2,1)S(1)} copy-done((bf16[256,8192]{1,0:T(8,128)(2,1)S(1)}, bf16[256,8192]{1,0:T(8,128)(2,1)}, u32[]{:S(2)}) %copy-start.3) | copy-done | bytes 4194328
  6.3 3.1 %collective-permute-start.3 = (bf16[10,128,128]{2,1,0:T(8,128)(2,1)S(1)}, bf16[10,128,128]{2,1,0:T(8,128)(2,1)S(1)}, u32[]{:S(2)}, u32[]{:S(2)}) collective-permute-start(bf16[10,128,128]{2,1,0:T(8,128)(2,1)S(1)} %pad_maximum_fusion), channel_id=1, source_target_pairs={{0,1},{1,0},{2,3},{3,2},{4,5},{5,4},{6,7},{7,6},{8,9},{9,8},{10,11... | collective-permute-start | bytes 983048 | tf_op jit(solution)/shard_map/ppermute | solution.py:152
  9.4 7.7 %collective-permute-done.3 = bf16[10,128,128]{2,1,0:T(8,128)(2,1)S(1)} collective-permute-done((bf16[10,128,128]{2,1,0:T(8,128)(2,1)S(1)}, bf16[10,128,128]{2,1,0:T(8,128)(2,1)S(1)}, u32[]{:S(2)}, u32[]{:S(2)}) %collective-permute-start.3) | collective-permute-done | bytes 327712 | tf_op jit(solution)/shard_map/ppermute | solution.py:152
  18.0 2.8 %collective-permute-start.4 = (bf16[10,128,128]{2,1,0:T(8,128)(2,1)}, bf16[10,128,128]{2,1,0:T(8,128)(2,1)}, u32[]{:S(2)}, u32[]{:S(2)}) collective-permute-start(bf16[10,128,128]{2,1,0:T(8,128)(2,1)} %pad_maximum_fusion.1), channel_id=1, source_target_pairs={{0,2},{1,3},{2,0},{3,1},{4,6},{5,7},{6,4},{7,5},{8,10},{9,11},{10,... | collective-permute-start | bytes 983048 | tf_op jit(solution)/shard_map/ppermute | solution.py:152
  20.7 1.6 %shard_map.49 = (bf16[8,128,128]{2,1,0:T(8,128)(2,1)S(1)}, bf16[8,128,128]{2,1,0:T(8,128)(2,1)}) custom-call(s32[1]{0:T(128)} %bitcast.side_ref, bf16[256,8192]{1,0:T(8,128)(2,1)S(1)} %copy-done.2, bf16[256,8192]{1,0:T(8,128)(2,1)S(1)} %copy-done.3), custom_call_target="tpu_custom_call" | custom-call | flops 134217728 | bytes 2621440 | tf_op jit(solution)/shard_map/pallas_call | solution.py:55
  22.3 1.6 %collective-permute-start.2 = (bf16[8,128,128]{2,1,0:T(8,128)(2,1)}, bf16[8,128,128]{2,1,0:T(8,128)(2,1)}, u32[]{:S(2)}, u32[]{:S(2)}) collective-permute-start(bf16[8,128,128]{2,1,0:T(8,128)(2,1)} %get-tuple-element.25), channel_id=1, source_target_pairs={{0,1},{1,0},{2,3},{3,2},{4,5},{5,4},{6,7},{7,6},{8,9},{9,8},{10,11... | collective-permute-start | bytes 786440 | tf_op jit(solution)/shard_map/ppermute | solution.py:152
  23.9 1.6 %shard_map.48 = (bf16[8,128,128]{2,1,0:T(8,128)(2,1)S(1)}, bf16[8,128,128]{2,1,0:T(8,128)(2,1)}) custom-call(s32[1]{0:T(128)} %bitcast.side_ref, bf16[256,8192]{1,0:T(8,128)(2,1)S(1)} %copy-done.2, bf16[256,8192]{1,0:T(8,128)(2,1)S(1)} %copy-done.3), custom_call_target="tpu_custom_call" | custom-call | flops 134217728 | bytes 2621440 | tf_op jit(solution)/shard_map/pallas_call | solution.py:55
  26.9 1.6 %collective-permute-start = (bf16[8,128,128]{2,1,0:T(8,128)(2,1)S(1)}, bf16[8,128,128]{2,1,0:T(8,128)(2,1)}, u32[]{:S(2)}, u32[]{:S(2)}) collective-permute-start(bf16[8,128,128]{2,1,0:T(8,128)(2,1)S(1)} %get-tuple-element.21), channel_id=1, source_target_pairs={{0,1},{1,0},{2,3},{3,2},{4,5},{5,4},{6,7},{7,6},{8,9},{9,8},{10,11... | collective-permute-start | bytes 786440 | tf_op jit(solution)/shard_map/ppermute | solution.py:152
  28.6 2.2 %shard_map.53.local_ref = f32[256,2048]{1,0:T(8,128)S(1)} custom-call(bf16[256,8192]{1,0:T(8,128)(2,1)S(1)} %copy-done, bf16[256,8192]{1,0:T(8,128)(2,1)S(1)} %copy-done.2, bf16[256,8192]{1,0:T(8,128)(2,1)S(1)} %copy-done.3), custom_call_target="tpu_custom_call" | custom-call | flops 536870912 | bytes 5242880 | tf_op jit(solution)/shard_map/pallas_call | solution.py:92
  32.1 2.2 %shard_map.52.local_ref = f32[256,2048]{1,0:T(8,128)S(1)} custom-call(bf16[256,8192]{1,0:T(8,128)(2,1)S(1)} %copy-done, bf16[256,8192]{1,0:T(8,128)(2,1)S(1)} %copy-done.2, bf16[256,8192]{1,0:T(8,128)(2,1)S(1)} %copy-done.3), custom_call_target="tpu_custom_call" | custom-call | flops 536870912 | bytes 5242880 | tf_op jit(solution)/shard_map/pallas_call | solution.py:92
  35.6 2.2 %shard_map.51.local_ref = f32[256,2048]{1,0:T(8,128)S(1)} custom-call(bf16[256,8192]{1,0:T(8,128)(2,1)S(1)} %copy-done, bf16[256,8192]{1,0:T(8,128)(2,1)S(1)} %copy-done.2, bf16[256,8192]{1,0:T(8,128)(2,1)S(1)} %copy-done.3), custom_call_target="tpu_custom_call" | custom-call | flops 536870912 | bytes 5242880 | tf_op jit(solution)/shard_map/pallas_call | solution.py:92
  39.2 2.2 %shard_map.46.local_ref = f32[256,2048]{1,0:T(8,128)S(1)} custom-call(bf16[256,8192]{1,0:T(8,128)(2,1)S(1)} %copy-done, bf16[256,8192]{1,0:T(8,128)(2,1)S(1)} %copy-done.2, bf16[256,8192]{1,0:T(8,128)(2,1)S(1)} %copy-done.3), custom_call_target="tpu_custom_call" | custom-call | flops 536870912 | bytes 5242880 | tf_op jit(solution)/shard_map/pallas_call | solution.py:92
  46.2 1.6 %collective-permute-start.21 = (bf16[8,128,128]{2,1,0:T(8,128)(2,1)S(1)}, bf16[8,128,128]{2,1,0:T(8,128)(2,1)S(1)}, u32[]{:S(2)}, u32[]{:S(2)}) collective-permute-start(bf16[8,128,128]{2,1,0:T(8,128)(2,1)S(1)} %fusion.39), channel_id=1, source_target_pairs={{0,8},{4,12},{8,0},{12,4},{16,24},{20,28},{24,16},{28,20},{1,9},{5... | collective-permute-start | bytes 786440 | tf_op jit(solution)/shard_map/ppermute | solution.py:152
  47.8 11.1 %collective-permute-done.5 = bf16[8,128,128]{2,1,0:T(8,128)(2,1)S(1)} collective-permute-done((bf16[8,128,128]{2,1,0:T(8,128)(2,1)S(1)}, bf16[8,128,128]{2,1,0:T(8,128)(2,1)S(1)}, u32[]{:S(2)}, u32[]{:S(2)}) %collective-permute-start.5) | collective-permute-done | bytes 262176 | tf_op jit(solution)/shard_map/ppermute | solution.py:152
  62.4 1.6 %collective-permute-start.22 = (bf16[8,128,128]{2,1,0:T(8,128)(2,1)S(1)}, bf16[8,128,128]{2,1,0:T(8,128)(2,1)S(1)}, u32[]{:S(2)}, u32[]{:S(2)}) collective-permute-start(bf16[8,128,128]{2,1,0:T(8,128)(2,1)S(1)} %fusion.31), channel_id=1, source_target_pairs={{0,16},{4,20},{8,24},{12,28},{16,0},{20,4},{24,8},{28,12},{1,17},{... | collective-permute-start | bytes 786440 | tf_op jit(solution)/shard_map/ppermute | solution.py:152
  65.0 1.6 %collective-permute-start.17 = (bf16[8,128,128]{2,1,0:T(8,128)(2,1)S(1)}, bf16[8,128,128]{2,1,0:T(8,128)(2,1)S(1)}, u32[]{:S(2)}, u32[]{:S(2)}) collective-permute-start(bf16[8,128,128]{2,1,0:T(8,128)(2,1)S(1)} %fusion.38), channel_id=1, source_target_pairs={{0,8},{4,12},{8,0},{12,4},{16,24},{20,28},{24,16},{28,20},{1,9},{5... | collective-permute-start | bytes 786440 | tf_op jit(solution)/shard_map/ppermute | solution.py:152
  66.6 7.5 %collective-permute-done.6 = bf16[8,128,128]{2,1,0:T(8,128)(2,1)S(1)} collective-permute-done((bf16[8,128,128]{2,1,0:T(8,128)(2,1)S(1)}, bf16[8,128,128]{2,1,0:T(8,128)(2,1)S(1)}, u32[]{:S(2)}, u32[]{:S(2)}) %collective-permute-start.6) | collective-permute-done | bytes 262176 | tf_op jit(solution)/shard_map/ppermute | solution.py:152
  77.7 3.2 %collective-permute-start.23 = (bf16[8,128,128]{2,1,0:T(8,128)(2,1)S(1)}, bf16[8,128,128]{2,1,0:T(8,128)(2,1)S(1)}, u32[]{:S(2)}, u32[]{:S(2)}) collective-permute-start(bf16[8,128,128]{2,1,0:T(8,128)(2,1)S(1)} %get-tuple-element.35), channel_id=1, source_target_pairs={{0,1},{1,0},{2,3},{3,2},{4,5},{5,4},{6,7},{7,6},{8,9},{9,8},{10,11... | collective-permute-start | bytes 786440 | tf_op jit(solution)/shard_map/ppermute | solution.py:152
  82.0 1.6 %collective-permute-start.18 = (bf16[8,128,128]{2,1,0:T(8,128)(2,1)S(1)}, bf16[8,128,128]{2,1,0:T(8,128)(2,1)S(1)}, u32[]{:S(2)}, u32[]{:S(2)}) collective-permute-start(bf16[8,128,128]{2,1,0:T(8,128)(2,1)S(1)} %fusion.27), channel_id=1, source_target_pairs={{0,16},{4,20},{8,24},{12,28},{16,0},{20,4},{24,8},{28,12},{1,17},{... | collective-permute-start | bytes 786440 | tf_op jit(solution)/shard_map/ppermute | solution.py:152
  84.7 1.6 %collective-permute-start.13 = (bf16[8,128,128]{2,1,0:T(8,128)(2,1)S(1)}, bf16[8,128,128]{2,1,0:T(8,128)(2,1)S(1)}, u32[]{:S(2)}, u32[]{:S(2)}) collective-permute-start(bf16[8,128,128]{2,1,0:T(8,128)(2,1)S(1)} %fusion.37), channel_id=1, source_target_pairs={{0,8},{4,12},{8,0},{12,4},{16,24},{20,28},{24,16},{28,20},{1,9},{5... | collective-permute-start | bytes 786440 | tf_op jit(solution)/shard_map/ppermute | solution.py:152
  86.3 5.3 %collective-permute-done.7 = bf16[8,128,128]{2,1,0:T(8,128)(2,1)S(1)} collective-permute-done((bf16[8,128,128]{2,1,0:T(8,128)(2,1)S(1)}, bf16[8,128,128]{2,1,0:T(8,128)(2,1)S(1)}, u32[]{:S(2)}, u32[]{:S(2)}) %collective-permute-start.7) | collective-permute-done | bytes 262176 | tf_op jit(solution)/shard_map/ppermute | solution.py:152
  95.5 1.6 %collective-permute-start.9 = (bf16[8,128,128]{2,1,0:T(8,128)(2,1)S(1)}, bf16[8,128,128]{2,1,0:T(8,128)(2,1)S(1)}, u32[]{:S(2)}, u32[]{:S(2)}) collective-permute-start(bf16[8,128,128]{2,1,0:T(8,128)(2,1)S(1)} %fusion.36), channel_id=1, source_target_pairs={{0,8},{4,12},{8,0},{12,4},{16,24},{20,28},{24,16},{28,20},{1,9},{5... | collective-permute-start | bytes 786440 | tf_op jit(solution)/shard_map/ppermute | solution.py:152
  98.3 1.6 %collective-permute-start.14 = (bf16[8,128,128]{2,1,0:T(8,128)(2,1)S(1)}, bf16[8,128,128]{2,1,0:T(8,128)(2,1)S(1)}, u32[]{:S(2)}, u32[]{:S(2)}) collective-permute-start(bf16[8,128,128]{2,1,0:T(8,128)(2,1)S(1)} %fusion.23), channel_id=1, source_target_pairs={{0,16},{4,20},{8,24},{12,28},{16,0},{20,4},{24,8},{28,12},{1,17},{... | collective-permute-start | bytes 786440 | tf_op jit(solution)/shard_map/ppermute | solution.py:152
  99.9 4.3 %collective-permute-done.9 = bf16[8,128,128]{2,1,0:T(8,128)(2,1)S(1)} collective-permute-done((bf16[8,128,128]{2,1,0:T(8,128)(2,1)S(1)}, bf16[8,128,128]{2,1,0:T(8,128)(2,1)S(1)}, u32[]{:S(2)}, u32[]{:S(2)}) %collective-permute-start.9) | collective-permute-done | bytes 262176 | tf_op jit(solution)/shard_map/ppermute | solution.py:152
  105.3 1.6 %collective-permute-start.10 = (bf16[8,128,128]{2,1,0:T(8,128)(2,1)S(1)}, bf16[8,128,128]{2,1,0:T(8,128)(2,1)S(1)}, u32[]{:S(2)}, u32[]{:S(2)}) collective-permute-start(bf16[8,128,128]{2,1,0:T(8,128)(2,1)S(1)} %fusion.19), channel_id=1, source_target_pairs={{0,16},{4,20},{8,24},{12,28},{16,0},{20,4},{24,8},{28,12},{1,17},{... | collective-permute-start | bytes 786440 | tf_op jit(solution)/shard_map/ppermute | solution.py:152
  108.2 1.6 %collective-permute-start.15 = (bf16[8,128,128]{2,1,0:T(8,128)(2,1)S(1)}, bf16[8,128,128]{2,1,0:T(8,128)(2,1)S(1)}, u32[]{:S(2)}, u32[]{:S(2)}) collective-permute-start(bf16[8,128,128]{2,1,0:T(8,128)(2,1)S(1)} %get-tuple-element.39), channel_id=1, source_target_pairs={{0,1},{1,0},{2,3},{3,2},{4,5},{5,4},{6,7},{7,6},{8,9},{9,8},{10,11... | collective-permute-start | bytes 786440 | tf_op jit(solution)/shard_map/ppermute | solution.py:152
  109.9 3.3 %collective-permute-done.10 = bf16[8,128,128]{2,1,0:T(8,128)(2,1)S(1)} collective-permute-done((bf16[8,128,128]{2,1,0:T(8,128)(2,1)S(1)}, bf16[8,128,128]{2,1,0:T(8,128)(2,1)S(1)}, u32[]{:S(2)}, u32[]{:S(2)}) %collective-permute-start.10) | collective-permute-done | bytes 262176 | tf_op jit(solution)/shard_map/ppermute | solution.py:152
  115.9 2.1 %shard_map.54.refs_0_ = bf16[256,8192]{1,0:T(8,128)(2,1)} custom-call(s32[1]{0:T(128)} %bitcast.side_ref, bf16[256,8192]{1,0:T(8,128)(2,1)S(1)} %copy-done.1, f32[256,2048]{1,0:T(8,128)S(1)} %copy-done.9, bf16[8,128,128]{2,1,0:T(8,128)(2,1)S(1)} %get-tuple-element.36.mine_ref, bf16[8,128,128]{2,1,0:T(8,128)(2,1)S(1)} %collective-permute-done.23.theirs_ref, ...), custom_call_target="tpu_custom_call" | custom-call | flops 134217728 | bytes 4456448 | tf_op jit(solution)/shard_map/pallas_call | solution.py:131
  118.1 2.1 %shard_map.55.refs_0_ = bf16[256,8192]{1,0:T(8,128)(2,1)} custom-call(s32[1]{0:T(128)} %bitcast.side_ref, bf16[256,8192]{1,0:T(8,128)(2,1)S(1)} %copy-done.1, f32[256,2048]{1,0:T(8,128)S(1)} %copy-done.7, bf16[8,128,128]{2,1,0:T(8,128)(2,1)S(1)} %get-tuple-element.38.mine_ref, ...), custom_call_target="tpu_custom_call", output_to_operand_aliasing={{}: (6, {})} | custom-call | flops 134217728 | bytes 4456448 | tf_op jit(solution)/shard_map/pallas_call | solution.py:131
  120.2 2.1 %shard_map.56.refs_0_ = bf16[256,8192]{1,0:T(8,128)(2,1)} custom-call(s32[1]{0:T(128)} %bitcast.side_ref, bf16[256,8192]{1,0:T(8,128)(2,1)S(1)} %copy-done.1, f32[256,2048]{1,0:T(8,128)S(1)} %copy-done.5, bf16[8,128,128]{2,1,0:T(8,128)(2,1)S(1)} %get-tuple-element.40.mine_ref, ...), custom_call_target="tpu_custom_call", output_to_operand_aliasing={{}: (6, {})} | custom-call | flops 134217728 | bytes 4456448 | tf_op jit(solution)/shard_map/pallas_call | solution.py:131
  122.3 2.1 %shard_map.57 = bf16[256,8192]{1,0:T(8,128)(2,1)} custom-call(s32[1]{0:T(128)} %bitcast.side_ref, bf16[256,8192]{1,0:T(8,128)(2,1)S(1)} %copy-done.1, f32[256,2048]{1,0:T(8,128)S(1)} %shard_map.46.local_ref, bf16[8,128,128]{2,1,0:T(8,128)(2,1)S(1)} %get-tuple-element.42.mine_ref, ...), custom_call_target="tpu_custom_call", output_to_operand_aliasing={{}: (6, {})} | custom-call | flops 134217728 | bytes 4456448 | tf_op jit(solution)/shard_map/pallas_call | solution.py:131
  (83 shorter events, 33.3 us)
Async XLA Ops:
  0.8 2.2 %copy-start.2 = (bf16[256,8192]{1,0:T(8,128)(2,1)S(1)}, bf16[256,8192]{1,0:T(8,128)(2,1)}, u32[]{:S(2)}) copy-start(bf16[256,8192]{1,0:T(8,128)(2,1)} %key_ref.15) | copy-start | bytes 12582916
  3.0 2.2 %copy-start.3 = (bf16[256,8192]{1,0:T(8,128)(2,1)S(1)}, bf16[256,8192]{1,0:T(8,128)(2,1)}, u32[]{:S(2)}) copy-start(bf16[256,8192]{1,0:T(8,128)(2,1)} %value_ref.15) | copy-start | bytes 12582916
  6.3 10.8 %collective-permute-start.3 = (bf16[10,128,128]{2,1,0:T(8,128)(2,1)S(1)}, bf16[10,128,128]{2,1,0:T(8,128)(2,1)S(1)}, u32[]{:S(2)}, u32[]{:S(2)}) collective-permute-start(bf16[10,128,128]{2,1,0:T(8,128)(2,1)S(1)} %pad_maximum_fusion), channel_id=1, source_target_pairs={{0,1},{1,0},{2,3},{3,2},{4,5},{5,4},{6,7},{7,6},{8,9},{9,8},{10,11... | collective-permute-start | bytes 983048 | tf_op jit(solution)/shard_map/ppermute | solution.py:152
  18.0 23.5 %collective-permute-start.4 = (bf16[10,128,128]{2,1,0:T(8,128)(2,1)}, bf16[10,128,128]{2,1,0:T(8,128)(2,1)}, u32[]{:S(2)}, u32[]{:S(2)}) collective-permute-start(bf16[10,128,128]{2,1,0:T(8,128)(2,1)} %pad_maximum_fusion.1), channel_id=1, source_target_pairs={{0,2},{1,3},{2,0},{3,1},{4,6},{5,7},{6,4},{7,5},{8,10},{9,11},{10,... | collective-permute-start | bytes 983048 | tf_op jit(solution)/shard_map/ppermute | solution.py:152
  22.3 20.4 %collective-permute-start.2 = (bf16[8,128,128]{2,1,0:T(8,128)(2,1)}, bf16[8,128,128]{2,1,0:T(8,128)(2,1)}, u32[]{:S(2)}, u32[]{:S(2)}) collective-permute-start(bf16[8,128,128]{2,1,0:T(8,128)(2,1)} %get-tuple-element.25), channel_id=1, source_target_pairs={{0,1},{1,0},{2,3},{3,2},{4,5},{5,4},{6,7},{7,6},{8,9},{9,8},{10,11... | collective-permute-start | bytes 786440 | tf_op jit(solution)/shard_map/ppermute | solution.py:152
  25.5 3.0 %copy-start = (bf16[256,8192]{1,0:T(8,128)(2,1)S(1)}, bf16[256,8192]{1,0:T(8,128)(2,1)}, u32[]{:S(2)}) copy-start(bf16[256,8192]{1,0:T(8,128)(2,1)} %query_ref.15) | copy-start | bytes 12582916
  25.5 34.6 %collective-permute-start.1 = (bf16[8,128,128]{2,1,0:T(8,128)(2,1)}, bf16[8,128,128]{2,1,0:T(8,128)(2,1)}, u32[]{:S(2)}, u32[]{:S(2)}) collective-permute-start(bf16[8,128,128]{2,1,0:T(8,128)(2,1)} %get-tuple-element.23), channel_id=1, source_target_pairs={{0,1},{1,0},{2,3},{3,2},{4,5},{5,4},{6,7},{7,6},{8,9},{9,8},{10,11... | collective-permute-start | bytes 786440 | tf_op jit(solution)/shard_map/ppermute | solution.py:152
  26.9 48.3 %collective-permute-start = (bf16[8,128,128]{2,1,0:T(8,128)(2,1)S(1)}, bf16[8,128,128]{2,1,0:T(8,128)(2,1)}, u32[]{:S(2)}, u32[]{:S(2)}) collective-permute-start(bf16[8,128,128]{2,1,0:T(8,128)(2,1)S(1)} %get-tuple-element.21), channel_id=1, source_target_pairs={{0,1},{1,0},{2,3},{3,2},{4,5},{5,4},{6,7},{7,6},{8,9},{9,8},{10,11... | collective-permute-start | bytes 786440 | tf_op jit(solution)/shard_map/ppermute | solution.py:152
  41.4 19.8 %copy-start.11 = (bf16[10,128,128]{2,1,0:T(8,128)(2,1)S(1)}, bf16[10,128,128]{2,1,0:T(8,128)(2,1)}, u32[]{:S(2)}) copy-start(bf16[10,128,128]{2,1,0:T(8,128)(2,1)} %copy-done.10) | copy-start | bytes 983044
  42.6 2.4 %collective-permute-start.20 = (bf16[8,128,128]{2,1,0:T(8,128)(2,1)S(1)}, bf16[8,128,128]{2,1,0:T(8,128)(2,1)S(1)}, u32[]{:S(2)}, u32[]{:S(2)}) collective-permute-start(bf16[8,128,128]{2,1,0:T(8,128)(2,1)S(1)} %fusion.46), channel_id=1, source_target_pairs={{0,4},{4,0},{8,12},{12,8},{16,20},{20,16},{24,28},{28,24},{1,5},{5... | collective-permute-start | bytes 786440 | tf_op jit(solution)/shard_map/ppermute | solution.py:152
  43.7 15.2 %collective-permute-start.5 = (bf16[8,128,128]{2,1,0:T(8,128)(2,1)S(1)}, bf16[8,128,128]{2,1,0:T(8,128)(2,1)S(1)}, u32[]{:S(2)}, u32[]{:S(2)}) collective-permute-start(bf16[8,128,128]{2,1,0:T(8,128)(2,1)S(1)} %fusion.33), channel_id=1, source_target_pairs={{0,2},{1,3},{2,0},{3,1},{4,6},{5,7},{6,4},{7,5},{8,10},{9,11},{10,... | collective-permute-start | bytes 786440 | tf_op jit(solution)/shard_map/ppermute | solution.py:152
  46.2 15.0 %collective-permute-start.21 = (bf16[8,128,128]{2,1,0:T(8,128)(2,1)S(1)}, bf16[8,128,128]{2,1,0:T(8,128)(2,1)S(1)}, u32[]{:S(2)}, u32[]{:S(2)}) collective-permute-start(bf16[8,128,128]{2,1,0:T(8,128)(2,1)S(1)} %fusion.39), channel_id=1, source_target_pairs={{0,8},{4,12},{8,0},{12,4},{16,24},{20,28},{24,16},{28,20},{1,9},{5... | collective-permute-start | bytes 786440 | tf_op jit(solution)/shard_map/ppermute | solution.py:152
  60.0 4.0 %collective-permute-start.16 = (bf16[8,128,128]{2,1,0:T(8,128)(2,1)S(1)}, bf16[8,128,128]{2,1,0:T(8,128)(2,1)S(1)}, u32[]{:S(2)}, u32[]{:S(2)}) collective-permute-start(bf16[8,128,128]{2,1,0:T(8,128)(2,1)S(1)} %fusion.42), channel_id=1, source_target_pairs={{0,4},{4,0},{8,12},{12,8},{16,20},{20,16},{24,28},{28,24},{1,5},{5... | collective-permute-start | bytes 786440 | tf_op jit(solution)/shard_map/ppermute | solution.py:152
  61.1 12.9 %collective-permute-start.6 = (bf16[8,128,128]{2,1,0:T(8,128)(2,1)S(1)}, bf16[8,128,128]{2,1,0:T(8,128)(2,1)S(1)}, u32[]{:S(2)}, u32[]{:S(2)}) collective-permute-start(bf16[8,128,128]{2,1,0:T(8,128)(2,1)S(1)} %fusion.34), channel_id=1, source_target_pairs={{0,2},{1,3},{2,0},{3,1},{4,6},{5,7},{6,4},{7,5},{8,10},{9,11},{10,... | collective-permute-start | bytes 786440 | tf_op jit(solution)/shard_map/ppermute | solution.py:152
  62.4 14.0 %collective-permute-start.22 = (bf16[8,128,128]{2,1,0:T(8,128)(2,1)S(1)}, bf16[8,128,128]{2,1,0:T(8,128)(2,1)S(1)}, u32[]{:S(2)}, u32[]{:S(2)}) collective-permute-start(bf16[8,128,128]{2,1,0:T(8,128)(2,1)S(1)} %fusion.31), channel_id=1, source_target_pairs={{0,16},{4,20},{8,24},{12,28},{16,0},{20,4},{24,8},{28,12},{1,17},{... | collective-permute-start | bytes 786440 | tf_op jit(solution)/shard_map/ppermute | solution.py:152
  65.0 15.8 %collective-permute-start.17 = (bf16[8,128,128]{2,1,0:T(8,128)(2,1)S(1)}, bf16[8,128,128]{2,1,0:T(8,128)(2,1)S(1)}, u32[]{:S(2)}, u32[]{:S(2)}) collective-permute-start(bf16[8,128,128]{2,1,0:T(8,128)(2,1)S(1)} %fusion.38), channel_id=1, source_target_pairs={{0,8},{4,12},{8,0},{12,4},{16,24},{20,28},{24,16},{28,20},{1,9},{5... | collective-permute-start | bytes 786440 | tf_op jit(solution)/shard_map/ppermute | solution.py:152
  75.1 8.5 %collective-permute-start.12 = (bf16[8,128,128]{2,1,0:T(8,128)(2,1)S(1)}, bf16[8,128,128]{2,1,0:T(8,128)(2,1)S(1)}, u32[]{:S(2)}, u32[]{:S(2)}) collective-permute-start(bf16[8,128,128]{2,1,0:T(8,128)(2,1)S(1)} %fusion.41), channel_id=1, source_target_pairs={{0,4},{4,0},{8,12},{12,8},{16,20},{20,16},{24,28},{28,24},{1,5},{5... | collective-permute-start | bytes 786440 | tf_op jit(solution)/shard_map/ppermute | solution.py:152
  76.3 15.3 %collective-permute-start.7 = (bf16[8,128,128]{2,1,0:T(8,128)(2,1)S(1)}, bf16[8,128,128]{2,1,0:T(8,128)(2,1)S(1)}, u32[]{:S(2)}, u32[]{:S(2)}) collective-permute-start(bf16[8,128,128]{2,1,0:T(8,128)(2,1)S(1)} %fusion.35), channel_id=1, source_target_pairs={{0,2},{1,3},{2,0},{3,1},{4,6},{5,7},{6,4},{7,5},{8,10},{9,11},{10,... | collective-permute-start | bytes 786440 | tf_op jit(solution)/shard_map/ppermute | solution.py:152
  77.7 38.2 %collective-permute-start.23 = (bf16[8,128,128]{2,1,0:T(8,128)(2,1)S(1)}, bf16[8,128,128]{2,1,0:T(8,128)(2,1)S(1)}, u32[]{:S(2)}, u32[]{:S(2)}) collective-permute-start(bf16[8,128,128]{2,1,0:T(8,128)(2,1)S(1)} %get-tuple-element.35), channel_id=1, source_target_pairs={{0,1},{1,0},{2,3},{3,2},{4,5},{5,4},{6,7},{7,6},{8,9},{9,8},{10,11... | collective-permute-start | bytes 786440 | tf_op jit(solution)/shard_map/ppermute | solution.py:152
  82.0 10.8 %collective-permute-start.18 = (bf16[8,128,128]{2,1,0:T(8,128)(2,1)S(1)}, bf16[8,128,128]{2,1,0:T(8,128)(2,1)S(1)}, u32[]{:S(2)}, u32[]{:S(2)}) collective-permute-start(bf16[8,128,128]{2,1,0:T(8,128)(2,1)S(1)} %fusion.27), channel_id=1, source_target_pairs={{0,16},{4,20},{8,24},{12,28},{16,0},{20,4},{24,8},{28,12},{1,17},{... | collective-permute-start | bytes 786440 | tf_op jit(solution)/shard_map/ppermute | solution.py:152
  84.7 9.4 %collective-permute-start.13 = (bf16[8,128,128]{2,1,0:T(8,128)(2,1)S(1)}, bf16[8,128,128]{2,1,0:T(8,128)(2,1)S(1)}, u32[]{:S(2)}, u32[]{:S(2)}) collective-permute-start(bf16[8,128,128]{2,1,0:T(8,128)(2,1)S(1)} %fusion.37), channel_id=1, source_target_pairs={{0,8},{4,12},{8,0},{12,4},{16,24},{20,28},{24,16},{28,20},{1,9},{5... | collective-permute-start | bytes 786440 | tf_op jit(solution)/shard_map/ppermute | solution.py:152
  92.7 1.6 %collective-permute-start.8 = (bf16[8,128,128]{2,1,0:T(8,128)(2,1)S(1)}, bf16[8,128,128]{2,1,0:T(8,128)(2,1)S(1)}, u32[]{:S(2)}, u32[]{:S(2)}) collective-permute-start(bf16[8,128,128]{2,1,0:T(8,128)(2,1)S(1)} %fusion.40), channel_id=1, source_target_pairs={{0,4},{4,0},{8,12},{12,8},{16,20},{20,16},{24,28},{28,24},{1,5},{5... | collective-permute-start | bytes 786440 | tf_op jit(solution)/shard_map/ppermute | solution.py:152
  94.1 21.8 %copy-start.1 = (bf16[256,8192]{1,0:T(8,128)(2,1)S(1)}, bf16[256,8192]{1,0:T(8,128)(2,1)}, u32[]{:S(2)}) copy-start(bf16[256,8192]{1,0:T(8,128)(2,1)} %query_ref.15) | copy-start | bytes 12582916
  94.1 21.8 %copy-start.9 = (f32[256,2048]{1,0:T(8,128)S(1)}, f32[256,2048]{1,0:T(8,128)}, u32[]{:S(2)}) copy-start(f32[256,2048]{1,0:T(8,128)} %copy-done.8) | copy-start | bytes 6291460
  94.1 24.0 %collective-permute-start.19 = (bf16[8,128,128]{2,1,0:T(8,128)(2,1)S(1)}, bf16[8,128,128]{2,1,0:T(8,128)(2,1)S(1)}, u32[]{:S(2)}, u32[]{:S(2)}) collective-permute-start(bf16[8,128,128]{2,1,0:T(8,128)(2,1)S(1)} %get-tuple-element.37), channel_id=1, source_target_pairs={{0,1},{1,0},{2,3},{3,2},{4,5},{5,4},{6,7},{7,6},{8,9},{9,8},{10,11... | collective-permute-start | bytes 786440 | tf_op jit(solution)/shard_map/ppermute | solution.py:152
  95.5 8.7 %collective-permute-start.9 = (bf16[8,128,128]{2,1,0:T(8,128)(2,1)S(1)}, bf16[8,128,128]{2,1,0:T(8,128)(2,1)S(1)}, u32[]{:S(2)}, u32[]{:S(2)}) collective-permute-start(bf16[8,128,128]{2,1,0:T(8,128)(2,1)S(1)} %fusion.36), channel_id=1, source_target_pairs={{0,8},{4,12},{8,0},{12,4},{16,24},{20,28},{24,16},{28,20},{1,9},{5... | collective-permute-start | bytes 786440 | tf_op jit(solution)/shard_map/ppermute | solution.py:152
  98.3 8.7 %collective-permute-start.14 = (bf16[8,128,128]{2,1,0:T(8,128)(2,1)S(1)}, bf16[8,128,128]{2,1,0:T(8,128)(2,1)S(1)}, u32[]{:S(2)}, u32[]{:S(2)}) collective-permute-start(bf16[8,128,128]{2,1,0:T(8,128)(2,1)S(1)} %fusion.23), channel_id=1, source_target_pairs={{0,16},{4,20},{8,24},{12,28},{16,0},{20,4},{24,8},{28,12},{1,17},{... | collective-permute-start | bytes 786440 | tf_op jit(solution)/shard_map/ppermute | solution.py:152
  105.3 7.8 %collective-permute-start.10 = (bf16[8,128,128]{2,1,0:T(8,128)(2,1)S(1)}, bf16[8,128,128]{2,1,0:T(8,128)(2,1)S(1)}, u32[]{:S(2)}, u32[]{:S(2)}) collective-permute-start(bf16[8,128,128]{2,1,0:T(8,128)(2,1)S(1)} %fusion.19), channel_id=1, source_target_pairs={{0,16},{4,20},{8,24},{12,28},{16,0},{20,4},{24,8},{28,12},{1,17},{... | collective-permute-start | bytes 786440 | tf_op jit(solution)/shard_map/ppermute | solution.py:152
  108.2 11.9 %collective-permute-start.15 = (bf16[8,128,128]{2,1,0:T(8,128)(2,1)S(1)}, bf16[8,128,128]{2,1,0:T(8,128)(2,1)S(1)}, u32[]{:S(2)}, u32[]{:S(2)}) collective-permute-start(bf16[8,128,128]{2,1,0:T(8,128)(2,1)S(1)} %get-tuple-element.39), channel_id=1, source_target_pairs={{0,1},{1,0},{2,3},{3,2},{4,5},{5,4},{6,7},{7,6},{8,9},{9,8},{10,11... | collective-permute-start | bytes 786440 | tf_op jit(solution)/shard_map/ppermute | solution.py:152
  114.4 7.8 %collective-permute-start.11 = (bf16[8,128,128]{2,1,0:T(8,128)(2,1)S(1)}, bf16[8,128,128]{2,1,0:T(8,128)(2,1)S(1)}, u32[]{:S(2)}, u32[]{:S(2)}) collective-permute-start(bf16[8,128,128]{2,1,0:T(8,128)(2,1)S(1)} %get-tuple-element.41), channel_id=1, source_target_pairs={{0,1},{1,0},{2,3},{3,2},{4,5},{5,4},{6,7},{7,6},{8,9},{9,8},{10,11... | collective-permute-start | bytes 786440 | tf_op jit(solution)/shard_map/ppermute | solution.py:152
  115.9 2.1 %copy-start.7 = (f32[256,2048]{1,0:T(8,128)S(1)}, f32[256,2048]{1,0:T(8,128)}, u32[]{:S(2)}) copy-start(f32[256,2048]{1,0:T(8,128)} %copy-done.6) | copy-start | bytes 6291460
  118.1 2.1 %copy-start.5 = (f32[256,2048]{1,0:T(8,128)S(1)}, f32[256,2048]{1,0:T(8,128)}, u32[]{:S(2)}) copy-start(f32[256,2048]{1,0:T(8,128)} %copy-done.4) | copy-start | bytes 6291460
  (4 other events, 4.9 us)

commit v3 on v2

--- a/solution.py
+++ b/solution.py
@@ -10,9 +10,11 @@
 HD = 128
 SIZES = ((16, 1),) * 4
 LOCAL_STEP = 8
+LOCAL_AFTER = (-1, 1)
+KEEP = False
 LOCAL_SWAP = 4
 LOCAL_TIE = True
-STEPS = "0 1 2 3 0 1,01 2,11 3,21 0 1 2 3 0 1 2 3 0 1 2 3 0 1 2 3 0 1 2 3"
+STEPS = ((0,), (1, (0, 0)), (2, (1, 0)), (3, (2, 0)), (0,), (1,), (2,), (3,), (0,), (1,), (2,), (3,), (0,), (1,), (2,), (3,), (0,), (1,), (2,), (3,), (0,), (1,), (2,), (3,), (0,), (1,), (2,), (3,))
 VMEM = 24 << 20
 
 
@@ -70,7 +72,8 @@
     )(side, key_vectors, value_vectors)
 
 
-def local_kernel(query_ref, key_ref, value_ref, local_ref):
+def local_kernel(query_ref, key_ref, value_ref, *refs):
+    local_ref = refs[-1]
     tokens = query_ref.shape[0]
     rows = lax.broadcasted_iota(jnp.int32, (tokens, tokens), 0)
     causal = rows >= lax.broadcasted_iota(jnp.int32, (tokens, tokens), 1)
@@ -86,13 +89,13 @@
         local_ref[:, columns] = jnp.dot(scores, value_ref[:, columns], preferred_element_type=jnp.float32)
 
 
-def locals_of(queries, key_vectors, value_vectors, first, count):
+def locals_of(queries, key_vectors, value_vectors, first, count, wait_for):
     tokens, step = queries.shape[0], min(count, LOCAL_STEP)
     tokens_spec = pl.BlockSpec((tokens, step * HD), lambda i: (0, first // step + i))
     return pl.pallas_call(
         local_kernel,
         grid=(count // step,),
-        in_specs=[tokens_spec] * 3,
+        in_specs=[tokens_spec] * 3 + [pl.BlockSpec(memory_space=pl.ANY)] * len(wait_for),
         out_specs=pl.BlockSpec((tokens, step * HD), lambda i: (0, i)),
         out_shape=jax.ShapeDtypeStruct((tokens, count * HD), jnp.float32),
         compiler_params=pltpu.CompilerParams(vmem_limit_bytes=VMEM),
@@ -101,7 +104,7 @@
             bytes_accessed=count * HD * 10 * tokens,
             transcendentals=0,
         ),
-    )(queries, key_vectors, value_vectors)
+    )(queries, key_vectors, value_vectors, *wait_for)
 
 
 def output_kernel(side_ref, query_ref, local_ref, mine_ref, theirs_ref, gain_ref, *refs):
@@ -148,6 +151,10 @@
     return lax.optimization_barrier((block, *done))[0] if done else block
 
 
+def kept_whole(total):
+    return lax.optimization_barrier(total) if KEEP else total
+
+
 def swapped(block, axis, step):
     return lax.ppermute(block, axis, [(i, i ^ step) for i in range(lax.axis_size(axis))])
 
@@ -157,30 +164,33 @@
     done = yield
     sent = theirs if extra is None else jnp.concatenate([theirs, extra])
     arrived = swapped(after(sent, done), "head", 1)
-    arrived = after(arrived, (yield arrived))
+    done = yield arrived
     neighbour = arrived[:half]
-    whole = added(mine, neighbour)
+    whole = kept_whole(added(mine, neighbour))
     if extra is not None:
         extra = added(extra, arrived[half:])
-    earlier = jnp.zeros_like(whole)
+    pieces = []
     for axis, step in [("head", 2), ("seq", 1)]:
         index = lax.axis_index(axis)
         while step < lax.axis_size(axis):
             sent = packed(whole)
-            with_extra = extra is not None and axis == "head"
-            if with_extra:
+            if extra is not None and axis == "head":
                 sent = jnp.concatenate([sent, packed(extra)])
-            arrived = swapped(sent, axis, step)
+            arrived = swapped(after(sent, done), axis, step)
+            done = ()
             if (axis, step) in (("head", 2), ("seq", 1), ("seq", 2), ("seq", 4)):
-                arrived = after(arrived, (yield arrived))
-            earlier += kept(index & step != 0, arrived[:half])
-            whole += f32(arrived[:half])
-            if with_extra:
+                done = yield arrived
+                if (axis, step) != ("head", 2):
+                    arrived, done = after(arrived, done), ()
+            pieces.append(kept(index & step != 0, arrived[:half]))
+            whole = kept_whole(whole + f32(arrived[:half]))
+            if extra is not None and axis == "head":
                 extra = extra + f32(arrived[half:])
             step *= 2
+    earlier = functools.reduce(jnp.add, pieces)
     carried_mine = packed(earlier + kept(side == 1, neighbour))
     carried_theirs = packed(earlier + kept(side == 0, mine))
-    arrived = swapped(carried_theirs, "head", 1)
+    arrived = swapped(after(carried_theirs, done), "head", 1)
     arrived = after(arrived, (yield arrived))
     yield carried_mine, arrived, extra
 
@@ -217,13 +227,13 @@
 
     count = len(scans)
     done, out, gain = [[] for _ in scans], None, None
-    for step in STEPS.split():
-        piece, *wait_for = step.split(",")
-        piece = int(piece)
-        wait_for = [done[int(item[0])][int(item[1])] for item in wait_for]
+    for piece, *wait_for in STEPS:
+        wait_for = [done[other][swap] for other, swap in wait_for]
         swap = len(done[piece])
         if swap == LOCAL_SWAP:
-            local = locals_of(queries, key_vectors, value_vectors, firsts[piece], sizes[piece])
+            other, brought = piece + LOCAL_AFTER[0], LOCAL_AFTER[1]
+            before = [done[other][brought]] if 0 <= other and len(done[other]) > brought else []
+            local = locals_of(queries, key_vectors, value_vectors, firsts[piece], sizes[piece], before)
             wait_for += [local] if LOCAL_TIE else []
         result = scans[piece].send(wait_for)
         if swap == LOCAL_SWAP:

time: 125 us -> 106 us (0.85)
  other arithmetic: 23.6 us -> 3.57 us
  starting transfers between devices: 29.5 us -> 26.4 us
  local copies, waits for them, and re-layouts: 9.16 us -> 12 us
  waiting for transfers between devices: 39.4 us -> 41.9 us
    convert_element_type x22, other arithmetic: 21.8 us -> 3.38 us  [packed(): return total.astype(jnp.bfloat16)]
    ppermute x24, starting transfers between devices: 29.5 us -> 26.4 us  [swapped(): lax.ppermute(block, axis, [(i, i ^ step) for i in range(lax.axis_size(axi...]
    unnamed x24 -> x12, local copies, waits for them, and re-layouts: 8.38 us -> 11.2 us
    ppermute x24, waiting for transfers between devices: 39.4 us -> 41.9 us  [swapped(): lax.ppermute(block, axis, [(i, i ^ step) for i in range(lax.axis_size(axi...]
    pallas_call x4, Pallas kernels: 5.12 us -> 3.79 us  [states_of(): pl.pallas_call(state_kernel, grid_spec=pltpu.PrefetchScalarGridSpec(num_s...]
  transfers between devices with their start and end apart: 24 -> 24, of which waited for: 7 -> 9; matrix products, arithmetic and copies ran while one was open for 18% -> 3% of each run, Pallas kernels for 16% -> 17%
where the time goes in v3:
time: 106 us; the launch traced here: 105 us
  waiting for transfers between devices  41.9 us (40%)
  starting transfers between devices  26.4 us (25%)
  Pallas kernels  21.1 us (20%)
  local copies, waits for them, and re-layouts  12 us (11%)
  other arithmetic  3.57 us (3%)
    ppermute x24, waiting for transfers between devices, swapped(): lax.ppermute(block, axis, [(i, i ^ step) for i in range(lax.axis_size(axi...  41.9 us
    ppermute x24, starting transfers between devices, swapped(): lax.ppermute(block, axis, [(i, i ^ step) for i in range(lax.axis_size(axi...  26.4 us
    unnamed x12, local copies, waits for them, and re-layouts  11.2 us
    pallas_call x4, Pallas kernels, locals_of(): pl.pallas_call(local_kernel, grid=(count // step,), in_specs=[tokens_spec...  8.81 us
    pallas_call x4, Pallas kernels, outputs_of(): pl.pallas_call(output_kernel, grid_spec=pltpu.PrefetchScalarGridSpec(num_...  8.53 us
    pallas_call x4, Pallas kernels, states_of(): pl.pallas_call(state_kernel, grid_spec=pltpu.PrefetchScalarGridSpec(num_s...  3.79 us
    convert_element_type x22, other arithmetic, packed(): return total.astype(jnp.bfloat16)  3.38 us
  transfers between devices with their start and end apart: 24, of which 9 were waited for; matrix products, arithmetic and copies ran while one was open for 3% of the time, Pallas kernels for 17%

profile of v3, /device:TPU:0, one launch (start us, length us, event | category | flops | bytes accessed | tf_op | source)
XLA Modules:
  0.0 105.3 jit_solution(7457089105823914099)
XLA Ops:
  0.8 2.2 %copy-done.1 = bf16[256,8192]{1,0:T(8,128)(2,1)S(1)} copy-done((bf16[256,8192]{1,0:T(8,128)(2,1)S(1)}, bf16[256,8192]{1,0:T(8,128)(2,1)}, u32[]{:S(2)}) %copy-start.1) | copy-done | bytes 4194328
  3.0 2.2 %copy-done.4 = bf16[256,8192]{1,0:T(8,128)(2,1)S(1)} copy-done((bf16[256,8192]{1,0:T(8,128)(2,1)S(1)}, bf16[256,8192]{1,0:T(8,128)(2,1)}, u32[]{:S(2)}) %copy-start.4) | copy-done | bytes 4194328
  6.3 3.1 %collective-permute-start = (bf16[10,128,128]{2,1,0:T(8,128)(2,1)S(1)}, bf16[10,128,128]{2,1,0:T(8,128)(2,1)S(1)}, u32[]{:S(2)}, u32[]{:S(2)}) collective-permute-start(bf16[10,128,128]{2,1,0:T(8,128)(2,1)S(1)} %pad_maximum_fusion), channel_id=1, source_target_pairs={{0,1},{1,0},{2,3},{3,2},{4,5},{5,4},{6,7},{7,6},{8,9},{9,8},{10,11... | collective-permute-start | bytes 983048 | tf_op jit(solution)/shard_map/ppermute | solution.py:159
  10.3 6.7 %collective-permute-done = bf16[10,128,128]{2,1,0:T(8,128)(2,1)S(1)} collective-permute-done((bf16[10,128,128]{2,1,0:T(8,128)(2,1)S(1)}, bf16[10,128,128]{2,1,0:T(8,128)(2,1)S(1)}, u32[]{:S(2)}, u32[]{:S(2)}) %collective-permute-start) | collective-permute-done | bytes 327712 | tf_op jit(solution)/shard_map/ppermute | solution.py:159
  17.1 1.7 %collective-permute-start.1 = (bf16[8,128,128]{2,1,0:T(8,128)(2,1)S(1)}, bf16[8,128,128]{2,1,0:T(8,128)(2,1)S(1)}, u32[]{:S(2)}, u32[]{:S(2)}) collective-permute-start(bf16[8,128,128]{2,1,0:T(8,128)(2,1)S(1)} %get-tuple-element.24), channel_id=1, source_target_pairs={{0,1},{1,0},{2,3},{3,2},{4,5},{5,4},{6,7},{7,6},{8,9},{9,8},{10,11... | collective-permute-start | bytes 786440 | tf_op jit(solution)/shard_map/ppermute | solution.py:159
  19.0 2.7 %collective-permute-start.10 = (bf16[10,128,128]{2,1,0:T(8,128)(2,1)S(1)}, bf16[10,128,128]{2,1,0:T(8,128)(2,1)S(1)}, u32[]{:S(2)}, u32[]{:S(2)}) collective-permute-start(bf16[10,128,128]{2,1,0:T(8,128)(2,1)S(1)} %pad_maximum_fusion.1), channel_id=1, source_target_pairs={{0,2},{1,3},{2,0},{3,1},{4,6},{5,7},{6,4},{7,5},{8,10},{9,11},{10,... | collective-permute-start | bytes 983048 | tf_op jit(solution)/shard_map/ppermute | solution.py:159
  21.6 2.2 %copy-done.2 = bf16[256,8192]{1,0:T(8,128)(2,1)S(1)} copy-done((bf16[256,8192]{1,0:T(8,128)(2,1)S(1)}, bf16[256,8192]{1,0:T(8,128)(2,1)}, u32[]{:S(2)}) %copy-start.2) | copy-done | bytes 4194328
  23.8 2.2 %copy-done.5 = bf16[256,8192]{1,0:T(8,128)(2,1)S(1)} copy-done((bf16[256,8192]{1,0:T(8,128)(2,1)S(1)}, bf16[256,8192]{1,0:T(8,128)(2,1)}, u32[]{:S(2)}) %copy-start.5) | copy-done | bytes 4194328
  29.1 1.3 %copy-done.3 = bf16[256,8192]{1,0:T(8,128)(2,1)S(1)} copy-done((bf16[256,8192]{1,0:T(8,128)(2,1)S(1)}, bf16[256,8192]{1,0:T(8,128)(2,1)}, u32[]{:S(2)}) %copy-start.3) | copy-done | bytes 4194328
  30.4 2.2 %shard_map.53.local_ref = f32[256,2048]{1,0:T(8,128)S(1)} custom-call(bf16[256,8192]{1,0:T(8,128)(2,1)S(1)} %copy-done, bf16[256,8192]{1,0:T(8,128)(2,1)S(1)} %copy-done.3, bf16[256,8192]{1,0:T(8,128)(2,1)S(1)} %copy-done.5), custom_call_target="tpu_custom_call" | custom-call | flops 536870912 | bytes 5242880 | tf_op jit(solution)/shard_map/pallas_call | solution.py:95
  33.4 6.7 %collective-permute-done.10.refs_0_ = bf16[10,128,128]{2,1,0:T(8,128)(2,1)S(1)} collective-permute-done((bf16[10,128,128]{2,1,0:T(8,128)(2,1)S(1)}, bf16[10,128,128]{2,1,0:T(8,128)(2,1)S(1)}, u32[]{:S(2)}, u32[]{:S(2)}) %collective-permute-start.10) | collective-permute-done | bytes 327712 | tf_op jit(solution)/shard_map/ppermute | solution.py:159
  40.4 2.2 %shard_map.52.local_ref = f32[256,2048]{1,0:T(8,128)S(1)} custom-call(bf16[256,8192]{1,0:T(8,128)(2,1)S(1)} %copy-done, bf16[256,8192]{1,0:T(8,128)(2,1)S(1)} %copy-done.3, bf16[256,8192]{1,0:T(8,128)(2,1)S(1)} %copy-done.5, bf16[10,128,128]{2,1,0:T(8,128)(2,1)S(1)} %collective-permute-done.10.refs_0_), custom_call_target="tpu_custom_call" | custom-call | flops 536870912 | bytes 5242880 | tf_op jit(solution)/shard_map/pallas_call | solution.py:95
  42.6 4.0 %collective-permute-done.11.refs_0_ = bf16[8,128,128]{2,1,0:T(8,128)(2,1)S(1)} collective-permute-done((bf16[8,128,128]{2,1,0:T(8,128)(2,1)S(1)}, bf16[8,128,128]{2,1,0:T(8,128)(2,1)S(1)}, u32[]{:S(2)}, u32[]{:S(2)}) %collective-permute-start.11) | collective-permute-done | bytes 262176 | tf_op jit(solution)/shard_map/ppermute | solution.py:159
  47.6 2.5 %collective-permute-start.4 = (bf16[8,128,128]{2,1,0:T(8,128)(2,1)S(1)}, bf16[8,128,128]{2,1,0:T(8,128)(2,1)S(1)}, u32[]{:S(2)}, u32[]{:S(2)}) collective-permute-start(bf16[8,128,128]{2,1,0:T(8,128)(2,1)S(1)} %get-tuple-element.28), channel_id=1, source_target_pairs={{0,1},{1,0},{2,3},{3,2},{4,5},{5,4},{6,7},{7,6},{8,9},{9,8},{10,11... | collective-permute-start | bytes 786440 | tf_op jit(solution)/shard_map/ppermute | solution.py:159
  50.0 2.2 %shard_map.51.local_ref = f32[256,2048]{1,0:T(8,128)S(1)} custom-call(bf16[256,8192]{1,0:T(8,128)(2,1)S(1)} %copy-done, bf16[256,8192]{1,0:T(8,128)(2,1)S(1)} %copy-done.3, bf16[256,8192]{1,0:T(8,128)(2,1)S(1)} %copy-done.5, bf16[8,128,128]{2,1,0:T(8,128)(2,1)S(1)} %collective-permute-done.11.refs_0_), custom_call_target="tpu_custom_call" | custom-call | flops 536870912 | bytes 5242880 | tf_op jit(solution)/shard_map/pallas_call | solution.py:95
  52.4 1.6 %collective-permute-start.21 = (bf16[8,128,128]{2,1,0:T(8,128)(2,1)S(1)}, bf16[8,128,128]{2,1,0:T(8,128)(2,1)S(1)}, u32[]{:S(2)}, u32[]{:S(2)}) collective-permute-start(bf16[8,128,128]{2,1,0:T(8,128)(2,1)S(1)} %fusion.39), channel_id=1, source_target_pairs={{0,8},{4,12},{8,0},{12,4},{16,24},{20,28},{24,16},{28,20},{1,9},{5... | collective-permute-start | bytes 786440 | tf_op jit(solution)/shard_map/ppermute | solution.py:159
  54.7 7.4 %collective-permute-done.3.refs_0_ = bf16[8,128,128]{2,1,0:T(8,128)(2,1)S(1)} collective-permute-done((bf16[8,128,128]{2,1,0:T(8,128)(2,1)S(1)}, bf16[8,128,128]{2,1,0:T(8,128)(2,1)S(1)}, u32[]{:S(2)}, u32[]{:S(2)}) %collective-permute-start.3) | collective-permute-done | bytes 262176 | tf_op jit(solution)/shard_map/ppermute | solution.py:159
  62.8 2.2 %shard_map.49.local_ref = f32[256,2048]{1,0:T(8,128)S(1)} custom-call(bf16[256,8192]{1,0:T(8,128)(2,1)S(1)} %copy-done, bf16[256,8192]{1,0:T(8,128)(2,1)S(1)} %copy-done.3, bf16[256,8192]{1,0:T(8,128)(2,1)S(1)} %copy-done.5, bf16[8,128,128]{2,1,0:T(8,128)(2,1)S(1)} %collective-permute-done.3.refs_0_), custom_call_target="tpu_custom_call" | custom-call | flops 536870912 | bytes 5242880 | tf_op jit(solution)/shard_map/pallas_call | solution.py:95
  65.2 1.6 %collective-permute-start.22 = (bf16[8,128,128]{2,1,0:T(8,128)(2,1)S(1)}, bf16[8,128,128]{2,1,0:T(8,128)(2,1)S(1)}, u32[]{:S(2)}, u32[]{:S(2)}) collective-permute-start(bf16[8,128,128]{2,1,0:T(8,128)(2,1)S(1)} %fusion.31), channel_id=1, source_target_pairs={{0,16},{4,20},{8,24},{12,28},{16,0},{20,4},{24,8},{28,12},{1,17},{... | collective-permute-start | bytes 786440 | tf_op jit(solution)/shard_map/ppermute | solution.py:159
  68.1 1.6 %collective-permute-start.13 = (bf16[8,128,128]{2,1,0:T(8,128)(2,1)S(1)}, bf16[8,128,128]{2,1,0:T(8,128)(2,1)S(1)}, u32[]{:S(2)}, u32[]{:S(2)}) collective-permute-start(bf16[8,128,128]{2,1,0:T(8,128)(2,1)S(1)} %fusion.37), channel_id=1, source_target_pairs={{0,8},{4,12},{8,0},{12,4},{16,24},{20,28},{24,16},{28,20},{1,9},{5... | collective-permute-start | bytes 786440 | tf_op jit(solution)/shard_map/ppermute | solution.py:159
  69.7 6.6 %collective-permute-done.5 = bf16[8,128,128]{2,1,0:T(8,128)(2,1)S(1)} collective-permute-done((bf16[8,128,128]{2,1,0:T(8,128)(2,1)S(1)}, bf16[8,128,128]{2,1,0:T(8,128)(2,1)S(1)}, u32[]{:S(2)}, u32[]{:S(2)}) %collective-permute-start.5) | collective-permute-done | bytes 262176 | tf_op jit(solution)/shard_map/ppermute | solution.py:159
  77.0 2.3 %collective-permute-done.18 = bf16[8,128,128]{2,1,0:T(8,128)(2,1)S(1)} collective-permute-done((bf16[8,128,128]{2,1,0:T(8,128)(2,1)S(1)}, bf16[8,128,128]{2,1,0:T(8,128)(2,1)S(1)}, u32[]{:S(2)}, u32[]{:S(2)}) %collective-permute-start.18) | collective-permute-done | bytes 262176 | tf_op jit(solution)/shard_map/ppermute | solution.py:159
  79.6 1.6 %collective-permute-start.19 = (bf16[8,128,128]{2,1,0:T(8,128)(2,1)S(1)}, bf16[8,128,128]{2,1,0:T(8,128)(2,1)S(1)}, u32[]{:S(2)}, u32[]{:S(2)}) collective-permute-start(bf16[8,128,128]{2,1,0:T(8,128)(2,1)S(1)} %get-tuple-element.37), channel_id=1, source_target_pairs={{0,1},{1,0},{2,3},{3,2},{4,5},{5,4},{6,7},{7,6},{8,9},{9,8},{10,11... | collective-permute-start | bytes 786440 | tf_op jit(solution)/shard_map/ppermute | solution.py:159
  81.4 1.6 %collective-permute-start.7 = (bf16[8,128,128]{2,1,0:T(8,128)(2,1)S(1)}, bf16[8,128,128]{2,1,0:T(8,128)(2,1)S(1)}, u32[]{:S(2)}, u32[]{:S(2)}) collective-permute-start(bf16[8,128,128]{2,1,0:T(8,128)(2,1)S(1)} %fusion.36), channel_id=1, source_target_pairs={{0,8},{4,12},{8,0},{12,4},{16,24},{20,28},{24,16},{28,20},{1,9},{5... | collective-permute-start | bytes 786440 | tf_op jit(solution)/shard_map/ppermute | solution.py:159
  83.1 1.6 %collective-permute-start.14 = (bf16[8,128,128]{2,1,0:T(8,128)(2,1)S(1)}, bf16[8,128,128]{2,1,0:T(8,128)(2,1)S(1)}, u32[]{:S(2)}, u32[]{:S(2)}) collective-permute-start(bf16[8,128,128]{2,1,0:T(8,128)(2,1)S(1)} %fusion.23), channel_id=1, source_target_pairs={{0,16},{4,20},{8,24},{12,28},{16,0},{20,4},{24,8},{28,12},{1,17},{... | collective-permute-start | bytes 786440 | tf_op jit(solution)/shard_map/ppermute | solution.py:159
  84.7 3.7 %collective-permute-done.7 = bf16[8,128,128]{2,1,0:T(8,128)(2,1)S(1)} collective-permute-done((bf16[8,128,128]{2,1,0:T(8,128)(2,1)S(1)}, bf16[8,128,128]{2,1,0:T(8,128)(2,1)S(1)}, u32[]{:S(2)}, u32[]{:S(2)}) %collective-permute-start.7) | collective-permute-done | bytes 262176 | tf_op jit(solution)/shard_map/ppermute | solution.py:159
  88.6 1.6 %collective-permute-start.8 = (bf16[8,128,128]{2,1,0:T(8,128)(2,1)S(1)}, bf16[8,128,128]{2,1,0:T(8,128)(2,1)S(1)}, u32[]{:S(2)}, u32[]{:S(2)}) collective-permute-start(bf16[8,128,128]{2,1,0:T(8,128)(2,1)S(1)} %fusion.11), channel_id=1, source_target_pairs={{0,16},{4,20},{8,24},{12,28},{16,0},{20,4},{24,8},{28,12},{1,17},{... | collective-permute-start | bytes 786440 | tf_op jit(solution)/shard_map/ppermute | solution.py:159
  91.5 4.0 %collective-permute-done.8 = bf16[8,128,128]{2,1,0:T(8,128)(2,1)S(1)} collective-permute-done((bf16[8,128,128]{2,1,0:T(8,128)(2,1)S(1)}, bf16[8,128,128]{2,1,0:T(8,128)(2,1)S(1)}, u32[]{:S(2)}, u32[]{:S(2)}) %collective-permute-start.8) | collective-permute-done | bytes 262176 | tf_op jit(solution)/shard_map/ppermute | solution.py:159
  96.8 2.1 %shard_map.54.refs_0_ = bf16[256,8192]{1,0:T(8,128)(2,1)} custom-call(s32[1]{0:T(128)} %bitcast.side_ref, bf16[256,8192]{1,0:T(8,128)(2,1)S(1)} %copy-done, f32[256,2048]{1,0:T(8,128)S(1)} %shard_map.53.local_ref, bf16[8,128,128]{2,1,0:T(8,128)(2,1)S(1)} %get-tuple-element.36.mine_ref, bf16[8,128,128]{2,1,0:T(8,128)(2,1)S(1)} %collective-permute-done.23.theirs_ref, ...), custom_call_target="tpu_custom_call" | custom-call | flops 134217728 | bytes 4456448 | tf_op jit(solution)/shard_map/pallas_call | solution.py:134
  98.9 2.1 %shard_map.55.refs_0_ = bf16[256,8192]{1,0:T(8,128)(2,1)} custom-call(s32[1]{0:T(128)} %bitcast.side_ref, bf16[256,8192]{1,0:T(8,128)(2,1)S(1)} %copy-done, f32[256,2048]{1,0:T(8,128)S(1)} %shard_map.52.local_ref, bf16[8,128,128]{2,1,0:T(8,128)(2,1)S(1)} %get-tuple-element.38.mine_ref, ...), custom_call_target="tpu_custom_call", output_to_operand_aliasing={{}: (6, {})} | custom-call | flops 134217728 | bytes 4456448 | tf_op jit(solution)/shard_map/pallas_call | solution.py:134
  101.1 2.1 %shard_map.56.refs_0_ = bf16[256,8192]{1,0:T(8,128)(2,1)} custom-call(s32[1]{0:T(128)} %bitcast.side_ref, bf16[256,8192]{1,0:T(8,128)(2,1)S(1)} %copy-done, f32[256,2048]{1,0:T(8,128)S(1)} %shard_map.51.local_ref, bf16[8,128,128]{2,1,0:T(8,128)(2,1)S(1)} %get-tuple-element.40.mine_ref, ...), custom_call_target="tpu_custom_call", output_to_operand_aliasing={{}: (6, {})} | custom-call | flops 134217728 | bytes 4456448 | tf_op jit(solution)/shard_map/pallas_call | solution.py:134
  103.2 2.1 %shard_map.57 = bf16[256,8192]{1,0:T(8,128)(2,1)} custom-call(s32[1]{0:T(128)} %bitcast.side_ref, bf16[256,8192]{1,0:T(8,128)(2,1)S(1)} %copy-done, f32[256,2048]{1,0:T(8,128)S(1)} %shard_map.49.local_ref, bf16[8,128,128]{2,1,0:T(8,128)(2,1)S(1)} %get-tuple-element.42.mine_ref, ...), custom_call_target="tpu_custom_call", output_to_operand_aliasing={{}: (6, {})} | custom-call | flops 134217728 | bytes 4456448 | tf_op jit(solution)/shard_map/pallas_call | solution.py:134
  (71 shorter events, 15.1 us)
Async XLA Ops:
  0.8 2.2 %copy-start.1 = (bf16[256,8192]{1,0:T(8,128)(2,1)S(1)}, bf16[256,8192]{1,0:T(8,128)(2,1)}, u32[]{:S(2)}) copy-start(bf16[256,8192]{1,0:T(8,128)(2,1)} %key_ref.15) | copy-start | bytes 12582916
  3.0 2.2 %copy-start.4 = (bf16[256,8192]{1,0:T(8,128)(2,1)S(1)}, bf16[256,8192]{1,0:T(8,128)(2,1)}, u32[]{:S(2)}) copy-start(bf16[256,8192]{1,0:T(8,128)(2,1)} %value_ref.15) | copy-start | bytes 12582916
  6.3 10.8 %collective-permute-start = (bf16[10,128,128]{2,1,0:T(8,128)(2,1)S(1)}, bf16[10,128,128]{2,1,0:T(8,128)(2,1)S(1)}, u32[]{:S(2)}, u32[]{:S(2)}) collective-permute-start(bf16[10,128,128]{2,1,0:T(8,128)(2,1)S(1)} %pad_maximum_fusion), channel_id=1, source_target_pairs={{0,1},{1,0},{2,3},{3,2},{4,5},{5,4},{6,7},{7,6},{8,9},{9,8},{10,11... | collective-permute-start | bytes 983048 | tf_op jit(solution)/shard_map/ppermute | solution.py:159
  17.1 15.5 %collective-permute-start.1 = (bf16[8,128,128]{2,1,0:T(8,128)(2,1)S(1)}, bf16[8,128,128]{2,1,0:T(8,128)(2,1)S(1)}, u32[]{:S(2)}, u32[]{:S(2)}) collective-permute-start(bf16[8,128,128]{2,1,0:T(8,128)(2,1)S(1)} %get-tuple-element.24), channel_id=1, source_target_pairs={{0,1},{1,0},{2,3},{3,2},{4,5},{5,4},{6,7},{7,6},{8,9},{9,8},{10,11... | collective-permute-start | bytes 786440 | tf_op jit(solution)/shard_map/ppermute | solution.py:159
  19.0 21.2 %collective-permute-start.10 = (bf16[10,128,128]{2,1,0:T(8,128)(2,1)S(1)}, bf16[10,128,128]{2,1,0:T(8,128)(2,1)S(1)}, u32[]{:S(2)}, u32[]{:S(2)}) collective-permute-start(bf16[10,128,128]{2,1,0:T(8,128)(2,1)S(1)} %pad_maximum_fusion.1), channel_id=1, source_target_pairs={{0,2},{1,3},{2,0},{3,1},{4,6},{5,7},{6,4},{7,5},{8,10},{9,11},{10,... | collective-permute-start | bytes 983048 | tf_op jit(solution)/shard_map/ppermute | solution.py:159
  21.6 2.2 %copy-start.2 = (bf16[256,8192]{1,0:T(8,128)(2,1)S(1)}, bf16[256,8192]{1,0:T(8,128)(2,1)}, u32[]{:S(2)}) copy-start(bf16[256,8192]{1,0:T(8,128)(2,1)} %key_ref.15) | copy-start | bytes 12582916
  23.8 2.2 %copy-start.5 = (bf16[256,8192]{1,0:T(8,128)(2,1)S(1)}, bf16[256,8192]{1,0:T(8,128)(2,1)}, u32[]{:S(2)}) copy-start(bf16[256,8192]{1,0:T(8,128)(2,1)} %value_ref.15) | copy-start | bytes 12582916
  27.0 2.2 %copy-start = (bf16[256,8192]{1,0:T(8,128)(2,1)S(1)}, bf16[256,8192]{1,0:T(8,128)(2,1)}, u32[]{:S(2)}) copy-start(bf16[256,8192]{1,0:T(8,128)(2,1)} %query_ref.15) | copy-start | bytes 12582916
  27.0 3.5 %copy-start.3 = (bf16[256,8192]{1,0:T(8,128)(2,1)S(1)}, bf16[256,8192]{1,0:T(8,128)(2,1)}, u32[]{:S(2)}) copy-start(bf16[256,8192]{1,0:T(8,128)(2,1)} %key_ref.15) | copy-start | bytes 12582916
  32.7 13.8 %collective-permute-start.11 = (bf16[8,128,128]{2,1,0:T(8,128)(2,1)S(1)}, bf16[8,128,128]{2,1,0:T(8,128)(2,1)S(1)}, u32[]{:S(2)}, u32[]{:S(2)}) collective-permute-start(bf16[8,128,128]{2,1,0:T(8,128)(2,1)S(1)} %fusion.35), channel_id=1, source_target_pairs={{0,2},{1,3},{2,0},{3,1},{4,6},{5,7},{6,4},{7,5},{8,10},{9,11},{10,... | collective-permute-start | bytes 786440 | tf_op jit(solution)/shard_map/ppermute | solution.py:159
  33.1 13.6 %collective-permute-start.2 = (bf16[8,128,128]{2,1,0:T(8,128)(2,1)S(1)}, bf16[8,128,128]{2,1,0:T(8,128)(2,1)S(1)}, u32[]{:S(2)}, u32[]{:S(2)}) collective-permute-start(bf16[8,128,128]{2,1,0:T(8,128)(2,1)S(1)} %get-tuple-element.25), channel_id=1, source_target_pairs={{0,1},{1,0},{2,3},{3,2},{4,5},{5,4},{6,7},{7,6},{8,9},{9,8},{10,11... | collective-permute-start | bytes 786440 | tf_op jit(solution)/shard_map/ppermute | solution.py:159
  40.2 12.0 %collective-permute-start.20 = (bf16[8,128,128]{2,1,0:T(8,128)(2,1)S(1)}, bf16[8,128,128]{2,1,0:T(8,128)(2,1)S(1)}, u32[]{:S(2)}, u32[]{:S(2)}) collective-permute-start(bf16[8,128,128]{2,1,0:T(8,128)(2,1)S(1)} %fusion.46), channel_id=1, source_target_pairs={{0,4},{4,0},{8,12},{12,8},{16,20},{20,16},{24,28},{28,24},{1,5},{5... | collective-permute-start | bytes 786440 | tf_op jit(solution)/shard_map/ppermute | solution.py:159
  46.6 7.4 %collective-permute-start.16 = (bf16[8,128,128]{2,1,0:T(8,128)(2,1)S(1)}, bf16[8,128,128]{2,1,0:T(8,128)(2,1)S(1)}, u32[]{:S(2)}, u32[]{:S(2)}) collective-permute-start(bf16[8,128,128]{2,1,0:T(8,128)(2,1)S(1)} %fusion.42), channel_id=1, source_target_pairs={{0,4},{4,0},{8,12},{12,8},{16,20},{20,16},{24,28},{28,24},{1,5},{5... | collective-permute-start | bytes 786440 | tf_op jit(solution)/shard_map/ppermute | solution.py:159
  46.8 15.3 %collective-permute-start.3 = (bf16[8,128,128]{2,1,0:T(8,128)(2,1)S(1)}, bf16[8,128,128]{2,1,0:T(8,128)(2,1)S(1)}, u32[]{:S(2)}, u32[]{:S(2)}) collective-permute-start(bf16[8,128,128]{2,1,0:T(8,128)(2,1)S(1)} %fusion.32), channel_id=1, source_target_pairs={{0,2},{1,3},{2,0},{3,1},{4,6},{5,7},{6,4},{7,5},{8,10},{9,11},{10,... | collective-permute-start | bytes 786440 | tf_op jit(solution)/shard_map/ppermute | solution.py:159
  47.6 14.8 %collective-permute-start.4 = (bf16[8,128,128]{2,1,0:T(8,128)(2,1)S(1)}, bf16[8,128,128]{2,1,0:T(8,128)(2,1)S(1)}, u32[]{:S(2)}, u32[]{:S(2)}) collective-permute-start(bf16[8,128,128]{2,1,0:T(8,128)(2,1)S(1)} %get-tuple-element.28), channel_id=1, source_target_pairs={{0,1},{1,0},{2,3},{3,2},{4,5},{5,4},{6,7},{7,6},{8,9},{9,8},{10,11... | collective-permute-start | bytes 786440 | tf_op jit(solution)/shard_map/ppermute | solution.py:159
  52.4 12.6 %collective-permute-start.21 = (bf16[8,128,128]{2,1,0:T(8,128)(2,1)S(1)}, bf16[8,128,128]{2,1,0:T(8,128)(2,1)S(1)}, u32[]{:S(2)}, u32[]{:S(2)}) collective-permute-start(bf16[8,128,128]{2,1,0:T(8,128)(2,1)S(1)} %fusion.39), channel_id=1, source_target_pairs={{0,8},{4,12},{8,0},{12,4},{16,24},{20,28},{24,16},{28,20},{1,9},{5... | collective-permute-start | bytes 786440 | tf_op jit(solution)/shard_map/ppermute | solution.py:159
  54.2 12.6 %collective-permute-start.17 = (bf16[8,128,128]{2,1,0:T(8,128)(2,1)S(1)}, bf16[8,128,128]{2,1,0:T(8,128)(2,1)S(1)}, u32[]{:S(2)}, u32[]{:S(2)}) collective-permute-start(bf16[8,128,128]{2,1,0:T(8,128)(2,1)S(1)} %fusion.38), channel_id=1, source_target_pairs={{0,8},{4,12},{8,0},{12,4},{16,24},{20,28},{24,16},{28,20},{1,9},{5... | collective-permute-start | bytes 786440 | tf_op jit(solution)/shard_map/ppermute | solution.py:159
  62.3 5.7 %collective-permute-start.12 = (bf16[8,128,128]{2,1,0:T(8,128)(2,1)S(1)}, bf16[8,128,128]{2,1,0:T(8,128)(2,1)S(1)}, u32[]{:S(2)}, u32[]{:S(2)}) collective-permute-start(bf16[8,128,128]{2,1,0:T(8,128)(2,1)S(1)} %fusion.41), channel_id=1, source_target_pairs={{0,4},{4,0},{8,12},{12,8},{16,20},{20,16},{24,28},{28,24},{1,5},{5... | collective-permute-start | bytes 786440 | tf_op jit(solution)/shard_map/ppermute | solution.py:159
  62.4 13.9 %collective-permute-start.5 = (bf16[8,128,128]{2,1,0:T(8,128)(2,1)S(1)}, bf16[8,128,128]{2,1,0:T(8,128)(2,1)S(1)}, u32[]{:S(2)}, u32[]{:S(2)}) collective-permute-start(bf16[8,128,128]{2,1,0:T(8,128)(2,1)S(1)} %fusion.33), channel_id=1, source_target_pairs={{0,2},{1,3},{2,0},{3,1},{4,6},{5,7},{6,4},{7,5},{8,10},{9,11},{10,... | collective-permute-start | bytes 786440 | tf_op jit(solution)/shard_map/ppermute | solution.py:159
  65.2 11.4 %collective-permute-start.22 = (bf16[8,128,128]{2,1,0:T(8,128)(2,1)S(1)}, bf16[8,128,128]{2,1,0:T(8,128)(2,1)S(1)}, u32[]{:S(2)}, u32[]{:S(2)}) collective-permute-start(bf16[8,128,128]{2,1,0:T(8,128)(2,1)S(1)} %fusion.31), channel_id=1, source_target_pairs={{0,16},{4,20},{8,24},{12,28},{16,0},{20,4},{24,8},{28,12},{1,17},{... | collective-permute-start | bytes 786440 | tf_op jit(solution)/shard_map/ppermute | solution.py:159
  67.0 12.3 %collective-permute-start.18 = (bf16[8,128,128]{2,1,0:T(8,128)(2,1)S(1)}, bf16[8,128,128]{2,1,0:T(8,128)(2,1)S(1)}, u32[]{:S(2)}, u32[]{:S(2)}) collective-permute-start(bf16[8,128,128]{2,1,0:T(8,128)(2,1)S(1)} %fusion.27), channel_id=1, source_target_pairs={{0,16},{4,20},{8,24},{12,28},{16,0},{20,4},{24,8},{28,12},{1,17},{... | collective-permute-start | bytes 786440 | tf_op jit(solution)/shard_map/ppermute | solution.py:159
  68.1 13.1 %collective-permute-start.13 = (bf16[8,128,128]{2,1,0:T(8,128)(2,1)S(1)}, bf16[8,128,128]{2,1,0:T(8,128)(2,1)S(1)}, u32[]{:S(2)}, u32[]{:S(2)}) collective-permute-start(bf16[8,128,128]{2,1,0:T(8,128)(2,1)S(1)} %fusion.37), channel_id=1, source_target_pairs={{0,8},{4,12},{8,0},{12,4},{16,24},{20,28},{24,16},{28,20},{1,9},{5... | collective-permute-start | bytes 786440 | tf_op jit(solution)/shard_map/ppermute | solution.py:159
  76.4 4.8 %collective-permute-start.6 = (bf16[8,128,128]{2,1,0:T(8,128)(2,1)S(1)}, bf16[8,128,128]{2,1,0:T(8,128)(2,1)S(1)}, u32[]{:S(2)}, u32[]{:S(2)}) collective-permute-start(bf16[8,128,128]{2,1,0:T(8,128)(2,1)S(1)} %fusion.40), channel_id=1, source_target_pairs={{0,4},{4,0},{8,12},{12,8},{16,20},{20,16},{24,28},{28,24},{1,5},{5... | collective-permute-start | bytes 786440 | tf_op jit(solution)/shard_map/ppermute | solution.py:159
  76.9 19.9 %collective-permute-start.23 = (bf16[8,128,128]{2,1,0:T(8,128)(2,1)S(1)}, bf16[8,128,128]{2,1,0:T(8,128)(2,1)S(1)}, u32[]{:S(2)}, u32[]{:S(2)}) collective-permute-start(bf16[8,128,128]{2,1,0:T(8,128)(2,1)S(1)} %get-tuple-element.35), channel_id=1, source_target_pairs={{0,1},{1,0},{2,3},{3,2},{4,5},{5,4},{6,7},{7,6},{8,9},{9,8},{10,11... | collective-permute-start | bytes 786440 | tf_op jit(solution)/shard_map/ppermute | solution.py:159
  79.6 19.3 %collective-permute-start.19 = (bf16[8,128,128]{2,1,0:T(8,128)(2,1)S(1)}, bf16[8,128,128]{2,1,0:T(8,128)(2,1)S(1)}, u32[]{:S(2)}, u32[]{:S(2)}) collective-permute-start(bf16[8,128,128]{2,1,0:T(8,128)(2,1)S(1)} %get-tuple-element.37), channel_id=1, source_target_pairs={{0,1},{1,0},{2,3},{3,2},{4,5},{5,4},{6,7},{7,6},{8,9},{9,8},{10,11... | collective-permute-start | bytes 786440 | tf_op jit(solution)/shard_map/ppermute | solution.py:159
  81.4 7.1 %collective-permute-start.7 = (bf16[8,128,128]{2,1,0:T(8,128)(2,1)S(1)}, bf16[8,128,128]{2,1,0:T(8,128)(2,1)S(1)}, u32[]{:S(2)}, u32[]{:S(2)}) collective-permute-start(bf16[8,128,128]{2,1,0:T(8,128)(2,1)S(1)} %fusion.36), channel_id=1, source_target_pairs={{0,8},{4,12},{8,0},{12,4},{16,24},{20,28},{24,16},{28,20},{1,9},{5... | collective-permute-start | bytes 786440 | tf_op jit(solution)/shard_map/ppermute | solution.py:159
  83.1 7.4 %collective-permute-start.14 = (bf16[8,128,128]{2,1,0:T(8,128)(2,1)S(1)}, bf16[8,128,128]{2,1,0:T(8,128)(2,1)S(1)}, u32[]{:S(2)}, u32[]{:S(2)}) collective-permute-start(bf16[8,128,128]{2,1,0:T(8,128)(2,1)S(1)} %fusion.23), channel_id=1, source_target_pairs={{0,16},{4,20},{8,24},{12,28},{16,0},{20,4},{24,8},{28,12},{1,17},{... | collective-permute-start | bytes 786440 | tf_op jit(solution)/shard_map/ppermute | solution.py:159
  88.6 6.9 %collective-permute-start.8 = (bf16[8,128,128]{2,1,0:T(8,128)(2,1)S(1)}, bf16[8,128,128]{2,1,0:T(8,128)(2,1)S(1)}, u32[]{:S(2)}, u32[]{:S(2)}) collective-permute-start(bf16[8,128,128]{2,1,0:T(8,128)(2,1)S(1)} %fusion.11), channel_id=1, source_target_pairs={{0,16},{4,20},{8,24},{12,28},{16,0},{20,4},{24,8},{28,12},{1,17},{... | collective-permute-start | bytes 786440 | tf_op jit(solution)/shard_map/ppermute | solution.py:159
  90.9 10.2 %collective-permute-start.15 = (bf16[8,128,128]{2,1,0:T(8,128)(2,1)S(1)}, bf16[8,128,128]{2,1,0:T(8,128)(2,1)S(1)}, u32[]{:S(2)}, u32[]{:S(2)}) collective-permute-start(bf16[8,128,128]{2,1,0:T(8,128)(2,1)S(1)} %get-tuple-element.39), channel_id=1, source_target_pairs={{0,1},{1,0},{2,3},{3,2},{4,5},{5,4},{6,7},{7,6},{8,9},{9,8},{10,11... | collective-permute-start | bytes 786440 | tf_op jit(solution)/shard_map/ppermute | solution.py:159
  95.8 7.4 %collective-permute-start.9 = (bf16[8,128,128]{2,1,0:T(8,128)(2,1)S(1)}, bf16[8,128,128]{2,1,0:T(8,128)(2,1)S(1)}, u32[]{:S(2)}, u32[]{:S(2)}) collective-permute-start(bf16[8,128,128]{2,1,0:T(8,128)(2,1)S(1)} %get-tuple-element.41), channel_id=1, source_target_pairs={{0,1},{1,0},{2,3},{3,2},{4,5},{5,4},{6,7},{7,6},{8,9},{9,8},{10,11... | collective-permute-start | bytes 786440 | tf_op jit(solution)/shard_map/ppermute | solution.py:159

commit v4 on v3

--- a/solution.py
+++ b/solution.py
@@ -8,13 +8,16 @@
 from jax.sharding import PartitionSpec as P
 
 HD = 128
-SIZES = ((16, 1),) * 4
+SIZES = ((0, 16, 1), (16, 16, 3))
+OUT_ORDER = (0, 1, 3, 2)
+GAIN_PIECE = 0
+SEQ_FIRST = (False, False, False, True)
+SHARED = False
 LOCAL_STEP = 8
-LOCAL_AFTER = (-1, 1)
-KEEP = False
-LOCAL_SWAP = 4
+LOCAL_AFTER = ((0, 0), (0, 1), (1, 1), (1, 1))
+LOCAL_SWAP = (4, 4, 4, 5)
 LOCAL_TIE = True
-STEPS = ((0,), (1, (0, 0)), (2, (1, 0)), (3, (2, 0)), (0,), (1,), (2,), (3,), (0,), (1,), (2,), (3,), (0,), (1,), (2,), (3,), (0,), (1,), (2,), (3,), (0,), (1,), (2,), (3,), (0,), (1,), (2,), (3,))
+STEPS = ((0,), (3, (0, 0)), (1, (3, 0)), (2, (1, 0)), (0,), (1,), (2,), (3,), (0,), (1,), (2,), (3,), (0,), (1,), (2,), (3,), (0,), (1,), (2,), (3, (2, 2)), (0,), (1,), (2,), (3,), (0,), (1,), (2,), (3,))
 VMEM = 24 << 20
 
 
@@ -34,39 +37,48 @@
     return jnp.where(condition, f32(block), 0.0)
 
 
-def state_kernel(side_ref, key_ref, value_ref, mine_ref, theirs_ref):
-    half = mine_ref.shape[0]
-    for side, state_ref in enumerate((mine_ref, theirs_ref)):
-        base = (side_ref[0] ^ side) * half
+def state_kernel(side_ref, key_ref, value_ref, *refs, first):
+    *state_refs, keys, values, sems = refs
+    half = state_refs[0].shape[0]
+    copies = []
+    for part in range(len(state_refs)):
+        own = side_ref[0] if part % 2 else 1 - side_ref[0]
+        columns = pl.ds(pl.multiple_of((first + (part // 2 * 2 + own) * half) * HD, HD), half * HD)
+        for which, (ref, buffer) in enumerate(((key_ref, keys), (value_ref, values))):
+            copies.append(pltpu.make_async_copy(ref.at[:, columns], buffer.at[part], sems.at[part, which]))
+            copies[-1].start()
+    for part, state_ref in enumerate(state_refs):
+        copies[2 * part].wait()
+        copies[2 * part + 1].wait()
         for head in range(half):
-            columns = pl.ds(pl.multiple_of((base + head) * HD, HD), HD)
+            columns = slice(head * HD, (head + 1) * HD)
             state = lax.dot_general(
-                key_ref[:, columns],
-                value_ref[:, columns],
+                keys[part, :, columns],
+                values[part, :, columns],
                 (((0,), (0,)), ((), ())),
                 preferred_element_type=jnp.float32,
             )
             state_ref[head] = packed(state)
 
 
-def states_of(side, key_vectors, value_vectors, first, step, steps):
-    tokens, half = key_vectors.shape[0], step // 2
-    tokens_spec = pl.BlockSpec((tokens, step * HD), lambda i, side: (0, first // step + i))
-    side_spec = pl.BlockSpec((half, HD, HD), lambda i, side: (i, 0, 0))
-    half_shape = jax.ShapeDtypeStruct((steps * half, HD, HD), jnp.bfloat16)
+def states_of(side, key_vectors, value_vectors, first, size, count):
+    tokens, half = key_vectors.shape[0], size // 2
+    parts = 2 * count
+    buffer = pltpu.VMEM((parts, tokens, half * HD), jnp.bfloat16)
     return pl.pallas_call(
-        state_kernel,
+        functools.partial(state_kernel, first=first),
         grid_spec=pltpu.PrefetchScalarGridSpec(
             num_scalar_prefetch=1,
-            grid=(steps,),
-            in_specs=[tokens_spec, tokens_spec],
-            out_specs=[side_spec, side_spec],
-        ),
-        out_shape=[half_shape, half_shape],
+            grid=(1,),
+            in_specs=[pl.BlockSpec(memory_space=pl.ANY)] * 2,
+            out_specs=[pl.BlockSpec((half, HD, HD), lambda i, side: (0, 0, 0))] * parts,
+            scratch_shapes=[buffer, buffer, pltpu.SemaphoreType.DMA((parts, 2))],
+        ),
+        out_shape=[jax.ShapeDtypeStruct((half, HD, HD), jnp.bfloat16)] * parts,
         compiler_params=pltpu.CompilerParams(vmem_limit_bytes=VMEM),
         cost_estimate=pl.CostEstimate(
-            flops=2 * tokens * HD * HD * step * steps,
-            bytes_accessed=2 * step * steps * HD * (2 * tokens + HD),
+            flops=2 * tokens * HD * HD * size * count,
+            bytes_accessed=2 * size * count * HD * (2 * tokens + HD),
             transcendentals=0,
         ),
     )(side, key_vectors, value_vectors)
@@ -151,43 +163,66 @@
     return lax.optimization_barrier((block, *done))[0] if done else block
 
 
-def kept_whole(total):
-    return lax.optimization_barrier(total) if KEEP else total
-
-
 def swapped(block, axis, step):
     return lax.ppermute(block, axis, [(i, i ^ step) for i in range(lax.axis_size(axis))])
 
 
-def scan_of(mine, theirs, extra):
-    half, side = mine.shape[0], lax.axis_index("head") % 2
+def scan_of(mine, theirs, extra, seq_first):
+    half, place, index = mine.shape[0], lax.axis_index("head"), lax.axis_index("seq")
+    side, core = place % 2, index % 2
     done = yield
     sent = theirs if extra is None else jnp.concatenate([theirs, extra])
     arrived = swapped(after(sent, done), "head", 1)
     done = yield arrived
     neighbour = arrived[:half]
-    whole = kept_whole(added(mine, neighbour))
+    pair = added(mine, neighbour)
     if extra is not None:
         extra = added(extra, arrived[half:])
-    pieces = []
-    for axis, step in [("head", 2), ("seq", 1)]:
-        index = lax.axis_index(axis)
-        while step < lax.axis_size(axis):
-            sent = packed(whole)
-            if extra is not None and axis == "head":
-                sent = jnp.concatenate([sent, packed(extra)])
-            arrived = swapped(after(sent, done), axis, step)
-            done = ()
-            if (axis, step) in (("head", 2), ("seq", 1), ("seq", 2), ("seq", 4)):
-                done = yield arrived
-                if (axis, step) != ("head", 2):
-                    arrived, done = after(arrived, done), ()
-            pieces.append(kept(index & step != 0, arrived[:half]))
-            whole = kept_whole(whole + f32(arrived[:half]))
-            if extra is not None and axis == "head":
-                extra = extra + f32(arrived[half:])
-            step *= 2
-    earlier = functools.reduce(jnp.add, pieces)
+
+    whole, terms = pair, []
+    step = 2
+    while step < lax.axis_size("head") and not seq_first:
+        sent = packed(whole)
+        if extra is not None:
+            sent = jnp.concatenate([sent, packed(extra)])
+        arrived = swapped(after(sent, done), "head", step)
+        done = ()
+        if step == 2:
+            done = yield arrived
+        terms.append(kept(place & step != 0, arrived[:half]))
+        whole = whole + f32(arrived[:half])
+        if extra is not None:
+            extra = extra + f32(arrived[half:])
+        step *= 2
+
+    arrived = swapped(after(packed(whole), done), "seq", 1)
+    arrived = after(arrived, (yield arrived))
+    terms.append(kept(core == 1, arrived))
+    whole = whole + f32(arrived)
+    if SHARED:
+        part = half // 2
+        whole = jnp.where(core == 0, whole[:part], whole[part:])
+    chips, step = [], 2
+    while step < lax.axis_size("seq"):
+        arrived = swapped(packed(whole), "seq", step)
+        if step <= 4:
+            arrived = after(arrived, (yield arrived))
+        chips.append(kept(index & step != 0, arrived))
+        whole = whole + f32(arrived)
+        step *= 2
+    if SHARED:
+        chips = packed(functools.reduce(jnp.add, chips))
+        other = swapped(chips, "seq", 1)
+        chips = [f32(jnp.concatenate([jnp.where(core == 0, chips, other), jnp.where(core == 0, other, chips)]))]
+    earlier = functools.reduce(jnp.add, terms + chips)
+
+    if seq_first:
+        sent = packed(earlier + jnp.where(place & 2 == 0, pair, 0.0))
+        arrived = swapped(sent, "head", 2)
+        done = yield arrived
+        earlier = earlier + f32(arrived)
+    else:
+        done = ()
     carried_mine = packed(earlier + kept(side == 1, neighbour))
     carried_theirs = packed(earlier + kept(side == 0, mine))
     arrived = swapped(after(carried_theirs, done), "head", 1)
@@ -214,39 +249,34 @@
 
 
     firsts, sizes, scans, locals_by_piece = [], [], [], {}
-    first = 0
-    for size, count in SIZES:
-        own, other = states_of(side, key_vectors, value_vectors, first, size, count)
-        for piece in range(count):
-            part = slice(piece * size // 2, (piece + 1) * size // 2)
-            scans.append(scan_of(own[part], other[part], None if scans else gain_parts))
-            firsts.append(first)
+    for first, size, count in SIZES:
+        states = states_of(side, key_vectors, value_vectors, first, size, count)
+        for number, (theirs, mine) in enumerate(zip(states[0::2], states[1::2])):
+            seq_first = SEQ_FIRST[len(scans)] and lax.axis_size("head") == 4
+            scans.append(scan_of(mine, theirs, gain_parts if len(scans) == GAIN_PIECE else None, seq_first))
+            firsts.append(first + number * size)
             sizes.append(size)
-            first += size
             next(scans[-1])
 
     count = len(scans)
-    done, out, gain = [[] for _ in scans], None, None
+    done, out = [[] for _ in scans], None
     for piece, *wait_for in STEPS:
         wait_for = [done[other][swap] for other, swap in wait_for]
         swap = len(done[piece])
-        if swap == LOCAL_SWAP:
-            other, brought = piece + LOCAL_AFTER[0], LOCAL_AFTER[1]
-            before = [done[other][brought]] if 0 <= other and len(done[other]) > brought else []
+        if swap == LOCAL_SWAP[piece]:
+            other, brought = LOCAL_AFTER[piece]
+            before = [done[other][brought]] if len(done[other]) > brought else []
             local = locals_of(queries, key_vectors, value_vectors, firsts[piece], sizes[piece], before)
             wait_for += [local] if LOCAL_TIE else []
         result = scans[piece].send(wait_for)
-        if swap == LOCAL_SWAP:
+        if swap == LOCAL_SWAP[piece]:
             locals_by_piece[piece] = local
-        if isinstance(result, tuple):
-            mine, theirs, extra = result
-            if extra is not None:
-                rows = extra.reshape(-1, HD)
-                gain = rows[:heads] + rows[heads : 2 * heads] + rows[2 * heads : 3 * heads]
-                gain = gain.reshape(heads, 1, HD)
-            out = outputs_of(side, queries, locals_by_piece[piece], mine, theirs, gain, firsts[piece], out)
-            result = out
         done[piece].append(result)
+    rows = done[GAIN_PIECE][-1][2].reshape(-1, HD)
+    gain = (rows[:heads] + rows[heads : 2 * heads] + rows[2 * heads : 3 * heads]).reshape(heads, 1, HD)
+    for piece in OUT_ORDER:
+        mine, theirs, _ = done[piece][-1]
+        out = outputs_of(side, queries, locals_by_piece[piece], mine, theirs, gain, firsts[piece], out)
     return out
 
 

time: 106 us -> 103 us (0.972)
  waiting for transfers between devices: 41.9 us -> 38.2 us
  starting transfers between devices: 26.4 us -> 27.8 us
    ppermute x24, waiting for transfers between devices: 41.9 us -> 38.2 us  [swapped(): lax.ppermute(block, axis, [(i, i ^ step) for i in range(lax.axis_size(axi...]
    ppermute x24, starting transfers between devices: 26.4 us -> 27.8 us  [swapped(): lax.ppermute(block, axis, [(i, i ^ step) for i in range(lax.axis_size(axi...]
    unnamed x12 -> x10, local copies, waits for them, and re-layouts: 11.2 us -> 10.9 us
    pallas_call x4 -> x2, Pallas kernels: 3.79 us -> 3.76 us  [states_of(): pl.pallas_call(functools.partial(state_kernel, first=first), grid_spec=pl...]
  transfers between devices with their start and end apart: 24 -> 24, of which waited for: 9 -> 11; matrix products, arithmetic and copies ran while one was open for 3% -> 3% of each run, Pallas kernels for 17% -> 18%
where the time goes in v4:
time: 103 us
  waiting for transfers between devices  38.2 us (37%)
  starting transfers between devices  27.8 us (27%)
  Pallas kernels  21.3 us (21%)
  local copies, waits for them, and re-layouts  11.7 us (11%)
  other arithmetic  3.6 us (3%)
    ppermute x24, waiting for transfers between devices, swapped(): lax.ppermute(block, axis, [(i, i ^ step) for i in range(lax.axis_size(axi...  38.2 us
    ppermute x24, starting transfers between devices, swapped(): lax.ppermute(block, axis, [(i, i ^ step) for i in range(lax.axis_size(axi...  27.8 us
    unnamed x10, local copies, waits for them, and re-layouts  10.9 us
    pallas_call x4, Pallas kernels, locals_of(): pl.pallas_call(local_kernel, grid=(count // step,), in_specs=[tokens_spec...  9.01 us
    pallas_call x4, Pallas kernels, outputs_of(): pl.pallas_call(output_kernel, grid_spec=pltpu.PrefetchScalarGridSpec(num_...  8.5 us
    pallas_call x2, Pallas kernels, states_of(): pl.pallas_call(functools.partial(state_kernel, first=first), grid_spec=pl...  3.76 us
    convert_element_type x22, other arithmetic, packed(): return total.astype(jnp.bfloat16)  3.41 us
  transfers between devices with their start and end apart: 24, of which 11 were waited for; matrix products, arithmetic and copies ran while one was open for 3% of the time, Pallas kernels for 18%

profile of v4, /device:TPU:0, one launch (start us, length us, event | category | flops | bytes accessed | tf_op | source)
XLA Modules:
  0.0 102.8 jit_solution(14254806888169975937)
XLA Ops:
  0.8 2.2 %copy-done.1 = bf16[256,8192]{1,0:T(8,128)(2,1)S(1)} copy-done((bf16[256,8192]{1,0:T(8,128)(2,1)S(1)}, bf16[256,8192]{1,0:T(8,128)(2,1)}, u32[]{:S(2)}) %copy-start.1) | copy-done | bytes 4194328
  3.0 2.2 %copy-done.3 = bf16[256,8192]{1,0:T(8,128)(2,1)S(1)} copy-done((bf16[256,8192]{1,0:T(8,128)(2,1)S(1)}, bf16[256,8192]{1,0:T(8,128)(2,1)}, u32[]{:S(2)}) %copy-start.3) | copy-done | bytes 4194328
  6.3 3.1 %collective-permute-start = (bf16[10,128,128]{2,1,0:T(8,128)(2,1)S(1)}, bf16[10,128,128]{2,1,0:T(8,128)(2,1)S(1)}, u32[]{:S(2)}, u32[]{:S(2)}) collective-permute-start(bf16[10,128,128]{2,1,0:T(8,128)(2,1)S(1)} %pad_maximum_fusion), channel_id=1, source_target_pairs={{0,1},{1,0},{2,3},{3,2},{4,5},{5,4},{6,7},{7,6},{8,9},{9,8},{10,11... | collective-permute-start | bytes 983048 | tf_op jit(solution)/shard_map/ppermute | solution.py:167
  9.4 2.8 %shard_map.46 = (bf16[8,128,128]{2,1,0:T(8,128)(2,1)S(1)}, bf16[8,128,128]{2,1,0:T(8,128)(2,1)S(1)}, bf16[8,128,128]{2,1,0:T(8,128)(2,1)S(1)}, bf16[8,128,128]{2...) custom-call(s32[1]{0:T(128)} %bitcast.side_ref, ...), custom_call_target="tpu_custom_call" | custom-call | flops 402653184 | bytes 7864320 | tf_op jit(solution)/shard_map/pallas_call | solution.py:68
  12.2 4.9 %collective-permute-done.refs_0_ = bf16[10,128,128]{2,1,0:T(8,128)(2,1)S(1)} collective-permute-done((bf16[10,128,128]{2,1,0:T(8,128)(2,1)S(1)}, bf16[10,128,128]{2,1,0:T(8,128)(2,1)S(1)}, u32[]{:S(2)}, u32[]{:S(2)}) %collective-permute-start) | collective-permute-done | bytes 327712 | tf_op jit(solution)/shard_map/ppermute | solution.py:167
  17.1 1.7 %collective-permute-start.1 = (bf16[8,128,128]{2,1,0:T(8,128)(2,1)S(1)}, bf16[8,128,128]{2,1,0:T(8,128)(2,1)S(1)}, u32[]{:S(2)}, u32[]{:S(2)}) collective-permute-start(bf16[8,128,128]{2,1,0:T(8,128)(2,1)S(1)} %get-tuple-element.25), channel_id=1, source_target_pairs={{0,1},{1,0},{2,3},{3,2},{4,5},{5,4},{6,7},{7,6},{8,9},{9,8},{10,11... | collective-permute-start | bytes 786440 | tf_op jit(solution)/shard_map/ppermute | solution.py:167
  19.0 2.7 %collective-permute-start.10 = (bf16[10,128,128]{2,1,0:T(8,128)(2,1)S(1)}, bf16[10,128,128]{2,1,0:T(8,128)(2,1)S(1)}, u32[]{:S(2)}, u32[]{:S(2)}) collective-permute-start(bf16[10,128,128]{2,1,0:T(8,128)(2,1)S(1)} %pad_maximum_fusion.1), channel_id=1, source_target_pairs={{0,2},{1,3},{2,0},{3,1},{4,6},{5,7},{6,4},{7,5},{8,10},{9,11},{10,... | collective-permute-start | bytes 983048 | tf_op jit(solution)/shard_map/ppermute | solution.py:167
  21.6 2.2 %copy-done = bf16[256,8192]{1,0:T(8,128)(2,1)S(1)} copy-done((bf16[256,8192]{1,0:T(8,128)(2,1)S(1)}, bf16[256,8192]{1,0:T(8,128)(2,1)}, u32[]{:S(2)}) %copy-start) | copy-done | bytes 4194328
  23.8 2.2 %copy-done.2 = bf16[256,8192]{1,0:T(8,128)(2,1)S(1)} copy-done((bf16[256,8192]{1,0:T(8,128)(2,1)S(1)}, bf16[256,8192]{1,0:T(8,128)(2,1)}, u32[]{:S(2)}) %copy-start.2) | copy-done | bytes 4194328
  26.0 2.2 %copy-done.4 = bf16[256,8192]{1,0:T(8,128)(2,1)S(1)} copy-done((bf16[256,8192]{1,0:T(8,128)(2,1)S(1)}, bf16[256,8192]{1,0:T(8,128)(2,1)}, u32[]{:S(2)}) %copy-start.4) | copy-done | bytes 4194328
  28.2 2.2 %shard_map.51.local_ref = f32[256,2048]{1,0:T(8,128)S(1)} custom-call(bf16[256,8192]{1,0:T(8,128)(2,1)S(1)} %copy-done, bf16[256,8192]{1,0:T(8,128)(2,1)S(1)} %copy-done.2, bf16[256,8192]{1,0:T(8,128)(2,1)S(1)} %copy-done.4, bf16[10,128,128]{2,1,0:T(8,128)(2,1)S(1)} %collective-permute-done.refs_0_), custom_call_target="tpu_custom_call" | custom-call | flops 536870912 | bytes 5242880 | tf_op jit(solution)/shard_map/pallas_call | solution.py:107
  31.1 4.3 %collective-permute-done.10.refs_0_ = bf16[10,128,128]{2,1,0:T(8,128)(2,1)S(1)} collective-permute-done((bf16[10,128,128]{2,1,0:T(8,128)(2,1)S(1)}, bf16[10,128,128]{2,1,0:T(8,128)(2,1)S(1)}, u32[]{:S(2)}, u32[]{:S(2)}) %collective-permute-start.10) | collective-permute-done | bytes 327712 | tf_op jit(solution)/shard_map/ppermute | solution.py:167
  35.6 2.2 %shard_map.50.local_ref = f32[256,2048]{1,0:T(8,128)S(1)} custom-call(bf16[256,8192]{1,0:T(8,128)(2,1)S(1)} %copy-done, bf16[256,8192]{1,0:T(8,128)(2,1)S(1)} %copy-done.2, bf16[256,8192]{1,0:T(8,128)(2,1)S(1)} %copy-done.4, bf16[10,128,128]{2,1,0:T(8,128)(2,1)S(1)} %collective-permute-done.10.refs_0_), custom_call_target="tpu_custom_call" | custom-call | flops 536870912 | bytes 5242880 | tf_op jit(solution)/shard_map/pallas_call | solution.py:107
  40.2 1.6 %collective-permute-start.12 = (bf16[8,128,128]{2,1,0:T(8,128)(2,1)S(1)}, bf16[8,128,128]{2,1,0:T(8,128)(2,1)S(1)}, u32[]{:S(2)}, u32[]{:S(2)}) collective-permute-start(bf16[8,128,128]{2,1,0:T(8,128)(2,1)S(1)} %fusion.38), channel_id=1, source_target_pairs={{0,8},{4,12},{8,0},{12,4},{16,24},{20,28},{24,16},{28,20},{1,9},{5... | collective-permute-start | bytes 786440 | tf_op jit(solution)/shard_map/ppermute | solution.py:167
  41.8 2.5 %collective-permute-start.4 = (bf16[8,128,128]{2,1,0:T(8,128)(2,1)S(1)}, bf16[8,128,128]{2,1,0:T(8,128)(2,1)S(1)}, u32[]{:S(2)}, u32[]{:S(2)}) collective-permute-start(bf16[8,128,128]{2,1,0:T(8,128)(2,1)S(1)} %get-tuple-element.29), channel_id=1, source_target_pairs={{0,1},{1,0},{2,3},{3,2},{4,5},{5,4},{6,7},{7,6},{8,9},{9,8},{10,11... | collective-permute-start | bytes 786440 | tf_op jit(solution)/shard_map/ppermute | solution.py:167
  45.0 8.2 %collective-permute-done.3.refs_0_ = bf16[8,128,128]{2,1,0:T(8,128)(2,1)S(1)} collective-permute-done((bf16[8,128,128]{2,1,0:T(8,128)(2,1)S(1)}, bf16[8,128,128]{2,1,0:T(8,128)(2,1)S(1)}, u32[]{:S(2)}, u32[]{:S(2)}) %collective-permute-start.3) | collective-permute-done | bytes 262176 | tf_op jit(solution)/shard_map/ppermute | solution.py:167
  53.5 1.6 %collective-permute-start.13 = (bf16[8,128,128]{2,1,0:T(8,128)(2,1)S(1)}, bf16[8,128,128]{2,1,0:T(8,128)(2,1)S(1)}, u32[]{:S(2)}, u32[]{:S(2)}) collective-permute-start(bf16[8,128,128]{2,1,0:T(8,128)(2,1)S(1)} %fusion.22), channel_id=1, source_target_pairs={{0,16},{4,20},{8,24},{12,28},{16,0},{20,4},{24,8},{28,12},{1,17},{... | collective-permute-start | bytes 786440 | tf_op jit(solution)/shard_map/ppermute | solution.py:167
  55.3 2.2 %shard_map.49.local_ref = f32[256,2048]{1,0:T(8,128)S(1)} custom-call(bf16[256,8192]{1,0:T(8,128)(2,1)S(1)} %copy-done, bf16[256,8192]{1,0:T(8,128)(2,1)S(1)} %copy-done.2, bf16[256,8192]{1,0:T(8,128)(2,1)S(1)} %copy-done.4, bf16[8,128,128]{2,1,0:T(8,128)(2,1)S(1)} %collective-permute-done.3.refs_0_), custom_call_target="tpu_custom_call" | custom-call | flops 536870912 | bytes 5242880 | tf_op jit(solution)/shard_map/pallas_call | solution.py:107
  57.5 2.4 %shard_map.48.local_ref = f32[256,2048]{1,0:T(8,128)S(1)} custom-call(bf16[256,8192]{1,0:T(8,128)(2,1)S(1)} %copy-done, bf16[256,8192]{1,0:T(8,128)(2,1)S(1)} %copy-done.2, bf16[256,8192]{1,0:T(8,128)(2,1)S(1)} %copy-done.4, bf16[8,128,128]{2,1,0:T(8,128)(2,1)S(1)} %collective-permute-done.3.refs_0_), custom_call_target="tpu_custom_call" | custom-call | flops 536870912 | bytes 5242880 | tf_op jit(solution)/shard_map/pallas_call | solution.py:107
  62.4 6.5 %collective-permute-done.5 = bf16[8,128,128]{2,1,0:T(8,128)(2,1)S(1)} collective-permute-done((bf16[8,128,128]{2,1,0:T(8,128)(2,1)S(1)}, bf16[8,128,128]{2,1,0:T(8,128)(2,1)S(1)}, u32[]{:S(2)}, u32[]{:S(2)}) %collective-permute-start.5) | collective-permute-done | bytes 262176 | tf_op jit(solution)/shard_map/ppermute | solution.py:167
  71.6 2.1 %collective-permute-start.14 = (bf16[8,128,128]{2,1,0:T(8,128)(2,1)S(1)}, bf16[8,128,128]{2,1,0:T(8,128)(2,1)S(1)}, u32[]{:S(2)}, u32[]{:S(2)}) collective-permute-start(bf16[8,128,128]{2,1,0:T(8,128)(2,1)S(1)} %add_convert_fusion), channel_id=1, source_target_pairs={{0,2},{1,3},{2,0},{3,1},{4,6},{5,7},{6,4},{7,5},{8,10},{9,11},{10,... | collective-permute-start | bytes 786440 | tf_op jit(solution)/shard_map/ppermute | solution.py:167
  75.4 3.1 %collective-permute-done.18 = bf16[8,128,128]{2,1,0:T(8,128)(2,1)S(1)} collective-permute-done((bf16[8,128,128]{2,1,0:T(8,128)(2,1)S(1)}, bf16[8,128,128]{2,1,0:T(8,128)(2,1)S(1)}, u32[]{:S(2)}, u32[]{:S(2)}) %collective-permute-start.18) | collective-permute-done | bytes 262176 | tf_op jit(solution)/shard_map/ppermute | solution.py:167
  78.8 1.8 %collective-permute-start.19 = (bf16[8,128,128]{2,1,0:T(8,128)(2,1)S(1)}, bf16[8,128,128]{2,1,0:T(8,128)(2,1)S(1)}, u32[]{:S(2)}, u32[]{:S(2)}) collective-permute-start(bf16[8,128,128]{2,1,0:T(8,128)(2,1)S(1)} %get-tuple-element.39), channel_id=1, source_target_pairs={{0,1},{1,0},{2,3},{3,2},{4,5},{5,4},{6,7},{7,6},{8,9},{9,8},{10,11... | collective-permute-start | bytes 786440 | tf_op jit(solution)/shard_map/ppermute | solution.py:167
  81.9 1.6 %collective-permute-start.8 = (bf16[8,128,128]{2,1,0:T(8,128)(2,1)S(1)}, bf16[8,128,128]{2,1,0:T(8,128)(2,1)S(1)}, u32[]{:S(2)}, u32[]{:S(2)}) collective-permute-start(bf16[8,128,128]{2,1,0:T(8,128)(2,1)S(1)} %fusion.11), channel_id=1, source_target_pairs={{0,16},{4,20},{8,24},{12,28},{16,0},{20,4},{24,8},{28,12},{1,17},{... | collective-permute-start | bytes 786440 | tf_op jit(solution)/shard_map/ppermute | solution.py:167
  83.5 2.3 %collective-permute-done.14 = bf16[8,128,128]{2,1,0:T(8,128)(2,1)S(1)} collective-permute-done((bf16[8,128,128]{2,1,0:T(8,128)(2,1)S(1)}, bf16[8,128,128]{2,1,0:T(8,128)(2,1)S(1)}, u32[]{:S(2)}, u32[]{:S(2)}) %collective-permute-start.14) | collective-permute-done | bytes 262176 | tf_op jit(solution)/shard_map/ppermute | solution.py:167
  86.9 1.9 %collective-permute-done.8 = bf16[8,128,128]{2,1,0:T(8,128)(2,1)S(1)} collective-permute-done((bf16[8,128,128]{2,1,0:T(8,128)(2,1)S(1)}, bf16[8,128,128]{2,1,0:T(8,128)(2,1)S(1)}, u32[]{:S(2)}, u32[]{:S(2)}) %collective-permute-start.8) | collective-permute-done | bytes 262176 | tf_op jit(solution)/shard_map/ppermute | solution.py:167
  89.3 2.1 %shard_map.52.refs_0_ = bf16[256,8192]{1,0:T(8,128)(2,1)} custom-call(s32[1]{0:T(128)} %bitcast.side_ref, bf16[256,8192]{1,0:T(8,128)(2,1)S(1)} %copy-done, f32[256,2048]{1,0:T(8,128)S(1)} %shard_map.51.local_ref, bf16[8,128,128]{2,1,0:T(8,128)(2,1)S(1)} %get-tuple-element.38.mine_ref, bf16[8,128,128]{2,1,0:T(8,128)(2,1)S(1)} %collective-permute-done.23.theirs_ref, ...), custom_call_target="tpu_custom_call" | custom-call | flops 134217728 | bytes 4456448 | tf_op jit(solution)/shard_map/pallas_call | solution.py:146
  91.5 2.1 %shard_map.53.refs_0_ = bf16[256,8192]{1,0:T(8,128)(2,1)} custom-call(s32[1]{0:T(128)} %bitcast.side_ref, bf16[256,8192]{1,0:T(8,128)(2,1)S(1)} %copy-done, f32[256,2048]{1,0:T(8,128)S(1)} %shard_map.50.local_ref, bf16[8,128,128]{2,1,0:T(8,128)(2,1)S(1)} %get-tuple-element.40.mine_ref, ...), custom_call_target="tpu_custom_call", output_to_operand_aliasing={{}: (6, {})} | custom-call | flops 134217728 | bytes 4456448 | tf_op jit(solution)/shard_map/pallas_call | solution.py:146
  93.6 1.9 %collective-permute-done.15.theirs_ref = bf16[8,128,128]{2,1,0:T(8,128)(2,1)S(1)} collective-permute-done((bf16[8,128,128]{2,1,0:T(8,128)(2,1)S(1)}, bf16[8,128,128]{2,1,0:T(8,128)(2,1)S(1)}, u32[]{:S(2)}, u32[]{:S(2)}) %collective-permute-start.15) | collective-permute-done | bytes 262176 | tf_op jit(solution)/shard_map/ppermute | solution.py:167
  95.5 2.1 %shard_map.54.refs_0_ = bf16[256,8192]{1,0:T(8,128)(2,1)} custom-call(s32[1]{0:T(128)} %bitcast.side_ref, bf16[256,8192]{1,0:T(8,128)(2,1)S(1)} %copy-done, f32[256,2048]{1,0:T(8,128)S(1)} %shard_map.49.local_ref, bf16[8,128,128]{2,1,0:T(8,128)(2,1)S(1)} %get-tuple-element.42.mine_ref, ...), custom_call_target="tpu_custom_call", output_to_operand_aliasing={{}: (6, {})} | custom-call | flops 134217728 | bytes 4456448 | tf_op jit(solution)/shard_map/pallas_call | solution.py:146
  97.6 3.1 %collective-permute-done.9.theirs_ref = bf16[8,128,128]{2,1,0:T(8,128)(2,1)S(1)} collective-permute-done((bf16[8,128,128]{2,1,0:T(8,128)(2,1)S(1)}, bf16[8,128,128]{2,1,0:T(8,128)(2,1)S(1)}, u32[]{:S(2)}, u32[]{:S(2)}) %collective-permute-start.9) | collective-permute-done | bytes 262176 | tf_op jit(solution)/shard_map/ppermute | solution.py:167
  100.7 2.1 %shard_map.55 = bf16[256,8192]{1,0:T(8,128)(2,1)} custom-call(s32[1]{0:T(128)} %bitcast.side_ref, bf16[256,8192]{1,0:T(8,128)(2,1)S(1)} %copy-done, f32[256,2048]{1,0:T(8,128)S(1)} %shard_map.48.local_ref, bf16[8,128,128]{2,1,0:T(8,128)(2,1)S(1)} %get-tuple-element.44.mine_ref, ...), custom_call_target="tpu_custom_call", output_to_operand_aliasing={{}: (6, {})} | custom-call | flops 134217728 | bytes 4456448 | tf_op jit(solution)/shard_map/pallas_call | solution.py:146
  (67 shorter events, 16.5 us)
Async XLA Ops:
  0.8 2.2 %copy-start.1 = (bf16[256,8192]{1,0:T(8,128)(2,1)S(1)}, bf16[256,8192]{1,0:T(8,128)(2,1)}, u32[]{:S(2)}) copy-start(bf16[256,8192]{1,0:T(8,128)(2,1)} %key_ref.11) | copy-start | bytes 12582916
  3.0 2.2 %copy-start.3 = (bf16[256,8192]{1,0:T(8,128)(2,1)S(1)}, bf16[256,8192]{1,0:T(8,128)(2,1)}, u32[]{:S(2)}) copy-start(bf16[256,8192]{1,0:T(8,128)(2,1)} %value_ref.11) | copy-start | bytes 12582916
  6.3 10.8 %collective-permute-start = (bf16[10,128,128]{2,1,0:T(8,128)(2,1)S(1)}, bf16[10,128,128]{2,1,0:T(8,128)(2,1)S(1)}, u32[]{:S(2)}, u32[]{:S(2)}) collective-permute-start(bf16[10,128,128]{2,1,0:T(8,128)(2,1)S(1)} %pad_maximum_fusion), channel_id=1, source_target_pairs={{0,1},{1,0},{2,3},{3,2},{4,5},{5,4},{6,7},{7,6},{8,9},{9,8},{10,11... | collective-permute-start | bytes 983048 | tf_op jit(solution)/shard_map/ppermute | solution.py:167
  17.1 13.3 %collective-permute-start.1 = (bf16[8,128,128]{2,1,0:T(8,128)(2,1)S(1)}, bf16[8,128,128]{2,1,0:T(8,128)(2,1)S(1)}, u32[]{:S(2)}, u32[]{:S(2)}) collective-permute-start(bf16[8,128,128]{2,1,0:T(8,128)(2,1)S(1)} %get-tuple-element.25), channel_id=1, source_target_pairs={{0,1},{1,0},{2,3},{3,2},{4,5},{5,4},{6,7},{7,6},{8,9},{9,8},{10,11... | collective-permute-start | bytes 786440 | tf_op jit(solution)/shard_map/ppermute | solution.py:167
  19.0 16.4 %collective-permute-start.10 = (bf16[10,128,128]{2,1,0:T(8,128)(2,1)S(1)}, bf16[10,128,128]{2,1,0:T(8,128)(2,1)S(1)}, u32[]{:S(2)}, u32[]{:S(2)}) collective-permute-start(bf16[10,128,128]{2,1,0:T(8,128)(2,1)S(1)} %pad_maximum_fusion.1), channel_id=1, source_target_pairs={{0,2},{1,3},{2,0},{3,1},{4,6},{5,7},{6,4},{7,5},{8,10},{9,11},{10,... | collective-permute-start | bytes 983048 | tf_op jit(solution)/shard_map/ppermute | solution.py:167
  21.6 2.2 %copy-start = (bf16[256,8192]{1,0:T(8,128)(2,1)S(1)}, bf16[256,8192]{1,0:T(8,128)(2,1)}, u32[]{:S(2)}) copy-start(bf16[256,8192]{1,0:T(8,128)(2,1)} %query_ref.15) | copy-start | bytes 12582916
  23.8 2.2 %copy-start.2 = (bf16[256,8192]{1,0:T(8,128)(2,1)S(1)}, bf16[256,8192]{1,0:T(8,128)(2,1)}, u32[]{:S(2)}) copy-start(bf16[256,8192]{1,0:T(8,128)(2,1)} %key_ref.11) | copy-start | bytes 12582916
  26.0 2.2 %copy-start.4 = (bf16[256,8192]{1,0:T(8,128)(2,1)S(1)}, bf16[256,8192]{1,0:T(8,128)(2,1)}, u32[]{:S(2)}) copy-start(bf16[256,8192]{1,0:T(8,128)(2,1)} %value_ref.11) | copy-start | bytes 12582916
  30.4 8.4 %collective-permute-start.2 = (bf16[8,128,128]{2,1,0:T(8,128)(2,1)S(1)}, bf16[8,128,128]{2,1,0:T(8,128)(2,1)S(1)}, u32[]{:S(2)}, u32[]{:S(2)}) collective-permute-start(bf16[8,128,128]{2,1,0:T(8,128)(2,1)S(1)} %get-tuple-element.26), channel_id=1, source_target_pairs={{0,1},{1,0},{2,3},{3,2},{4,5},{5,4},{6,7},{7,6},{8,9},{9,8},{10,11... | collective-permute-start | bytes 786440 | tf_op jit(solution)/shard_map/ppermute | solution.py:167
  31.0 9.1 %collective-permute-start.11 = (bf16[8,128,128]{2,1,0:T(8,128)(2,1)S(1)}, bf16[8,128,128]{2,1,0:T(8,128)(2,1)S(1)}, u32[]{:S(2)}, u32[]{:S(2)}) collective-permute-start(bf16[8,128,128]{2,1,0:T(8,128)(2,1)S(1)} %fusion.34), channel_id=1, source_target_pairs={{0,4},{4,0},{8,12},{12,8},{16,20},{20,16},{24,28},{28,24},{1,5},{5... | collective-permute-start | bytes 786440 | tf_op jit(solution)/shard_map/ppermute | solution.py:167
  35.5 8.8 %collective-permute-start.20 = (bf16[8,128,128]{2,1,0:T(8,128)(2,1)S(1)}, bf16[8,128,128]{2,1,0:T(8,128)(2,1)S(1)}, u32[]{:S(2)}, u32[]{:S(2)}) collective-permute-start(bf16[8,128,128]{2,1,0:T(8,128)(2,1)S(1)} %fusion.44), channel_id=1, source_target_pairs={{0,4},{4,0},{8,12},{12,8},{16,20},{20,16},{24,28},{28,24},{1,5},{5... | collective-permute-start | bytes 786440 | tf_op jit(solution)/shard_map/ppermute | solution.py:167
  38.9 14.3 %collective-permute-start.3 = (bf16[8,128,128]{2,1,0:T(8,128)(2,1)S(1)}, bf16[8,128,128]{2,1,0:T(8,128)(2,1)S(1)}, u32[]{:S(2)}, u32[]{:S(2)}) collective-permute-start(bf16[8,128,128]{2,1,0:T(8,128)(2,1)S(1)} %fusion.31), channel_id=1, source_target_pairs={{0,2},{1,3},{2,0},{3,1},{4,6},{5,7},{6,4},{7,5},{8,10},{9,11},{10,... | collective-permute-start | bytes 786440 | tf_op jit(solution)/shard_map/ppermute | solution.py:167
  40.2 13.1 %collective-permute-start.12 = (bf16[8,128,128]{2,1,0:T(8,128)(2,1)S(1)}, bf16[8,128,128]{2,1,0:T(8,128)(2,1)S(1)}, u32[]{:S(2)}, u32[]{:S(2)}) collective-permute-start(bf16[8,128,128]{2,1,0:T(8,128)(2,1)S(1)} %fusion.38), channel_id=1, source_target_pairs={{0,8},{4,12},{8,0},{12,4},{16,24},{20,28},{24,16},{28,20},{1,9},{5... | collective-permute-start | bytes 786440 | tf_op jit(solution)/shard_map/ppermute | solution.py:167
  41.8 13.3 %collective-permute-start.4 = (bf16[8,128,128]{2,1,0:T(8,128)(2,1)S(1)}, bf16[8,128,128]{2,1,0:T(8,128)(2,1)S(1)}, u32[]{:S(2)}, u32[]{:S(2)}) collective-permute-start(bf16[8,128,128]{2,1,0:T(8,128)(2,1)S(1)} %get-tuple-element.29), channel_id=1, source_target_pairs={{0,1},{1,0},{2,3},{3,2},{4,5},{5,4},{6,7},{7,6},{8,9},{9,8},{10,11... | collective-permute-start | bytes 786440 | tf_op jit(solution)/shard_map/ppermute | solution.py:167
  44.5 15.5 %collective-permute-start.21 = (bf16[8,128,128]{2,1,0:T(8,128)(2,1)S(1)}, bf16[8,128,128]{2,1,0:T(8,128)(2,1)S(1)}, u32[]{:S(2)}, u32[]{:S(2)}) collective-permute-start(bf16[8,128,128]{2,1,0:T(8,128)(2,1)S(1)} %fusion.37), channel_id=1, source_target_pairs={{0,8},{4,12},{8,0},{12,4},{16,24},{20,28},{24,16},{28,20},{1,9},{5... | collective-permute-start | bytes 786440 | tf_op jit(solution)/shard_map/ppermute | solution.py:167
  53.3 7.9 %collective-permute-start.16 = (bf16[8,128,128]{2,1,0:T(8,128)(2,1)S(1)}, bf16[8,128,128]{2,1,0:T(8,128)(2,1)S(1)}, u32[]{:S(2)}, u32[]{:S(2)}) collective-permute-start(bf16[8,128,128]{2,1,0:T(8,128)(2,1)S(1)} %fusion.40), channel_id=1, source_target_pairs={{0,4},{4,0},{8,12},{12,8},{16,20},{20,16},{24,28},{28,24},{1,5},{5... | collective-permute-start | bytes 786440 | tf_op jit(solution)/shard_map/ppermute | solution.py:167
  53.5 17.8 %collective-permute-start.13 = (bf16[8,128,128]{2,1,0:T(8,128)(2,1)S(1)}, bf16[8,128,128]{2,1,0:T(8,128)(2,1)S(1)}, u32[]{:S(2)}, u32[]{:S(2)}) collective-permute-start(bf16[8,128,128]{2,1,0:T(8,128)(2,1)S(1)} %fusion.22), channel_id=1, source_target_pairs={{0,16},{4,20},{8,24},{12,28},{16,0},{20,4},{24,8},{28,12},{1,17},{... | collective-permute-start | bytes 786440 | tf_op jit(solution)/shard_map/ppermute | solution.py:167
  55.2 13.7 %collective-permute-start.5 = (bf16[8,128,128]{2,1,0:T(8,128)(2,1)S(1)}, bf16[8,128,128]{2,1,0:T(8,128)(2,1)S(1)}, u32[]{:S(2)}, u32[]{:S(2)}) collective-permute-start(bf16[8,128,128]{2,1,0:T(8,128)(2,1)S(1)} %fusion.32), channel_id=1, source_target_pairs={{0,2},{1,3},{2,0},{3,1},{4,6},{5,7},{6,4},{7,5},{8,10},{9,11},{10,... | collective-permute-start | bytes 786440 | tf_op jit(solution)/shard_map/ppermute | solution.py:167
  60.1 9.0 %collective-permute-start.22 = (bf16[8,128,128]{2,1,0:T(8,128)(2,1)S(1)}, bf16[8,128,128]{2,1,0:T(8,128)(2,1)S(1)}, u32[]{:S(2)}, u32[]{:S(2)}) collective-permute-start(bf16[8,128,128]{2,1,0:T(8,128)(2,1)S(1)} %fusion.30), channel_id=1, source_target_pairs={{0,16},{4,20},{8,24},{12,28},{16,0},{20,4},{24,8},{28,12},{1,17},{... | collective-permute-start | bytes 786440 | tf_op jit(solution)/shard_map/ppermute | solution.py:167
  61.3 9.2 %collective-permute-start.17 = (bf16[8,128,128]{2,1,0:T(8,128)(2,1)S(1)}, bf16[8,128,128]{2,1,0:T(8,128)(2,1)S(1)}, u32[]{:S(2)}, u32[]{:S(2)}) collective-permute-start(bf16[8,128,128]{2,1,0:T(8,128)(2,1)S(1)} %fusion.36), channel_id=1, source_target_pairs={{0,8},{4,12},{8,0},{12,4},{16,24},{20,28},{24,16},{28,20},{1,9},{5... | collective-permute-start | bytes 786440 | tf_op jit(solution)/shard_map/ppermute | solution.py:167
  69.0 2.3 %collective-permute-start.6 = (bf16[8,128,128]{2,1,0:T(8,128)(2,1)S(1)}, bf16[8,128,128]{2,1,0:T(8,128)(2,1)S(1)}, u32[]{:S(2)}, u32[]{:S(2)}) collective-permute-start(bf16[8,128,128]{2,1,0:T(8,128)(2,1)S(1)} %fusion.39), channel_id=1, source_target_pairs={{0,4},{4,0},{8,12},{12,8},{16,20},{20,16},{24,28},{28,24},{1,5},{5... | collective-permute-start | bytes 786440 | tf_op jit(solution)/shard_map/ppermute | solution.py:167
  69.5 19.9 %collective-permute-start.23 = (bf16[8,128,128]{2,1,0:T(8,128)(2,1)S(1)}, bf16[8,128,128]{2,1,0:T(8,128)(2,1)S(1)}, u32[]{:S(2)}, u32[]{:S(2)}) collective-permute-start(bf16[8,128,128]{2,1,0:T(8,128)(2,1)S(1)} %get-tuple-element.37), channel_id=1, source_target_pairs={{0,1},{1,0},{2,3},{3,2},{4,5},{5,4},{6,7},{7,6},{8,9},{9,8},{10,11... | collective-permute-start | bytes 786440 | tf_op jit(solution)/shard_map/ppermute | solution.py:167
  70.8 7.7 %collective-permute-start.18 = (bf16[8,128,128]{2,1,0:T(8,128)(2,1)S(1)}, bf16[8,128,128]{2,1,0:T(8,128)(2,1)S(1)}, u32[]{:S(2)}, u32[]{:S(2)}) collective-permute-start(bf16[8,128,128]{2,1,0:T(8,128)(2,1)S(1)} %fusion.26), channel_id=1, source_target_pairs={{0,16},{4,20},{8,24},{12,28},{16,0},{20,4},{24,8},{28,12},{1,17},{... | collective-permute-start | bytes 786440 | tf_op jit(solution)/shard_map/ppermute | solution.py:167
  71.6 14.1 %collective-permute-start.14 = (bf16[8,128,128]{2,1,0:T(8,128)(2,1)S(1)}, bf16[8,128,128]{2,1,0:T(8,128)(2,1)S(1)}, u32[]{:S(2)}, u32[]{:S(2)}) collective-permute-start(bf16[8,128,128]{2,1,0:T(8,128)(2,1)S(1)} %add_convert_fusion), channel_id=1, source_target_pairs={{0,2},{1,3},{2,0},{3,1},{4,6},{5,7},{6,4},{7,5},{8,10},{9,11},{10,... | collective-permute-start | bytes 786440 | tf_op jit(solution)/shard_map/ppermute | solution.py:167
  73.9 7.8 %collective-permute-start.7 = (bf16[8,128,128]{2,1,0:T(8,128)(2,1)S(1)}, bf16[8,128,128]{2,1,0:T(8,128)(2,1)S(1)}, u32[]{:S(2)}, u32[]{:S(2)}) collective-permute-start(bf16[8,128,128]{2,1,0:T(8,128)(2,1)S(1)} %fusion.35), channel_id=1, source_target_pairs={{0,8},{4,12},{8,0},{12,4},{16,24},{20,28},{24,16},{28,20},{1,9},{5... | collective-permute-start | bytes 786440 | tf_op jit(solution)/shard_map/ppermute | solution.py:167
  78.8 12.7 %collective-permute-start.19 = (bf16[8,128,128]{2,1,0:T(8,128)(2,1)S(1)}, bf16[8,128,128]{2,1,0:T(8,128)(2,1)S(1)}, u32[]{:S(2)}, u32[]{:S(2)}) collective-permute-start(bf16[8,128,128]{2,1,0:T(8,128)(2,1)S(1)} %get-tuple-element.39), channel_id=1, source_target_pairs={{0,1},{1,0},{2,3},{3,2},{4,5},{5,4},{6,7},{7,6},{8,9},{9,8},{10,11... | collective-permute-start | bytes 786440 | tf_op jit(solution)/shard_map/ppermute | solution.py:167
  81.9 6.9 %collective-permute-start.8 = (bf16[8,128,128]{2,1,0:T(8,128)(2,1)S(1)}, bf16[8,128,128]{2,1,0:T(8,128)(2,1)S(1)}, u32[]{:S(2)}, u32[]{:S(2)}) collective-permute-start(bf16[8,128,128]{2,1,0:T(8,128)(2,1)S(1)} %fusion.11), channel_id=1, source_target_pairs={{0,16},{4,20},{8,24},{12,28},{16,0},{20,4},{24,8},{28,12},{1,17},{... | collective-permute-start | bytes 786440 | tf_op jit(solution)/shard_map/ppermute | solution.py:167
  86.1 9.4 %collective-permute-start.15 = (bf16[8,128,128]{2,1,0:T(8,128)(2,1)S(1)}, bf16[8,128,128]{2,1,0:T(8,128)(2,1)S(1)}, u32[]{:S(2)}, u32[]{:S(2)}) collective-permute-start(bf16[8,128,128]{2,1,0:T(8,128)(2,1)S(1)} %get-tuple-element.34), channel_id=1, source_target_pairs={{0,1},{1,0},{2,3},{3,2},{4,5},{5,4},{6,7},{7,6},{8,9},{9,8},{10,11... | collective-permute-start | bytes 786440 | tf_op jit(solution)/shard_map/ppermute | solution.py:167
  89.1 11.6 %collective-permute-start.9 = (bf16[8,128,128]{2,1,0:T(8,128)(2,1)S(1)}, bf16[8,128,128]{2,1,0:T(8,128)(2,1)S(1)}, u32[]{:S(2)}, u32[]{:S(2)}) collective-permute-start(bf16[8,128,128]{2,1,0:T(8,128)(2,1)S(1)} %get-tuple-element.43), channel_id=1, source_target_pairs={{0,1},{1,0},{2,3},{3,2},{4,5},{5,4},{6,7},{7,6},{8,9},{9,8},{10,11... | collective-permute-start | bytes 786440 | tf_op jit(solution)/shard_map/ppermute | solution.py:167
